TPU v7x, 512 devices: a whole 4x8x8 slice. The times are simulated.
512 devices in a mesh: gx: 8 (over z), gy: 8 (over x, y_hi), gz: 8 (over y_lo, core).
Axes of the slice: x: 4, y: 8 (y_hi: 2, y_lo: 4; y = y_hi * 4 + y_lo), z: 8, core: 2. Of those that a mesh axis runs over, the one named last changes fastest.
Arguments:
- inputs: bfloat16 [2048, 6144], P(('gx', 'gy'), 'gz'), may hold values from -6 to 6
- value_weight: bfloat16 [6144, 6144], P(('gz', 'gx'), 'gy'), may hold values from -0.078125 to 0.078125
- probs: bfloat16 [48, 2048, 2048], P('gy', 'gz', 'gx'), may hold values from 0 to 1, as said below
- attended: bfloat16 [2048, 6144], P(('gz', 'gx'), 'gy'), may hold values from -6 to 6
- out_weight: bfloat16 [6144, 6144], P(('gy', 'gz'), 'gx'), may hold values from -0.078125 to 0.078125
- out_grad: bfloat16 [2048, 6144], P(('gz', 'gy'), 'gx'), may hold values from -6 to 6
Outputs:
- grad_inputs: bfloat16 [2048, 6144], P(('gx', 'gy'), 'gz')
- grad_value_weight: float32 [6144, 6144], P(('gz', 'gx'), 'gy')
- grad_out_weight: float32 [6144, 6144], P(('gy', 'gz'), 'gx')
Inputs may be any that keep to these rules, and one draw needn't show every extreme that they name: probs[h, q, k] is zero where k > q, and each row sums to one up to rounding.
All inputs are finite; a program needn't handle non-finite values.
Results may differ from a plain program's by a relative error of at most 0.03.
Values may be sent and summed in bfloat16 or wider, within the bound.
No kernel may reach another device: no remote copies, remote signals or barrier semaphores. Data moves between devices by JAX's collectives and lax.ppermute only.
A program may use at most 64 MiB of HBM per device.

v0:
```python
import math

import jax
import jax.numpy as jnp
from jax import lax
from jax.sharding import PartitionSpec as P

HEAD_DIM = 128


def body(inputs, value_weight, probs, attended, out_weight, out_grad):
    tokens_all = probs.shape[1] * lax.axis_size("gz")
    grad_scale = 1.0 / math.sqrt(tokens_all)
    heads_local = probs.shape[0]
    grad_gathered = lax.all_gather(out_grad, "gy", axis=0, tiled=True)
    head_partial = lax.dot_general(
        grad_gathered,
        lax.all_gather(out_weight, "gz", axis=0, tiled=True),
        (((1,), (1,)), ((), ())),
        preferred_element_type=jnp.float32,
    )
    head_grad = lax.psum(head_partial.astype(jnp.bfloat16), "gx")
    saved_gathered = lax.all_gather(attended, "gx", axis=0, tiled=True)
    columns = saved_gathered
    grad_out_weight = lax.psum_scatter(
        (
            lax.dot_general(
                columns, grad_gathered, (((0,), (0,)), ((), ())), preferred_element_type=jnp.float32
            )
            * grad_scale
        ).astype(jnp.bfloat16),
        "gz",
        scatter_dimension=0,
        tiled=True,
    ).astype(jnp.float32)
    queries = head_grad.reshape(head_grad.shape[0], heads_local, HEAD_DIM)
    value_partial = jnp.einsum("hqk,qhd->khd", probs, queries, preferred_element_type=jnp.float32)
    value_partial = value_partial.reshape(probs.shape[2], heads_local * HEAD_DIM)
    value_grad = lax.psum(value_partial.astype(jnp.bfloat16), "gz")
    input_gathered = lax.all_gather(inputs, "gy", axis=0, tiled=True)
    columns = input_gathered
    grad_value_weight = lax.psum_scatter(
        (
            lax.dot_general(
                columns, value_grad, (((0,), (0,)), ((), ())), preferred_element_type=jnp.float32
            )
            * grad_scale
        ).astype(jnp.bfloat16),
        "gx",
        scatter_dimension=0,
        tiled=True,
    ).astype(jnp.float32)
    input_partial = lax.dot_general(
        value_grad,
        lax.all_gather(value_weight, "gx", axis=0, tiled=True),
        (((1,), (1,)), ((), ())),
        preferred_element_type=jnp.float32,
    )
    grad_inputs = lax.psum_scatter(
        input_partial.astype(jnp.bfloat16), "gy", scatter_dimension=0, tiled=True
    )
    return (grad_inputs, grad_value_weight, grad_out_weight)


def solution(mesh):
    in_specs = (
        P(("gx", "gy"), "gz"),
        P(("gz", "gx"), "gy"),
        P("gy", "gz", "gx"),
        P(("gz", "gx"), "gy"),
        P(("gy", "gz"), "gx"),
        P(("gz", "gy"), "gx"),
    )
    out_specs = (P(("gx", "gy"), "gz"), P(("gz", "gx"), "gy"), P(("gy", "gz"), "gx"))
    return jax.shard_map(body, mesh=mesh, in_specs=in_specs, out_specs=out_specs, check_vma=False)
```

profile of v0, /device:TPU:1, one launch (start us, length us, event | category | flops | bytes accessed | tf_op | source)
XLA Modules:
  0.0 447.6 jit_solution(13850280388668995562)
XLA Ops:
  7.2 0.0 copy-start
  7.2 0.0 all-gather.3.cloned.1.call-start
  7.2 0.7 all-gather.3.cloned.1.call-update
  7.9 0.0 all-reduce.3.cloned.1.call-start
  8.0 44.6 %all_gather.15 = bf16[256,768]{1,0:T(8,128)(2,1)S(1)} all-gather(bf16[32,768]{1,0:T(8,128)(2,1)} %param.11), channel_id=1, replica_groups=mesh['gx'=8,'gy'=8,'gz'=8] {'gy'}, dimensions={0}, use_global_device_ids=true | all-gather | bytes 442368 | tf_op jit(solution)/shard_map/all_gather | solution.py:15
  52.5 2.9 all-gather.3.cloned.1.call-done
  55.4 1.8 convolution_convert_fusion.2
  57.2 0.9 copy.13
  58.1 0.0 copy-start.2
  58.1 0.0 all-reduce.3.cloned.1.call-update
  58.2 0.0 all-reduce.5.cloned.1.call-start
  58.2 80.7 %all-reduce.3.cloned.1.call-done = bf16[256,6,128]{0,2,1:T(8,128)(2,1)} async-done(((bf16[256,6,128]{0,2,1:T(8,128)(2,1)}), bf16[256,6,128]{0,2,1:T(8,128)(2,1)}) %all-reduce.3.cloned.1.call-update) | async-done | bytes 393232 | tf_op jit(solution)/shard_map/psum | solution.py:22
  138.9 0.0 copy-done
  138.9 2.0 convolution_convert_fusion.1
  140.9 0.0 all-reduce.5.cloned.1.call-update
  141.0 0.0 all-gather.5.cloned.1.call-start
  141.0 0.5 all-gather.5.cloned.1.call-update
  141.5 0.0 reduce-scatter.8.cloned.1.call-start
  141.6 0.0 copy-done.2
  141.6 18.9 %all_gather.19 = bf16[256,768]{1,0:T(8,128)(2,1)S(1)} all-gather(bf16[32,768]{1,0:T(8,128)(2,1)S(1)} %copy-done.2), channel_id=1, replica_groups=mesh['gx'=8,'gy'=8,'gz'=8] {'gx'}, dimensions={0}, use_global_device_ids=true | all-gather | bytes 442368 | tf_op jit(solution)/shard_map/all_gather | solution.py:23
  160.5 0.0 copy-start.3
  160.5 1.6 multiply_convert_fusion
  162.0 0.0 reduce-scatter.8.cloned.1.call-update
  162.1 0.0 reduce-scatter.10.cloned.1.call-start
  162.1 0.0 copy-done.3
  162.1 40.0 %all_gather.18 = bf16[256,768]{1,0:T(8,128)(2,1)S(1)} all-gather(bf16[32,768]{1,0:T(8,128)(2,1)S(1)} %copy-done.3), channel_id=1, replica_groups=mesh['gx'=8,'gy'=8,'gz'=8] {'gy'}, dimensions={0}, use_global_device_ids=true | all-gather | bytes 442368 | tf_op jit(solution)/shard_map/all_gather | solution.py:40
  202.1 18.0 %all-reduce.5.cloned.1.call-done = bf16[256,768]{0,1:T(8,128)(2,1)} async-done(((bf16[256,768]{0,1:T(8,128)(2,1)}), bf16[256,768]{0,1:T(8,128)(2,1)}) %all-reduce.5.cloned.1.call-update) | async-done | bytes 393232 | tf_op jit(solution)/shard_map/psum | solution.py:39
  220.1 1.5 fusion
  221.6 1.4 copy.15
  223.0 0.0 copy-start.1
  223.0 0.0 reduce-scatter.10.cloned.1.call-update
  223.1 0.0 reduce-scatter.6.cloned.1.call-start
  223.1 38.1 %all-gather.5.cloned.1.call-done = bf16[768,768]{1,0:T(8,128)(2,1)} async-done(((bf16[96,768]{1,0:T(8,128)(2,1)}), bf16[768,768]{1,0:T(8,128)(2,1)}) %all-gather.5.cloned.1.call-update) | async-done | bytes 1179664 | tf_op jit(solution)/shard_map/all_gather | solution.py:55
  261.2 0.0 copy-done.1
  261.2 2.6 convolution_convert_fusion
  263.8 0.0 reduce-scatter.6.cloned.1.call-update
  263.8 40.8 %reduce-scatter.8.cloned.1.call-done = bf16[96,768]{1,0:T(8,128)(2,1)} async-done(((bf16[768,768]{1,0:T(8,128)(2,1)}), bf16[96,768]{1,0:T(8,128)(2,1)}) %reduce-scatter.8.cloned.1.call-update) | async-done | bytes 147472 | tf_op jit(solution)/shard_map/reduce_scatter | solution.py:25
  304.6 1.6 convert_element_type.39
  306.2 39.8 %reduce-scatter.10.cloned.1.call-done = bf16[96,768]{1,0:T(8,128)(2,1)} async-done(((bf16[768,768]{1,0:T(8,128)(2,1)}), bf16[96,768]{1,0:T(8,128)(2,1)}) %reduce-scatter.10.cloned.1.call-update) | async-done | bytes 147472
  346.0 1.1 copy.16
  347.1 0.9 copy.14
  347.9 92.8 %reduce-scatter.6.cloned.1.call-done = bf16[32,768]{1,0:T(8,128)(2,1)} async-done(((bf16[256,768]{1,0:T(8,128)(2,1)}), bf16[32,768]{1,0:T(8,128)(2,1)}) %reduce-scatter.6.cloned.1.call-update) | async-done | bytes 49168 | tf_op jit(solution)/shard_map/reduce_scatter | solution.py:59
Async XLA Ops:
  7.2 131.8 %copy-start = (bf16[6,256,256]{2,1,0:T(8,128)(2,1)S(1)}, bf16[6,256,256]{2,1,0:T(8,128)(2,1)}, u32[]{:S(2)}) copy-start(bf16[6,256,256]{2,1,0:T(8,128)(2,1)} %param.8) | copy-start | bytes 2359300
  7.2 48.3 %all-gather.3.cloned.1.call-start = ((), (), s32[]{:S(2)}) async-start(), calls=%async_computation.3 | async-start | bytes 1327104 | tf_op jit(solution)/shard_map/all_gather | solution.py:18
  7.9 131.0 %all-reduce.3.cloned.1.call-start = ((), (), s32[]{:S(2)}) async-start(), calls=%async_computation.4 | async-start | bytes 786432 | tf_op jit(solution)/shard_map/psum | solution.py:22
  58.1 83.5 %copy-start.2 = (bf16[32,768]{1,0:T(8,128)(2,1)S(1)}, bf16[32,768]{1,0:T(8,128)(2,1)}, u32[]{:S(2)}) copy-start(bf16[32,768]{1,0:T(8,128)(2,1)} %param.9) | copy-start | bytes 147460
  58.2 162.0 %all-reduce.5.cloned.1.call-start = ((), (), s32[]{:S(2)}) async-start(), calls=%async_computation.5 | async-start | bytes 786432 | tf_op jit(solution)/shard_map/psum | solution.py:39
  141.0 120.3 %all-gather.5.cloned.1.call-start = ((), (), s32[]{:S(2)}) async-start(), calls=%async_computation.6 | async-start | bytes 1327104 | tf_op jit(solution)/shard_map/all_gather | solution.py:55
  141.5 163.0 %reduce-scatter.8.cloned.1.call-start = ((), (), s32[]{:S(2)}) async-start(), calls=%async_computation.8 | async-start | bytes 1327104 | tf_op jit(solution)/shard_map/reduce_scatter | solution.py:25
  160.5 1.6 copy-start.3
  162.1 184.0 %reduce-scatter.10.cloned.1.call-start = ((), (), s32[]{:S(2)}) async-start(), calls=%async_computation.9 | async-start | bytes 1327104
  223.0 38.2 %copy-start.1 = (bf16[256,768]{0,1:T(8,128)(2,1)S(1)}, bf16[256,768]{0,1:T(8,128)(2,1)}, u32[]{:S(2)}) copy-start(bf16[256,768]{0,1:T(8,128)(2,1)} %all-reduce.5.cloned.1.call-done) | copy-start | bytes 1179652
  223.1 217.7 %reduce-scatter.6.cloned.1.call-start = ((), (), s32[]{:S(2)}) async-start(), calls=%async_computation.7 | async-start | bytes 442368 | tf_op jit(solution)/shard_map/reduce_scatter | solution.py:59
Sparse Core Ops, SparseCore 0:
  10.1 45.2 all-gather.2
  58.3 80.5 all-reduce.2
  142.1 77.9 all-reduce.4
  222.1 39.1 all-gather.4
  263.9 40.6 reduce-scatter.7
  307.3 38.6 reduce-scatter.9
  351.0 89.7 reduce-scatter.5
where the time goes:
time: 449 us; the launch traced here: 448 us
  waiting for transfers between devices  314 us (70%)
  blocking collectives  103 us (23%)
  between operations  14.2 us (3%)
  matrix products  9.36 us (2%)
    reduce_scatter x1, waiting for transfers between devices, body(): lax.psum_scatter(input_partial.astype(jnp.bfloat16), 'gy', scatter_dimens...  92.8 us
    psum x1, waiting for transfers between devices, body(): head_grad = lax.psum(head_partial.astype(jnp.bfloat16), 'gx')  80.7 us
    all_gather x1, blocking collectives, body(): grad_gathered = lax.all_gather(out_grad, 'gy', axis=0, tiled=True)  44.6 us
    unnamed x8, waiting for transfers between devices  41.1 us
    reduce_scatter x1, waiting for transfers between devices, body(): lax.psum_scatter((lax.dot_general(columns, grad_gathered, (((0,), (0,)),...  40.8 us
    all_gather x1, blocking collectives, body(): input_gathered = lax.all_gather(inputs, 'gy', axis=0, tiled=True)  40 us
    all_gather x1, waiting for transfers between devices, body(): lax.all_gather(value_weight, 'gx', axis=0, tiled=True)  38.1 us
    all_gather x1, blocking collectives, body(): saved_gathered = lax.all_gather(attended, 'gx', axis=0, tiled=True)  18.9 us
  transfers between devices with their start and end apart: 7, of which 7 were waited for; matrix products, arithmetic and copies ran while one was open for 2% of the time, Pallas kernels for 0%

commit v1 on v0

v1 whole, which is shorter than its diff:
```python
import math

import jax
import jax.numpy as jnp
from jax import lax
from jax.sharding import PartitionSpec as P

HEAD_DIM = 128
Y_GROUPS = [[0, 2, 4, 6], [1, 3, 5, 7]]
CORE_GROUPS = [[0, 1], [2, 3], [4, 5], [6, 7]]
F32 = jnp.float32
BF16 = jnp.bfloat16


def spread(x, axis, groups=None):
    n = len(groups[0]) if groups else lax.axis_size(axis)
    copies = jnp.broadcast_to(x[None], (n,) + x.shape)
    return lax.all_to_all(copies, axis, 0, 0, tiled=True, axis_index_groups=groups)


def scatter_sum(x, axis):
    n = lax.axis_size(axis)
    parts = x.reshape((n, x.shape[0] // n) + x.shape[1:])
    parts = lax.all_to_all(parts, axis, 0, 0, tiled=True)
    return jnp.sum(parts.astype(F32), axis=0)


def dot(a, b, dims):
    return lax.dot_general(a, b, (dims, ((), ())), preferred_element_type=F32)


def body(inputs, value_weight, probs, attended, out_weight, out_grad):
    tokens_all = probs.shape[1] * lax.axis_size("gz")
    grad_scale = 1.0 / math.sqrt(tokens_all)
    heads = probs.shape[0]
    width = heads * HEAD_DIM
    rows = inputs.shape[0]
    depth = value_weight.shape[0]

    side = lax.all_gather(jnp.concatenate([value_weight, attended]), "gx", axis=0)
    weight_all = side[:, :depth].reshape(-1, width)
    saved = side[:, depth:].reshape(-1, width)

    quarter = lax.all_gather(out_weight, "gz", axis=0, axis_index_groups=Y_GROUPS)
    halves = spread(quarter, "gz", CORE_GROUPS)
    out_all = halves.transpose(1, 0, 2, 3).reshape(width, -1)
    both = spread(jnp.concatenate([out_grad, inputs]), "gy")
    grad_all = both[:, :rows].reshape(-1, out_grad.shape[1])
    input_all = both[:, rows:].reshape(-1, inputs.shape[1])

    head_partial = dot(grad_all, out_all, ((1,), (1,))).astype(BF16)
    head_rows = scatter_sum(head_partial, "gx").astype(BF16)
    head_grad = spread(head_rows, "gx").reshape(-1, heads, HEAD_DIM)

    out_terms = (dot(saved, grad_all, ((0,), (0,))) * grad_scale).astype(BF16)
    grad_out_weight = lax.psum_scatter(out_terms, "gz", scatter_dimension=0, tiled=True)

    value_partial = jnp.einsum("hqk,qhd->khd", probs, head_grad, preferred_element_type=F32)
    value_partial = value_partial.reshape(-1, width).astype(BF16)
    value_rows = scatter_sum(value_partial, "gz").astype(BF16)
    value_grad = lax.all_gather(value_rows, "gz", axis=0, tiled=True)

    value_terms = (dot(input_all, value_grad, ((0,), (0,))) * grad_scale).astype(BF16)
    grad_value_weight = lax.psum_scatter(value_terms, "gx", scatter_dimension=0, tiled=True)
    input_partial = dot(value_grad, weight_all, ((1,), (1,))).astype(BF16)
    grad_inputs = scatter_sum(input_partial, "gy").astype(BF16)
    return grad_inputs, grad_value_weight.astype(F32), grad_out_weight.astype(F32)


def solution(mesh):
    in_specs = (
        P(("gx", "gy"), "gz"),
        P(("gz", "gx"), "gy"),
        P("gy", "gz", "gx"),
        P(("gz", "gx"), "gy"),
        P(("gy", "gz"), "gx"),
        P(("gz", "gy"), "gx"),
    )
    out_specs = (P(("gx", "gy"), "gz"), P(("gz", "gx"), "gy"), P(("gy", "gz"), "gx"))
    return jax.shard_map(body, mesh=mesh, in_specs=in_specs, out_specs=out_specs, check_vma=False)
```

time: 449 us -> 188 us (0.42)
  waiting for transfers between devices: 314 us -> 42.7 us
  starting transfers between devices: 0.28 us -> 26.6 us
  blocking collectives: 103 us -> 84.5 us
    reduce_scatter x2, waiting for transfers between devices: 134 us -> 11.3 us  [the longest x1 11.3 us: body(): lax.psum_scatter(value_terms, 'gx', scatter_dimension=0, tiled=True)]
    psum x2 -> x0, waiting for transfers between devices: 98.7 us -> none  [the longest x1 80.7 us: body(): head_grad = lax.psum(head_partial.astype(jnp.bfloat16), 'gx')]
    all_gather x3 -> x2, blocking collectives: 103 us -> 29.7 us  [the longest x1 14.9 us: body(): value_grad = lax.all_gather(value_rows, 'gz', axis=0, tiled=True)]
    all_to_all x0 -> x3, blocking collectives: none -> 54.9 us  [the longest x2 40.3 us: scatter_sum(): parts = lax.all_to_all(parts, axis, 0, 0, tiled=True)]
    unnamed x8 -> x3, waiting for transfers between devices: 41.1 us -> 0.05 us
    all_gather x2 -> x1, waiting for transfers between devices: 41 us -> 0.02 us  [body(): lax.all_gather(jnp.concatenate([value_weight, attended]), 'gx', axis=0)]
    all_to_all x0 -> x3, waiting for transfers between devices: none -> 31.4 us  [the longest x2 21.8 us: spread(): lax.all_to_all(copies, axis, 0, 0, tiled=True, axis_index_groups=groups)]
    all_to_all x0 -> x3, starting transfers between devices: none -> 26.5 us  [the longest x2 16.6 us: spread(): lax.all_to_all(copies, axis, 0, 0, tiled=True, axis_index_groups=groups)]
  transfers between devices with their start and end apart: 7 -> 6, of which waited for: 7 -> 4; matrix products, arithmetic and copies ran while one was open for 2% -> 7% of each run, Pallas kernels for 0% -> 0%
where the time goes in v1:
time: 188 us; the launch traced here: 184 us
  blocking collectives  84.5 us (45%)
  waiting for transfers between devices  42.7 us (23%)
  starting transfers between devices  26.6 us (14%)
  between operations  13.9 us (7%)
  matrix products  6.23 us (3%)
  other arithmetic  5.77 us (3%)
  local copies, waits for them, and re-layouts  4.67 us (2%)
    all_to_all x2, blocking collectives, scatter_sum(): parts = lax.all_to_all(parts, axis, 0, 0, tiled=True)  40.3 us
    all_to_all x2, waiting for transfers between devices, spread(): lax.all_to_all(copies, axis, 0, 0, tiled=True, axis_index_groups=groups)  21.8 us
    all_to_all x2, starting transfers between devices, spread(): lax.all_to_all(copies, axis, 0, 0, tiled=True, axis_index_groups=groups)  16.6 us
    all_gather x1, blocking collectives, body(): value_grad = lax.all_gather(value_rows, 'gz', axis=0, tiled=True)  14.9 us
    all_gather x1, blocking collectives, body(): lax.all_gather(out_weight, 'gz', axis=0, axis_index_groups=Y_GROUPS)  14.8 us
    all_to_all x1, blocking collectives, spread(): lax.all_to_all(copies, axis, 0, 0, tiled=True, axis_index_groups=groups)  14.6 us
    reduce_scatter x1, waiting for transfers between devices, body(): lax.psum_scatter(value_terms, 'gx', scatter_dimension=0, tiled=True)  11.3 us
    all_to_all x1, starting transfers between devices, scatter_sum(): parts = lax.all_to_all(parts, axis, 0, 0, tiled=True)  9.9 us
  transfers between devices with their start and end apart: 6, of which 4 were waited for; matrix products, arithmetic and copies ran while one was open for 7% of the time, Pallas kernels for 0%

profile of v1, /device:TPU:1, one launch (start us, length us, event | category | flops | bytes accessed | tf_op | source)
XLA Modules:
  0.0 184.3 jit_solution(15320569890996122844)
XLA Ops:
  7.2 0.0 copy-start
  7.2 0.0 all-gather.4.cloned.1.call-start
  7.2 1.7 pad_maximum_fusion
  8.9 0.0 all-gather.4.cloned.1.call-update
  8.9 14.8 %all-gather = bf16[384,768]{1,0:T(8,128)(2,1)S(1)} all-gather(bf16[96,768]{1,0:T(8,128)(2,1)} %param.10), channel_id=2, replica_groups={{0,2,4,6},{1,3,5,7},{8,10,12,14},{9,11,13,15},{16,18,20,22},{17,19,21,2..., dimensions={0}, use_global_device_ids=true | all-gather | bytes 737280 | tf_op jit(solution)/shard_map/all_gather | solution.py:44
  23.7 1.1 broadcast_in_dim.7
  24.8 0.0 copy-start.2
  24.8 0.0 copy-start.3
  24.8 12.3 %all-to-all-start.1 = ((bf16[2,4,96,768]{3,2,1,0:T(8,128)(2,1)}), bf16[2,4,96,768]{3,2,1,0:T(8,128)(2,1)S(1)}, u32[]{:S(2)}, u32[]{:S(2)}) async-start(bf16[2,4,96,768]{3,2,1,0:T(8,128)(2,1)} %broadcast_in_dim.7), calls=%async_computation.1 | async-start | bytes 2359296 | tf_op jit(solution)/shard_map/all_to_all | solution.py:18
  37.2 0.0 copy-done.2
  37.2 0.0 copy-done.3
  37.2 1.8 all-to-all-done.1
  39.0 1.0 broadcast_in_dim.6
  40.0 4.2 %all-to-all-start = ((bf16[8,64,768]{2,1,0:T(8,128)(2,1)}), bf16[8,64,768]{2,1,0:T(8,128)(2,1)}, u32[]{:S(2)}, u32[]{:S(2)}) async-start(bf16[8,64,768]{2,1,0:T(8,128)(2,1)} %broadcast_in_dim.6), calls=%async_computation | async-start | bytes 1572864 | tf_op jit(solution)/shard_map/all_to_all | solution.py:18
  44.2 0.1 copy.11
  44.3 20.0 %all-to-all-done = bf16[8,64,768]{2,1,0:T(8,128)(2,1)} async-done(((bf16[8,64,768]{2,1,0:T(8,128)(2,1)}), bf16[8,64,768]{2,1,0:T(8,128)(2,1)}, u32[]{:S(2)}, u32[]{:S(2)}) %all-to-all-start) | async-done | bytes 786464 | tf_op jit(solution)/shard_map/all_to_all | solution.py:18
  64.3 1.2 fusion.5
  65.4 1.2 convolution_convert_fusion.2
  66.7 9.9 %all-to-all-start.2 = ((bf16[8,32,768]{2,1,0:T(8,128)(2,1)}), bf16[8,32,768]{2,1,0:T(8,128)(2,1)S(1)}, u32[]{:S(2)}, u32[]{:S(2)}) async-start(bf16[8,32,768]{2,1,0:T(8,128)(2,1)} %bitcast.4), calls=%async_computation.2 | async-start | bytes 786432 | tf_op jit(solution)/shard_map/all_to_all | solution.py:24
  76.6 0.0 reduce-scatter.5.cloned.1.call-start
  76.6 0.0 all-gather.4.cloned.1.call-done
  76.7 2.7 %fusion = bf16[768,768]{1,0:T(8,128)(2,1)} fusion(bf16[8,128,768]{2,1,0:T(8,128)(2,1)} %bitcast.28, bf16[8,64,768]{2,1,0:T(8,128)(2,1)} %all-to-all-done), kind=kOutput, calls=%fused_computation.1 | convolution fusion | flops 303169536 | bytes 1966080 | tf_op jit(solution)/shard_map/dot_general | solution.py:29
  79.3 0.0 reduce-scatter.5.cloned.1.call-update
  79.3 0.0 reduce-scatter.3.cloned.1.call-start
  79.4 9.5 %all-to-all-done.2 = bf16[8,32,768]{2,1,0:T(8,128)(2,1)S(1)} async-done(((bf16[8,32,768]{2,1,0:T(8,128)(2,1)}), bf16[8,32,768]{2,1,0:T(8,128)(2,1)S(1)}, u32[]{:S(2)}, u32[]{:S(2)}) %all-to-all-start.2) | async-done | bytes 393248 | tf_op jit(solution)/shard_map/all_to_all | solution.py:24
  88.9 0.1 reduce_sum.36
  89.0 14.6 %all_to_all.30 = bf16[8,32,768]{2,1,0:T(8,128)(2,1)S(1)} all-to-all(bf16[8,32,768]{2,1,0:T(8,128)(2,1)S(1)} %broadcast_in_dim.8), channel_id=1, replica_groups=mesh['gx'=8,'gy'=8,'gz'=8] {'gx'}, dimensions={0} | all-to-all | bytes 786432 | tf_op jit(solution)/shard_map/all_to_all | solution.py:18
  103.6 0.5 reshape.38
  104.0 0.0 copy-done
  104.1 0.3 fusion.1
  104.4 0.3 copy.13
  104.7 0.5 convert_element_type.37
  105.2 22.7 %all_to_all.31 = bf16[8,32,768]{2,1,0:T(8,128)(2,1)S(1)} all-to-all(bf16[8,32,768]{2,1,0:T(8,128)(2,1)S(1)} %convert_element_type.37), channel_id=1, replica_groups=mesh['gx'=8,'gy'=8,'gz'=8] {'gz'}, dimensions={0} | all-to-all | bytes 786432 | tf_op jit(solution)/shard_map/all_to_all | solution.py:24
  127.8 0.1 reduce_sum.37
  127.9 14.9 %all_gather.17 = bf16[256,768]{1,0:T(8,128)(2,1)S(1)} all-gather(bf16[32,768]{1,0:T(8,128)(2,1)S(1)} %reduce_sum.37), channel_id=1, replica_groups=mesh['gx'=8,'gy'=8,'gz'=8] {'gz'}, dimensions={0}, use_global_device_ids=true | all-gather | bytes 442368 | tf_op jit(solution)/shard_map/all_gather | solution.py:61
  142.8 0.0 copy-start.1
  142.8 1.5 multiply_convert_fusion
  144.3 0.0 reduce-scatter.3.cloned.1.call-update
  144.3 0.0 copy-done.1
  144.4 0.1 slice.17
  144.4 0.5 convolution_convert_fusion
  145.0 17.6 %all_to_all.32 = bf16[8,32,768]{2,1,0:T(8,128)(2,1)S(1)} all-to-all(bf16[8,32,768]{2,1,0:T(8,128)(2,1)S(1)} %bitcast.26), channel_id=1, replica_groups=mesh['gx'=8,'gy'=8,'gz'=8] {'gy'}, dimensions={0} | all-to-all | bytes 786432 | tf_op jit(solution)/shard_map/all_to_all | solution.py:24
  162.6 0.7 reduce_sum.38
  163.2 0.0 reduce-scatter.5.cloned.1.call-done
  163.2 1.6 convert_element_type.42
  164.9 11.3 %reduce-scatter.3.cloned.1.call-done = bf16[96,768]{1,0:T(8,128)(2,1)} async-done(((bf16[768,768]{1,0:T(8,128)(2,1)}), bf16[96,768]{1,0:T(8,128)(2,1)}) %reduce-scatter.3.cloned.1.call-update) | async-done | bytes 147472 | tf_op jit(solution)/shard_map/reduce_scatter | solution.py:64
  176.2 1.6 convert_element_type.40
  (2 shorter events, 0.0 us)
Async XLA Ops:
  7.2 96.9 %copy-start = (bf16[6,256,256]{2,1,0:T(8,128)(2,1)S(1)}, bf16[6,256,256]{2,1,0:T(8,128)(2,1)}, u32[]{:S(2)}) copy-start(bf16[6,256,256]{2,1,0:T(8,128)(2,1)} %param.8) | copy-start | bytes 2359300
  7.2 69.5 %all-gather.4.cloned.1.call-start = ((), (), s32[]{:S(2)}) async-start(), calls=%async_computation.10 | async-start | bytes 1769472 | tf_op jit(solution)/shard_map/all_gather | solution.py:40
  24.8 12.3 %copy-start.2 = (bf16[32,768]{1,0:T(8,128)(2,1)S(1)}, bf16[32,768]{1,0:T(8,128)(2,1)}, u32[]{:S(2)}) copy-start(bf16[32,768]{1,0:T(8,128)(2,1)} %param.6) | copy-start | bytes 147460
  24.8 12.3 %copy-start.3 = (bf16[32,768]{1,0:T(8,128)(2,1)S(1)}, bf16[32,768]{1,0:T(8,128)(2,1)}, u32[]{:S(2)}) copy-start(bf16[32,768]{1,0:T(8,128)(2,1)} %param.11) | copy-start | bytes 147460
  24.8 14.2 %all-to-all-start.1 = ((bf16[2,4,96,768]{3,2,1,0:T(8,128)(2,1)}), bf16[2,4,96,768]{3,2,1,0:T(8,128)(2,1)S(1)}, u32[]{:S(2)}, u32[]{:S(2)}) async-start(bf16[2,4,96,768]{3,2,1,0:T(8,128)(2,1)} %broadcast_in_dim.7), calls=%async_computation.1 | async-start | bytes 2359296 | tf_op jit(solution)/shard_map/all_to_all | solution.py:18
  40.0 24.3 %all-to-all-start = ((bf16[8,64,768]{2,1,0:T(8,128)(2,1)}), bf16[8,64,768]{2,1,0:T(8,128)(2,1)}, u32[]{:S(2)}, u32[]{:S(2)}) async-start(bf16[8,64,768]{2,1,0:T(8,128)(2,1)} %broadcast_in_dim.6), calls=%async_computation | async-start | bytes 1572864 | tf_op jit(solution)/shard_map/all_to_all | solution.py:18
  66.7 22.2 %all-to-all-start.2 = ((bf16[8,32,768]{2,1,0:T(8,128)(2,1)}), bf16[8,32,768]{2,1,0:T(8,128)(2,1)S(1)}, u32[]{:S(2)}, u32[]{:S(2)}) async-start(bf16[8,32,768]{2,1,0:T(8,128)(2,1)} %bitcast.4), calls=%async_computation.2 | async-start | bytes 786432 | tf_op jit(solution)/shard_map/all_to_all | solution.py:24
  76.6 86.7 %reduce-scatter.5.cloned.1.call-start = ((), (), s32[]{:S(2)}) async-start(), calls=%async_computation.9 | async-start | bytes 1327104 | tf_op jit(solution)/shard_map/reduce_scatter | solution.py:56
  79.3 96.8 %reduce-scatter.3.cloned.1.call-start = ((), (), s32[]{:S(2)}) async-start(), calls=%async_computation.8 | async-start | bytes 1327104 | tf_op jit(solution)/shard_map/reduce_scatter | solution.py:64
  142.8 1.6 copy-start.1
Sparse Core Ops, SparseCore 0:
  10.7 45.0 all-gather.3
  80.2 38.6 reduce-scatter.4
  144.5 31.6 reduce-scatter.2

commit v2 on v1

v2 whole, which is shorter than its diff:
```python
import math

import jax
import jax.numpy as jnp
from jax import lax
from jax.sharding import PartitionSpec as P

HEAD_DIM = 128
Y_GROUPS = [[0, 2, 4, 6], [1, 3, 5, 7]]
X_GROUPS = [[0, 2, 4, 6], [1, 3, 5, 7]]
FAR_PAIRS = [(i, i ^ 1) for i in range(8)]
F32 = jnp.float32
BF16 = jnp.bfloat16


def spread(x, axis, groups=None):
    n = len(groups[0]) if groups else lax.axis_size(axis)
    copies = jnp.broadcast_to(x[None], (n,) + x.shape)
    return lax.all_to_all(copies, axis, 0, 0, tiled=True, axis_index_groups=groups)


def exchange(x, axis):
    n = lax.axis_size(axis)
    parts = x.reshape((n, x.shape[0] // n) + x.shape[1:])
    return lax.all_to_all(parts, axis, 0, 0, tiled=True)


def scatter_sum(x, axis):
    return jnp.sum(exchange(x, axis).astype(F32), axis=0)


def scatter_sum_gy(x):
    me = lax.axis_index("gy")
    ring, far = me >> 1, me & 1
    parts = x.reshape((4, 2, x.shape[0] // 8) + x.shape[1:])
    total = lax.dynamic_index_in_dim(parts, ring, 0, False).astype(F32)
    for k in (1, 2, 3):
        pairs = [(i, (i + 2 * k) % 8) for i in range(8)]
        sent = lax.dynamic_index_in_dim(parts, (ring + k) & 3, 0, False)
        total = total + lax.ppermute(sent, "gy", pairs).astype(F32)
    sent = lax.dynamic_index_in_dim(total, 1 - far, 0, False).astype(BF16)
    kept = lax.dynamic_index_in_dim(total, far, 0, False)
    return kept + lax.ppermute(sent, "gy", FAR_PAIRS).astype(F32)

def far_pair(x):
    other = lax.ppermute(x, "gy", FAR_PAIRS)
    first = (lax.axis_index("gy") & 1) == 0
    return jnp.where(first, jnp.stack([x, other]), jnp.stack([other, x]))


def from_ring(x, k):
    return lax.ppermute(x, "gy", [(i, (i + 2 * k) % 8) for i in range(8)])


def in_ring_order(blocks):
    ring = lax.axis_index("gy") >> 1
    ordered = [lax.select_n((ring - j) & 3, *blocks) for j in range(4)]
    return jnp.stack(ordered).reshape((-1,) + blocks[0].shape[2:])


def dot(a, b, dims):
    return lax.dot_general(a, b, (dims, ((), ())), preferred_element_type=F32)


def body(inputs, value_weight, probs, attended, out_weight, out_grad):
    tokens_all = probs.shape[1] * lax.axis_size("gz")
    grad_scale = 1.0 / math.sqrt(tokens_all)
    heads = probs.shape[0]
    width = heads * HEAD_DIM
    rows = inputs.shape[0]
    depth = value_weight.shape[0]

    side = lax.all_gather(jnp.concatenate([value_weight, attended]), "gx", axis=0)
    weight_all = side[:, :depth].reshape(-1, width)
    saved = side[:, depth:].reshape(-1, width)

    pair = far_pair(out_grad)
    quarter = lax.all_gather(out_weight, "gz", axis=0, axis_index_groups=Y_GROUPS)
    pair, quarter = lax.optimization_barrier((pair, quarter))
    grad_all = spread(pair, "gy", X_GROUPS).reshape(-1, out_grad.shape[1])
    quarter = quarter.reshape((-1,) + out_weight.shape)
    sibling = lax.ppermute(quarter, "gz", FAR_PAIRS)
    first = (lax.axis_index("gz") & 1) == 0
    halves = jnp.where(
        first, jnp.stack([quarter, sibling], 1), jnp.stack([sibling, quarter], 1)
    )
    out_all = halves.reshape(width, -1)

    head_partial = dot(grad_all, out_all, ((1,), (1,))).astype(BF16)
    head_partial, late = lax.optimization_barrier((head_partial, inputs))
    head_parts = exchange(head_partial, "gx")
    out_terms = (dot(saved, grad_all, ((0,), (0,))) * grad_scale).astype(BF16)
    pair = far_pair(late)
    head_parts, out_terms, pair = lax.optimization_barrier((head_parts, out_terms, pair))
    grad_out_weight = lax.psum_scatter(out_terms, "gz", scatter_dimension=0, tiled=True)
    head_rows = jnp.sum(head_parts.astype(F32), axis=0).astype(BF16)
    head_grad = spread(head_rows, "gx").reshape(-1, width)
    blocks = [pair, from_ring(pair, 1), None, from_ring(pair, 3)]
    head_grad, blocks[1], blocks[3], pair = lax.optimization_barrier(
        (head_grad, blocks[1], blocks[3], pair)
    )
    head_grad = head_grad.reshape(-1, heads, HEAD_DIM)

    value_partial = jnp.einsum("hqk,qhd->khd", probs, head_grad, preferred_element_type=F32)
    value_partial = value_partial.reshape(-1, width).astype(BF16)
    value_partial, pair = lax.optimization_barrier((value_partial, pair))
    value_parts = exchange(value_partial, "gz")
    blocks[2] = from_ring(pair, 2)
    value_parts, blocks[2] = lax.optimization_barrier((value_parts, blocks[2]))
    input_all = in_ring_order(blocks)
    value_rows = jnp.sum(value_parts.astype(F32), axis=0).astype(BF16)
    value_grad = lax.all_gather(value_rows, "gz", axis=0, tiled=True)

    value_terms = (dot(input_all, value_grad, ((0,), (0,))) * grad_scale).astype(BF16)
    input_partial = dot(value_grad, weight_all, ((1,), (1,))).astype(BF16)
    grad_value_weight = scatter_sum(value_terms, "gx")
    grad_inputs = scatter_sum_gy(input_partial)
    return grad_inputs.astype(BF16), grad_value_weight.astype(F32), grad_out_weight.astype(F32)


def solution(mesh):
    in_specs = (
        P(("gx", "gy"), "gz"),
        P(("gz", "gx"), "gy"),
        P("gy", "gz", "gx"),
        P(("gz", "gx"), "gy"),
        P(("gy", "gz"), "gx"),
        P(("gz", "gy"), "gx"),
    )
    out_specs = (P(("gx", "gy"), "gz"), P(("gz", "gx"), "gy"), P(("gy", "gz"), "gx"))
    return jax.shard_map(body, mesh=mesh, in_specs=in_specs, out_specs=out_specs, check_vma=False)
```

time: 188 us -> 175 us (0.931); the launches traced: 184 us -> 174 us
  blocking collectives: 84.5 us -> 29.6 us
  starting transfers between devices: 26.6 us -> 71 us
    all_to_all x3 -> x0, blocking collectives: 54.9 us -> none  [the longest x2 40.3 us: scatter_sum(): parts = lax.all_to_all(parts, axis, 0, 0, tiled=True)]
    ppermute x0 -> x10, starting transfers between devices: none -> 38.1 us  [the longest x2 12 us: far_pair(): other = lax.ppermute(x, 'gy', FAR_PAIRS)]
    ppermute x0 -> x10, waiting for transfers between devices: none -> 24.7 us  [the longest x3 9.5 us: from_ring(): return lax.ppermute(x, 'gy', [(i, (i + 2 * k) % 8) for i in range(8)])]
    all_to_all x1 -> x3, starting transfers between devices: 9.9 us -> 23.4 us  [exchange(): return lax.all_to_all(parts, axis, 0, 0, tiled=True)]
    all_to_all x2, waiting for transfers between devices: 21.8 us -> 8.71 us  [spread(): lax.all_to_all(copies, axis, 0, 0, tiled=True, axis_index_groups=groups)]
    reduce_scatter x1 -> x0, waiting for transfers between devices: 11.3 us -> none  [body(): lax.psum_scatter(value_terms, 'gx', scatter_dimension=0, tiled=True)]
    all_to_all x2, starting transfers between devices: 16.6 us -> 9.43 us  [spread(): lax.all_to_all(copies, axis, 0, 0, tiled=True, axis_index_groups=groups)]
    all_to_all x1 -> x3, waiting for transfers between devices: 9.53 us -> 11 us  [exchange(): return lax.all_to_all(parts, axis, 0, 0, tiled=True)]
  transfers between devices with their start and end apart: 6 -> 17, of which waited for: 4 -> 11; matrix products, arithmetic and copies ran while one was open for 7% -> 5% of each run, Pallas kernels for 0% -> 0%
where the time goes in v2:
time: 175 us; the launch traced here: 174 us
  starting transfers between devices  71 us (41%)
  waiting for transfers between devices  44.5 us (25%)
  blocking collectives  29.6 us (17%)
  between operations  14.3 us (8%)
  other arithmetic  5.23 us (3%)
  matrix products  5.12 us (3%)
  local copies, waits for them, and re-layouts  4.74 us (3%)
    all_to_all x3, starting transfers between devices, exchange(): return lax.all_to_all(parts, axis, 0, 0, tiled=True)  23.4 us
    all_gather x1, blocking collectives, body(): value_grad = lax.all_gather(value_rows, 'gz', axis=0, tiled=True)  16.4 us
    all_gather x1, blocking collectives, body(): lax.all_gather(out_weight, 'gz', axis=0, axis_index_groups=Y_GROUPS)  13.2 us
    ppermute x2, starting transfers between devices, far_pair(): other = lax.ppermute(x, 'gy', FAR_PAIRS)  12 us
    all_to_all x3, waiting for transfers between devices, exchange(): return lax.all_to_all(parts, axis, 0, 0, tiled=True)  11 us
    ppermute x3, waiting for transfers between devices, from_ring(): return lax.ppermute(x, 'gy', [(i, (i + 2 * k) % 8) for i in range(8)])  9.5 us
    all_to_all x2, starting transfers between devices, spread(): lax.all_to_all(copies, axis, 0, 0, tiled=True, axis_index_groups=groups)  9.43 us
    all_to_all x2, waiting for transfers between devices, spread(): lax.all_to_all(copies, axis, 0, 0, tiled=True, axis_index_groups=groups)  8.71 us
  transfers between devices with their start and end apart: 17, of which 11 were waited for; matrix products, arithmetic and copies ran while one was open for 5% of the time, Pallas kernels for 0%

profile of v2, /device:TPU:1, one launch (start us, length us, event | category | flops | bytes accessed | tf_op | source)
XLA Modules:
  0.0 174.5 jit_solution(6099160030210763930)
XLA Ops:
  7.2 1.7 pad_maximum_fusion.1
  8.9 8.3 %collective-permute-start = (bf16[32,768]{1,0:T(8,128)(2,1)}, bf16[32,768]{1,0:T(8,128)(2,1)S(1)}, u32[]{:S(2)}, u32[]{:S(2)}) collective-permute-start(bf16[32,768]{1,0:T(8,128)(2,1)} %param.11), channel_id=1, source_target_pairs={{0,8},{8,0},{16,24},{24,16},{32,40},{40,32},{48,56},{56,48},{1,9},... | collective-permute-start | bytes 147464 | tf_op jit(solution)/shard_map/ppermute | solution.py:46
  17.2 13.2 %all-gather = bf16[384,768]{1,0:T(8,128)(2,1)S(1)} all-gather(bf16[96,768]{1,0:T(8,128)(2,1)} %param.10), channel_id=2, replica_groups={{0,2,4,6},{1,3,5,7},{8,10,12,14},{9,11,13,15},{16,18,20,22},{17,19,21,2..., dimensions={0}, use_global_device_ids=true | all-gather | bytes 737280 | tf_op jit(solution)/shard_map/all_gather | solution.py:78
  30.5 5.7 %collective-permute-start.1 = (bf16[4,96,768]{2,1,0:T(8,128)(2,1)S(1)}, bf16[4,96,768]{2,1,0:T(8,128)(2,1)S(1)}, u32[]{:S(2)}, u32[]{:S(2)}) collective-permute-start(bf16[4,96,768]{2,1,0:T(8,128)(2,1)S(1)} %bitcast.57), channel_id=1, source_target_pairs={{0,1},{1,0},{2,3},{3,2},{4,5},{5,4},{6,7},{7,6},{8,9},{9,8},{10,11... | collective-permute-start | bytes 1769480 | tf_op jit(solution)/shard_map/ppermute | solution.py:82
  36.2 0.8 broadcast_in_dim.4
  36.9 4.1 %all-to-all-start = ((bf16[4,2,32,768]{3,2,1,0:T(8,128)(2,1)}), bf16[4,2,32,768]{3,2,1,0:T(8,128)(2,1)S(1)}, u32[]{:S(2)}, u32[]{:S(2)}) async-start(bf16[4,2,32,768]{3,2,1,0:T(8,128)(2,1)} %broadcast_in_dim.4), calls=%async_computation | async-start | bytes 786432 | tf_op jit(solution)/shard_map/all_to_all | solution.py:19
  41.0 0.1 maximum_select_fusion
  41.2 7.8 %all-to-all-done = bf16[4,2,32,768]{3,2,1,0:T(8,128)(2,1)S(1)} async-done(((bf16[4,2,32,768]{3,2,1,0:T(8,128)(2,1)}), bf16[4,2,32,768]{3,2,1,0:T(8,128)(2,1)S(1)}, u32[]{:S(2)}, u32[]{:S(2)}) %all-to-all-start) | async-done | bytes 393248 | tf_op jit(solution)/shard_map/all_to_all | solution.py:19
  49.0 1.2 convolution_convert_fusion.2
  50.2 10.0 %all-to-all-start.1 = ((bf16[8,32,768]{2,1,0:T(8,128)(2,1)}), bf16[8,32,768]{2,1,0:T(8,128)(2,1)S(1)}, u32[]{:S(2)}, u32[]{:S(2)}) async-start(bf16[8,32,768]{2,1,0:T(8,128)(2,1)} %bitcast.7), calls=%async_computation.1 | async-start | bytes 786432 | tf_op jit(solution)/shard_map/all_to_all | solution.py:25
  60.2 3.7 %collective-permute-start.2 = (bf16[32,768]{1,0:T(8,128)(2,1)S(1)}, bf16[32,768]{1,0:T(8,128)(2,1)S(1)}, u32[]{:S(2)}, u32[]{:S(2)}) collective-permute-start(bf16[32,768]{1,0:T(8,128)(2,1)S(1)} %copy-done.5), channel_id=1, source_target_pairs={{0,8},{8,0},{16,24},{24,16},{32,40},{40,32},{48,56},{56,48},{1,9},... | collective-permute-start | bytes 147464 | tf_op jit(solution)/shard_map/ppermute | solution.py:46
  63.9 5.6 %collective-permute-done.2 = bf16[32,768]{1,0:T(8,128)(2,1)S(1)} collective-permute-done((bf16[32,768]{1,0:T(8,128)(2,1)S(1)}, bf16[32,768]{1,0:T(8,128)(2,1)S(1)}, u32[]{:S(2)}, u32[]{:S(2)}) %collective-permute-start.2) | collective-permute-done | bytes 49184 | tf_op jit(solution)/shard_map/ppermute | solution.py:46
  69.5 1.0 slice.8
  70.5 1.5 multiply_convert_fusion.1
  72.1 1.2 all-to-all-done.1
  73.3 0.1 reduce_sum.33
  73.4 0.8 broadcast_in_dim.5
  74.1 5.3 %all-to-all-start.2 = ((bf16[8,32,768]{2,1,0:T(8,128)(2,1)}), bf16[8,32,768]{2,1,0:T(8,128)(2,1)S(1)}, u32[]{:S(2)}, u32[]{:S(2)}) async-start(bf16[8,32,768]{2,1,0:T(8,128)(2,1)} %broadcast_in_dim.5), calls=%async_computation.2 | async-start | bytes 786432 | tf_op jit(solution)/shard_map/all_to_all | solution.py:19
  79.5 2.8 %collective-permute-start.4 = (bf16[2,32,768]{2,1,0:T(8,128)(2,1)S(1)}, bf16[2,32,768]{2,1,0:T(8,128)(2,1)S(1)}, u32[]{:S(2)}, u32[]{:S(2)}) collective-permute-start(bf16[2,32,768]{2,1,0:T(8,128)(2,1)S(1)} %maximum_select_fusion.2), channel_id=1, source_target_pairs={{0,48},{8,56},{16,0},{24,8},{32,16},{40,24},{48,32},{56,40},{1,49}... | collective-permute-start | bytes 294920 | tf_op jit(solution)/shard_map/ppermute | solution.py:52
  82.3 2.5 %collective-permute-start.3 = (bf16[2,32,768]{2,1,0:T(8,128)(2,1)S(1)}, bf16[2,32,768]{2,1,0:T(8,128)(2,1)S(1)}, u32[]{:S(2)}, u32[]{:S(2)}) collective-permute-start(bf16[2,32,768]{2,1,0:T(8,128)(2,1)S(1)} %maximum_select_fusion.2), channel_id=1, source_target_pairs={{0,16},{8,24},{16,32},{24,40},{32,48},{40,56},{48,0},{56,8},{1,17}... | collective-permute-start | bytes 294920 | tf_op jit(solution)/shard_map/ppermute | solution.py:52
  84.8 0.1 collective-permute-done.4
  84.8 4.3 %collective-permute-done.3 = bf16[2,32,768]{2,1,0:T(8,128)(2,1)S(1)} collective-permute-done((bf16[2,32,768]{2,1,0:T(8,128)(2,1)S(1)}, bf16[2,32,768]{2,1,0:T(8,128)(2,1)S(1)}, u32[]{:S(2)}, u32[]{:S(2)}) %collective-permute-start.3) | collective-permute-done | bytes 98336 | tf_op jit(solution)/shard_map/ppermute | solution.py:52
  89.1 0.9 all-to-all-done.2
  90.0 0.2 copy.11
  90.2 0.3 convolution_convert_fusion.1
  90.5 0.9 copy.12
  91.4 8.4 %all-to-all-start.3 = ((bf16[8,32,768]{2,1,0:T(8,128)(2,1)}), bf16[8,32,768]{2,1,0:T(8,128)(2,1)S(1)}, u32[]{:S(2)}, u32[]{:S(2)}) async-start(bf16[8,32,768]{2,1,0:T(8,128)(2,1)} %bitcast.16), calls=%async_computation.3 | async-start | bytes 786432 | tf_op jit(solution)/shard_map/all_to_all | solution.py:25
  99.9 2.4 %collective-permute-start.5 = (bf16[2,32,768]{2,1,0:T(8,128)(2,1)S(1)}, bf16[2,32,768]{2,1,0:T(8,128)(2,1)S(1)}, u32[]{:S(2)}, u32[]{:S(2)}) collective-permute-start(bf16[2,32,768]{2,1,0:T(8,128)(2,1)S(1)} %maximum_select_fusion.2), channel_id=1, source_target_pairs={{0,32},{8,40},{16,48},{24,56},{32,0},{40,8},{48,16},{56,24},{1,33}... | collective-permute-start | bytes 294920 | tf_op jit(solution)/shard_map/ppermute | solution.py:52
  102.4 5.1 %collective-permute-done.5 = bf16[2,32,768]{2,1,0:T(8,128)(2,1)S(1)} collective-permute-done((bf16[2,32,768]{2,1,0:T(8,128)(2,1)S(1)}, bf16[2,32,768]{2,1,0:T(8,128)(2,1)S(1)}, u32[]{:S(2)}, u32[]{:S(2)}) %collective-permute-start.5) | collective-permute-done | bytes 98336 | tf_op jit(solution)/shard_map/ppermute | solution.py:52
  107.5 4.1 %all-to-all-done.3 = bf16[8,32,768]{2,1,0:T(8,128)(2,1)S(1)} async-done(((bf16[8,32,768]{2,1,0:T(8,128)(2,1)}), bf16[8,32,768]{2,1,0:T(8,128)(2,1)S(1)}, u32[]{:S(2)}, u32[]{:S(2)}) %all-to-all-start.3) | async-done | bytes 393248 | tf_op jit(solution)/shard_map/all_to_all | solution.py:25
  111.6 0.1 reduce_sum.34
  111.6 16.4 %all_gather.19 = bf16[256,768]{1,0:T(8,128)(2,1)S(1)} all-gather(bf16[32,768]{1,0:T(8,128)(2,1)S(1)} %reduce_sum.34), channel_id=1, replica_groups=mesh['gx'=8,'gy'=8,'gz'=8] {'gz'}, dimensions={0}, use_global_device_ids=true | all-gather | bytes 442368 | tf_op jit(solution)/shard_map/all_gather | solution.py:112
  128.1 0.1 pad_maximum_fusion
  128.1 1.5 multiply_convert_fusion
  129.7 5.0 %all-to-all-start.4 = ((bf16[8,96,768]{2,1,0:T(8,128)(2,1)}), bf16[8,96,768]{2,1,0:T(8,128)(2,1)S(1)}, u32[]{:S(2)}, u32[]{:S(2)}) async-start(bf16[8,96,768]{2,1,0:T(8,128)(2,1)} %bitcast.68), calls=%async_computation.4 | async-start | bytes 2359296 | tf_op jit(solution)/shard_map/all_to_all | solution.py:25
  134.7 0.1 slice.9
  134.8 0.9 copy-done.3
  135.7 0.5 convolution_convert_fusion
  136.2 1.9 %collective-permute-start.6 = (bf16[2,32,768]{2,1,0:T(8,128)(2,1)S(1)}, bf16[2,32,768]{2,1,0:T(8,128)(2,1)S(1)}, u32[]{:S(2)}, u32[]{:S(2)}) collective-permute-start(bf16[2,32,768]{2,1,0:T(8,128)(2,1)S(1)} %get-tuple-element.37), channel_id=1, source_target_pairs={{0,16},{8,24},{16,32},{24,40},{32,48},{40,56},{48,0},{56,8},{1,17}... | collective-permute-start | bytes 294920 | tf_op jit(solution)/shard_map/ppermute | solution.py:40
  138.2 4.6 %collective-permute-start.8 = (bf16[2,32,768]{2,1,0:T(8,128)(2,1)S(1)}, bf16[2,32,768]{2,1,0:T(8,128)(2,1)S(1)}, u32[]{:S(2)}, u32[]{:S(2)}) collective-permute-start(bf16[2,32,768]{2,1,0:T(8,128)(2,1)S(1)} %get-tuple-element.38), channel_id=1, source_target_pairs={{0,48},{8,56},{16,0},{24,8},{32,16},{40,24},{48,32},{56,40},{1,49}... | collective-permute-start | bytes 294920 | tf_op jit(solution)/shard_map/ppermute | solution.py:40
  142.8 1.9 %collective-permute-start.7 = (bf16[2,32,768]{2,1,0:T(8,128)(2,1)S(1)}, bf16[2,32,768]{2,1,0:T(8,128)(2,1)S(1)}, u32[]{:S(2)}, u32[]{:S(2)}) collective-permute-start(bf16[2,32,768]{2,1,0:T(8,128)(2,1)S(1)} %get-tuple-element.39), channel_id=1, source_target_pairs={{0,32},{8,40},{16,48},{24,56},{32,0},{40,8},{48,16},{56,24},{1,33}... | collective-permute-start | bytes 294920 | tf_op jit(solution)/shard_map/ppermute | solution.py:40
  144.7 5.2 %collective-permute-done.7 = bf16[2,32,768]{2,1,0:T(8,128)(2,1)S(1)} collective-permute-done((bf16[2,32,768]{2,1,0:T(8,128)(2,1)S(1)}, bf16[2,32,768]{2,1,0:T(8,128)(2,1)S(1)}, u32[]{:S(2)}, u32[]{:S(2)}) %collective-permute-start.7) | collective-permute-done | bytes 98336 | tf_op jit(solution)/shard_map/ppermute | solution.py:40
  150.0 4.3 %collective-permute-start.9 = (bf16[32,768]{1,0:T(8,128)(2,1)S(1)}, bf16[32,768]{1,0:T(8,128)(2,1)S(1)}, u32[]{:S(2)}, u32[]{:S(2)}) collective-permute-start(bf16[32,768]{1,0:T(8,128)(2,1)S(1)} %fusion.3), channel_id=1, source_target_pairs={{0,8},{8,0},{16,24},{24,16},{32,40},{40,32},{48,56},{56,48},{1,9},... | collective-permute-start | bytes 147464 | tf_op jit(solution)/shard_map/ppermute | solution.py:43
  154.3 4.4 %collective-permute-done.9 = bf16[32,768]{1,0:T(8,128)(2,1)S(1)} collective-permute-done((bf16[32,768]{1,0:T(8,128)(2,1)S(1)}, bf16[32,768]{1,0:T(8,128)(2,1)S(1)}, u32[]{:S(2)}, u32[]{:S(2)}) %collective-permute-start.9) | collective-permute-done | bytes 49184 | tf_op jit(solution)/shard_map/ppermute | solution.py:43
  158.7 0.6 fusion.2
  159.4 1.6 convert_element_type.75
  161.0 5.7 %all-to-all-done.4 = bf16[8,96,768]{2,1,0:T(8,128)(2,1)S(1)} async-done(((bf16[8,96,768]{2,1,0:T(8,128)(2,1)}), bf16[8,96,768]{2,1,0:T(8,128)(2,1)S(1)}, u32[]{:S(2)}, u32[]{:S(2)}) %all-to-all-start.4) | async-done | bytes 1179680 | tf_op jit(solution)/shard_map/all_to_all | solution.py:25
  166.7 0.9 convert_reduce_fusion
  (27 shorter events, 0.3 us)
Async XLA Ops:
  7.2 83.0 %copy-start = (bf16[6,256,256]{2,1,0:T(8,128)(2,1)S(1)}, bf16[6,256,256]{2,1,0:T(8,128)(2,1)}, u32[]{:S(2)}) copy-start(bf16[6,256,256]{2,1,0:T(8,128)(2,1)} %param.8) | copy-start | bytes 2359300
  7.2 23.3 %copy-start.4 = (bf16[32,768]{1,0:T(8,128)(2,1)S(1)}, bf16[32,768]{1,0:T(8,128)(2,1)}, u32[]{:S(2)}) copy-start(bf16[32,768]{1,0:T(8,128)(2,1)} %param.11) | copy-start | bytes 147460
  7.2 62.3 %all-gather.4.cloned.1.call-start = ((), (), s32[]{:S(2)}) async-start(), calls=%async_computation.7 | async-start | bytes 1769472 | tf_op jit(solution)/shard_map/all_gather | solution.py:73
  8.9 21.5 %collective-permute-start = (bf16[32,768]{1,0:T(8,128)(2,1)}, bf16[32,768]{1,0:T(8,128)(2,1)S(1)}, u32[]{:S(2)}, u32[]{:S(2)}) collective-permute-start(bf16[32,768]{1,0:T(8,128)(2,1)} %param.11), channel_id=1, source_target_pairs={{0,8},{8,0},{16,24},{24,16},{32,40},{40,32},{48,56},{56,48},{1,9},... | collective-permute-start | bytes 147464 | tf_op jit(solution)/shard_map/ppermute | solution.py:46
  30.5 10.6 %collective-permute-start.1 = (bf16[4,96,768]{2,1,0:T(8,128)(2,1)S(1)}, bf16[4,96,768]{2,1,0:T(8,128)(2,1)S(1)}, u32[]{:S(2)}, u32[]{:S(2)}) collective-permute-start(bf16[4,96,768]{2,1,0:T(8,128)(2,1)S(1)} %bitcast.57), channel_id=1, source_target_pairs={{0,1},{1,0},{2,3},{3,2},{4,5},{5,4},{6,7},{7,6},{8,9},{9,8},{10,11... | collective-permute-start | bytes 1769480 | tf_op jit(solution)/shard_map/ppermute | solution.py:82
  36.9 12.0 %all-to-all-start = ((bf16[4,2,32,768]{3,2,1,0:T(8,128)(2,1)}), bf16[4,2,32,768]{3,2,1,0:T(8,128)(2,1)S(1)}, u32[]{:S(2)}, u32[]{:S(2)}) async-start(bf16[4,2,32,768]{3,2,1,0:T(8,128)(2,1)} %broadcast_in_dim.4), calls=%async_computation | async-start | bytes 786432 | tf_op jit(solution)/shard_map/all_to_all | solution.py:19
  49.0 11.2 %copy-start.5 = (bf16[32,768]{1,0:T(8,128)(2,1)S(1)}, bf16[32,768]{1,0:T(8,128)(2,1)}, u32[]{:S(2)}) copy-start(bf16[32,768]{1,0:T(8,128)(2,1)} %param.6) | copy-start | bytes 147460
  50.2 23.1 %all-to-all-start.1 = ((bf16[8,32,768]{2,1,0:T(8,128)(2,1)}), bf16[8,32,768]{2,1,0:T(8,128)(2,1)S(1)}, u32[]{:S(2)}, u32[]{:S(2)}) async-start(bf16[8,32,768]{2,1,0:T(8,128)(2,1)} %bitcast.7), calls=%async_computation.1 | async-start | bytes 786432 | tf_op jit(solution)/shard_map/all_to_all | solution.py:25
  60.2 9.3 %collective-permute-start.2 = (bf16[32,768]{1,0:T(8,128)(2,1)S(1)}, bf16[32,768]{1,0:T(8,128)(2,1)S(1)}, u32[]{:S(2)}, u32[]{:S(2)}) collective-permute-start(bf16[32,768]{1,0:T(8,128)(2,1)S(1)} %copy-done.5), channel_id=1, source_target_pairs={{0,8},{8,0},{16,24},{24,16},{32,40},{40,32},{48,56},{56,48},{1,9},... | collective-permute-start | bytes 147464 | tf_op jit(solution)/shard_map/ppermute | solution.py:46
  74.1 15.9 %all-to-all-start.2 = ((bf16[8,32,768]{2,1,0:T(8,128)(2,1)}), bf16[8,32,768]{2,1,0:T(8,128)(2,1)S(1)}, u32[]{:S(2)}, u32[]{:S(2)}) async-start(bf16[8,32,768]{2,1,0:T(8,128)(2,1)} %broadcast_in_dim.5), calls=%async_computation.2 | async-start | bytes 786432 | tf_op jit(solution)/shard_map/all_to_all | solution.py:19
  79.5 5.3 %collective-permute-start.4 = (bf16[2,32,768]{2,1,0:T(8,128)(2,1)S(1)}, bf16[2,32,768]{2,1,0:T(8,128)(2,1)S(1)}, u32[]{:S(2)}, u32[]{:S(2)}) collective-permute-start(bf16[2,32,768]{2,1,0:T(8,128)(2,1)S(1)} %maximum_select_fusion.2), channel_id=1, source_target_pairs={{0,48},{8,56},{16,0},{24,8},{32,16},{40,24},{48,32},{56,40},{1,49}... | collective-permute-start | bytes 294920 | tf_op jit(solution)/shard_map/ppermute | solution.py:52
  82.3 6.9 %collective-permute-start.3 = (bf16[2,32,768]{2,1,0:T(8,128)(2,1)S(1)}, bf16[2,32,768]{2,1,0:T(8,128)(2,1)S(1)}, u32[]{:S(2)}, u32[]{:S(2)}) collective-permute-start(bf16[2,32,768]{2,1,0:T(8,128)(2,1)S(1)} %maximum_select_fusion.2), channel_id=1, source_target_pairs={{0,16},{8,24},{16,32},{24,40},{32,48},{40,56},{48,0},{56,8},{1,17}... | collective-permute-start | bytes 294920 | tf_op jit(solution)/shard_map/ppermute | solution.py:52
  91.4 20.1 %all-to-all-start.3 = ((bf16[8,32,768]{2,1,0:T(8,128)(2,1)}), bf16[8,32,768]{2,1,0:T(8,128)(2,1)S(1)}, u32[]{:S(2)}, u32[]{:S(2)}) async-start(bf16[8,32,768]{2,1,0:T(8,128)(2,1)} %bitcast.16), calls=%async_computation.3 | async-start | bytes 786432 | tf_op jit(solution)/shard_map/all_to_all | solution.py:25
  99.9 59.5 %reduce-scatter.2.cloned.1.call-start = ((), (), s32[]{:S(2)}) async-start(), calls=%async_computation.6 | async-start | bytes 1327104 | tf_op jit(solution)/shard_map/reduce_scatter | solution.py:95
  99.9 7.6 %collective-permute-start.5 = (bf16[2,32,768]{2,1,0:T(8,128)(2,1)S(1)}, bf16[2,32,768]{2,1,0:T(8,128)(2,1)S(1)}, u32[]{:S(2)}, u32[]{:S(2)}) collective-permute-start(bf16[2,32,768]{2,1,0:T(8,128)(2,1)S(1)} %maximum_select_fusion.2), channel_id=1, source_target_pairs={{0,32},{8,40},{16,48},{24,56},{32,0},{40,8},{48,16},{56,24},{1,33}... | collective-permute-start | bytes 294920 | tf_op jit(solution)/shard_map/ppermute | solution.py:52
  128.0 1.7 copy-start.2
  129.7 5.0 %copy-start.1 = (bf16[1024,768]{1,0:T(8,128)(2,1)S(1)}, bf16[1024,768]{1,0:T(8,128)(2,1)}, u32[]{:S(2)}) copy-start(bf16[1024,768]{1,0:T(8,128)(2,1)} %all-gather.4.cloned.1.call-done) | copy-start | bytes 4718596
  129.7 37.1 %all-to-all-start.4 = ((bf16[8,96,768]{2,1,0:T(8,128)(2,1)}), bf16[8,96,768]{2,1,0:T(8,128)(2,1)S(1)}, u32[]{:S(2)}, u32[]{:S(2)}) async-start(bf16[8,96,768]{2,1,0:T(8,128)(2,1)} %bitcast.68), calls=%async_computation.4 | async-start | bytes 2359296 | tf_op jit(solution)/shard_map/all_to_all | solution.py:25
  134.7 1.0 copy-start.3
  136.2 8.4 %collective-permute-start.6 = (bf16[2,32,768]{2,1,0:T(8,128)(2,1)S(1)}, bf16[2,32,768]{2,1,0:T(8,128)(2,1)S(1)}, u32[]{:S(2)}, u32[]{:S(2)}) collective-permute-start(bf16[2,32,768]{2,1,0:T(8,128)(2,1)S(1)} %get-tuple-element.37), channel_id=1, source_target_pairs={{0,16},{8,24},{16,32},{24,40},{32,48},{40,56},{48,0},{56,8},{1,17}... | collective-permute-start | bytes 294920 | tf_op jit(solution)/shard_map/ppermute | solution.py:40
  138.2 6.5 %collective-permute-start.8 = (bf16[2,32,768]{2,1,0:T(8,128)(2,1)S(1)}, bf16[2,32,768]{2,1,0:T(8,128)(2,1)S(1)}, u32[]{:S(2)}, u32[]{:S(2)}) collective-permute-start(bf16[2,32,768]{2,1,0:T(8,128)(2,1)S(1)} %get-tuple-element.38), channel_id=1, source_target_pairs={{0,48},{8,56},{16,0},{24,8},{32,16},{40,24},{48,32},{56,40},{1,49}... | collective-permute-start | bytes 294920 | tf_op jit(solution)/shard_map/ppermute | solution.py:40
  142.8 7.2 %collective-permute-start.7 = (bf16[2,32,768]{2,1,0:T(8,128)(2,1)S(1)}, bf16[2,32,768]{2,1,0:T(8,128)(2,1)S(1)}, u32[]{:S(2)}, u32[]{:S(2)}) collective-permute-start(bf16[2,32,768]{2,1,0:T(8,128)(2,1)S(1)} %get-tuple-element.39), channel_id=1, source_target_pairs={{0,32},{8,40},{16,48},{24,56},{32,0},{40,8},{48,16},{56,24},{1,33}... | collective-permute-start | bytes 294920 | tf_op jit(solution)/shard_map/ppermute | solution.py:40
  150.0 8.8 %collective-permute-start.9 = (bf16[32,768]{1,0:T(8,128)(2,1)S(1)}, bf16[32,768]{1,0:T(8,128)(2,1)S(1)}, u32[]{:S(2)}, u32[]{:S(2)}) collective-permute-start(bf16[32,768]{1,0:T(8,128)(2,1)S(1)} %fusion.3), channel_id=1, source_target_pairs={{0,8},{8,0},{16,24},{24,16},{32,40},{40,32},{48,56},{56,48},{1,9},... | collective-permute-start | bytes 147464 | tf_op jit(solution)/shard_map/ppermute | solution.py:43
Sparse Core Ops, SparseCore 0:
  10.7 44.5 all-gather.3
  103.5 35.3 reduce-scatter.1

commit v3 on v2

--- a/solution.py
+++ b/solution.py
@@ -7,8 +7,10 @@
 
 HEAD_DIM = 128
 Y_GROUPS = [[0, 2, 4, 6], [1, 3, 5, 7]]
+CORE_GROUPS = [[0, 1], [2, 3], [4, 5], [6, 7]]
 X_GROUPS = [[0, 2, 4, 6], [1, 3, 5, 7]]
 FAR_PAIRS = [(i, i ^ 1) for i in range(8)]
+PAD_ROWS = 128
 F32 = jnp.float32
 BF16 = jnp.bfloat16
 
@@ -48,14 +50,15 @@
     return jnp.where(first, jnp.stack([x, other]), jnp.stack([other, x]))
 
 
-def from_ring(x, k):
-    return lax.ppermute(x, "gy", [(i, (i + 2 * k) % 8) for i in range(8)])
-
-
-def in_ring_order(blocks):
-    ring = lax.axis_index("gy") >> 1
-    ordered = [lax.select_n((ring - j) & 3, *blocks) for j in range(4)]
-    return jnp.stack(ordered).reshape((-1,) + blocks[0].shape[2:])
+def all_sum_gz(x, later):
+    both = lax.all_gather(x, "gz", axis=0, axis_index_groups=CORE_GROUPS)
+    both = both.reshape((2, 2, x.shape[0] // 2) + x.shape[1:])
+    half = lax.dynamic_index_in_dim(both, lax.axis_index("gz") & 1, 1, False)
+    half = jnp.sum(half.astype(F32), axis=0).astype(BF16)
+    run = lax.all_gather(half, "gz", axis=0, axis_index_groups=Y_GROUPS)
+    run, later = lax.optimization_barrier((run, later))
+    half = jnp.sum(run.astype(F32), axis=0).astype(BF16)
+    return lax.all_gather(half, "gz", axis=0, axis_index_groups=CORE_GROUPS, tiled=True), later
 
 
 def dot(a, b, dims):
@@ -67,7 +70,6 @@
     grad_scale = 1.0 / math.sqrt(tokens_all)
     heads = probs.shape[0]
     width = heads * HEAD_DIM
-    rows = inputs.shape[0]
     depth = value_weight.shape[0]
 
     side = lax.all_gather(jnp.concatenate([value_weight, attended]), "gx", axis=0)
@@ -76,7 +78,8 @@
 
     pair = far_pair(out_grad)
     quarter = lax.all_gather(out_weight, "gz", axis=0, axis_index_groups=Y_GROUPS)
-    pair, quarter = lax.optimization_barrier((pair, quarter))
+    pair, quarter, late = lax.optimization_barrier((pair, quarter, inputs))
+    input_pair = far_pair(late)
     grad_all = spread(pair, "gy", X_GROUPS).reshape(-1, out_grad.shape[1])
     quarter = quarter.reshape((-1,) + out_weight.shape)
     sibling = lax.ppermute(quarter, "gz", FAR_PAIRS)
@@ -87,30 +90,22 @@
     out_all = halves.reshape(width, -1)
 
     head_partial = dot(grad_all, out_all, ((1,), (1,))).astype(BF16)
-    head_partial, late = lax.optimization_barrier((head_partial, inputs))
     head_parts = exchange(head_partial, "gx")
     out_terms = (dot(saved, grad_all, ((0,), (0,))) * grad_scale).astype(BF16)
-    pair = far_pair(late)
-    head_parts, out_terms, pair = lax.optimization_barrier((head_parts, out_terms, pair))
-    grad_out_weight = lax.psum_scatter(out_terms, "gz", scatter_dimension=0, tiled=True)
+    input_pair, out_terms = lax.optimization_barrier((input_pair, out_terms))
+    mine = input_pair.reshape(-1, inputs.shape[1])
+    mine = jnp.pad(mine, ((0, PAD_ROWS), (0, 0)))
+    head_parts, out_terms, mine = lax.optimization_barrier((head_parts, out_terms, mine))
+    input_all = lax.all_gather(mine, "gy", axis=0, axis_index_groups=X_GROUPS)
     head_rows = jnp.sum(head_parts.astype(F32), axis=0).astype(BF16)
-    head_grad = spread(head_rows, "gx").reshape(-1, width)
-    blocks = [pair, from_ring(pair, 1), None, from_ring(pair, 3)]
-    head_grad, blocks[1], blocks[3], pair = lax.optimization_barrier(
-        (head_grad, blocks[1], blocks[3], pair)
-    )
-    head_grad = head_grad.reshape(-1, heads, HEAD_DIM)
+    head_grad = spread(head_rows, "gx").reshape(-1, heads, HEAD_DIM)
 
     value_partial = jnp.einsum("hqk,qhd->khd", probs, head_grad, preferred_element_type=F32)
     value_partial = value_partial.reshape(-1, width).astype(BF16)
-    value_partial, pair = lax.optimization_barrier((value_partial, pair))
-    value_parts = exchange(value_partial, "gz")
-    blocks[2] = from_ring(pair, 2)
-    value_parts, blocks[2] = lax.optimization_barrier((value_parts, blocks[2]))
-    input_all = in_ring_order(blocks)
-    value_rows = jnp.sum(value_parts.astype(F32), axis=0).astype(BF16)
-    value_grad = lax.all_gather(value_rows, "gz", axis=0, tiled=True)
+    value_grad, out_terms = all_sum_gz(value_partial, out_terms)
+    grad_out_weight = lax.psum_scatter(out_terms, "gz", scatter_dimension=0, tiled=True)
 
+    input_all = input_all[:, : 2 * inputs.shape[0]].reshape(-1, inputs.shape[1])
     value_terms = (dot(input_all, value_grad, ((0,), (0,))) * grad_scale).astype(BF16)
     input_partial = dot(value_grad, weight_all, ((1,), (1,))).astype(BF16)
     grad_value_weight = scatter_sum(value_terms, "gx")

time: 175 us -> 165 us (0.943)
  starting transfers between devices: 71 us -> 53.6 us
  blocking collectives: 29.6 us -> 40.2 us
  waiting for transfers between devices: 44.5 us -> 37.6 us
  local copies, waits for them, and re-layouts: 4.74 us -> 6.73 us
    all_gather x1 -> x3, blocking collectives: 16.4 us -> 27 us  [the longest x1 17 us: all_sum_gz(): run = lax.all_gather(half, 'gz', axis=0, axis_index_groups=Y_GROUPS)]
    all_to_all x3 -> x2, starting transfers between devices: 23.4 us -> 13.5 us  [exchange(): return lax.all_to_all(parts, axis, 0, 0, tiled=True)]
    all_to_all x2, waiting for transfers between devices: 8.71 us -> 18.3 us  [spread(): lax.all_to_all(copies, axis, 0, 0, tiled=True, axis_index_groups=groups)]
    ppermute x3 -> x0, waiting for transfers between devices: 9.5 us -> none  [from_ring(): return lax.ppermute(x, 'gy', [(i, (i + 2 * k) % 8) for i in range(8)])]
    all_to_all x3 -> x2, waiting for transfers between devices: 11 us -> 2.43 us  [exchange(): return lax.all_to_all(parts, axis, 0, 0, tiled=True)]
    ppermute x3 -> x0, starting transfers between devices: 7.7 us -> none  [from_ring(): return lax.ppermute(x, 'gy', [(i, (i + 2 * k) % 8) for i in range(8)])]
  transfers between devices with their start and end apart: 17 -> 14, of which waited for: 11 -> 7; matrix products, arithmetic and copies ran while one was open for 5% -> 9% of each run, Pallas kernels for 0% -> 0%
where the time goes in v3:
time: 165 us; the launch traced here: 163 us
  starting transfers between devices  53.6 us (32%)
  blocking collectives  40.2 us (24%)
  waiting for transfers between devices  37.6 us (23%)
  between operations  14 us (8%)
  local copies, waits for them, and re-layouts  6.73 us (4%)
  other arithmetic  6.13 us (4%)
  matrix products  5.18 us (3%)
    all_to_all x2, waiting for transfers between devices, spread(): lax.all_to_all(copies, axis, 0, 0, tiled=True, axis_index_groups=groups)  18.3 us
    all_gather x1, blocking collectives, all_sum_gz(): run = lax.all_gather(half, 'gz', axis=0, axis_index_groups=Y_GROUPS)  17 us
    all_to_all x2, starting transfers between devices, exchange(): return lax.all_to_all(parts, axis, 0, 0, tiled=True)  13.5 us
    all_gather x1, blocking collectives, body(): lax.all_gather(out_weight, 'gz', axis=0, axis_index_groups=Y_GROUPS)  13.2 us
    ppermute x2, starting transfers between devices, far_pair(): other = lax.ppermute(x, 'gy', FAR_PAIRS)  12 us
    all_to_all x2, starting transfers between devices, spread(): lax.all_to_all(copies, axis, 0, 0, tiled=True, axis_index_groups=groups)  10.2 us
    ppermute x3, starting transfers between devices, scatter_sum_gy(): total = total + lax.ppermute(sent, 'gy', pairs).astype(F32)  8.41 us
    all_gather x1, blocking collectives, all_sum_gz(): both = lax.all_gather(x, 'gz', axis=0, axis_index_groups=CORE_GROUPS)  7.07 us
  transfers between devices with their start and end apart: 14, of which 7 were waited for; matrix products, arithmetic and copies ran while one was open for 9% of the time, Pallas kernels for 0%

profile of v3, /device:TPU:1, one launch (start us, length us, event | category | flops | bytes accessed | tf_op | source)
XLA Modules:
  0.0 163.4 jit_solution(11711705131717009673)
XLA Ops:
  7.2 0.0 all-gather.7.cloned.1.call-start
  7.2 1.7 %pad_maximum_fusion = bf16[128,768]{1,0:T(8,128)(2,1)} fusion(bf16[32,768]{1,0:T(8,128)(2,1)} %param.9, bf16[96,768]{1,0:T(8,128)(2,1)} %param.7), kind=kLoop, calls=%fused_computation.9 | loop fusion | flops 393216 | bytes 393216 | tf_op jit(solution)/shard_map/concatenate | solution.py:75
  8.9 8.3 %collective-permute-start = (bf16[32,768]{1,0:T(8,128)(2,1)}, bf16[32,768]{1,0:T(8,128)(2,1)S(1)}, u32[]{:S(2)}, u32[]{:S(2)}) collective-permute-start(bf16[32,768]{1,0:T(8,128)(2,1)} %param.11), channel_id=1, source_target_pairs={{0,8},{8,0},{16,24},{24,16},{32,40},{40,32},{48,56},{56,48},{1,9},... | collective-permute-start | bytes 147464 | tf_op jit(solution)/shard_map/ppermute | solution.py:48
  17.2 13.2 %all-gather = bf16[384,768]{1,0:T(8,128)(2,1)S(1)} all-gather(bf16[96,768]{1,0:T(8,128)(2,1)} %param.10), channel_id=2, replica_groups={{0,2,4,6},{1,3,5,7},{8,10,12,14},{9,11,13,15},{16,18,20,22},{17,19,21,2..., dimensions={0}, use_global_device_ids=true | all-gather | bytes 737280 | tf_op jit(solution)/shard_map/all_gather | solution.py:80
  30.5 5.7 %collective-permute-start.1 = (bf16[4,96,768]{2,1,0:T(8,128)(2,1)S(1)}, bf16[4,96,768]{2,1,0:T(8,128)(2,1)S(1)}, u32[]{:S(2)}, u32[]{:S(2)}) collective-permute-start(bf16[4,96,768]{2,1,0:T(8,128)(2,1)S(1)} %bitcast.50), channel_id=1, source_target_pairs={{0,1},{1,0},{2,3},{3,2},{4,5},{5,4},{6,7},{7,6},{8,9},{9,8},{10,11... | collective-permute-start | bytes 1769480 | tf_op jit(solution)/shard_map/ppermute | solution.py:85
  36.2 0.8 broadcast_in_dim.4
  36.9 4.1 %all-to-all-start = ((bf16[4,2,32,768]{3,2,1,0:T(8,128)(2,1)}), bf16[4,2,32,768]{3,2,1,0:T(8,128)(2,1)S(1)}, u32[]{:S(2)}, u32[]{:S(2)}) async-start(bf16[4,2,32,768]{3,2,1,0:T(8,128)(2,1)} %broadcast_in_dim.4), calls=%async_computation | async-start | bytes 786432 | tf_op jit(solution)/shard_map/all_to_all | solution.py:21
  41.0 0.1 maximum_select_fusion
  41.1 7.8 %all-to-all-done = bf16[4,2,32,768]{3,2,1,0:T(8,128)(2,1)S(1)} async-done(((bf16[4,2,32,768]{3,2,1,0:T(8,128)(2,1)}), bf16[4,2,32,768]{3,2,1,0:T(8,128)(2,1)S(1)}, u32[]{:S(2)}, u32[]{:S(2)}) %all-to-all-start) | async-done | bytes 393248 | tf_op jit(solution)/shard_map/all_to_all | solution.py:21
  48.9 1.3 convolution_convert_fusion.2
  50.2 10.0 %all-to-all-start.1 = ((bf16[8,32,768]{2,1,0:T(8,128)(2,1)}), bf16[8,32,768]{2,1,0:T(8,128)(2,1)S(1)}, u32[]{:S(2)}, u32[]{:S(2)}) async-start(bf16[8,32,768]{2,1,0:T(8,128)(2,1)} %bitcast.7), calls=%async_computation.1 | async-start | bytes 786432 | tf_op jit(solution)/shard_map/all_to_all | solution.py:27
  60.2 0.0 all-gather.9.cloned.1.call-start
  60.2 3.7 %collective-permute-start.2 = (bf16[32,768]{1,0:T(8,128)(2,1)S(1)}, bf16[32,768]{1,0:T(8,128)(2,1)S(1)}, u32[]{:S(2)}, u32[]{:S(2)}) collective-permute-start(bf16[32,768]{1,0:T(8,128)(2,1)S(1)} %copy-done.2), channel_id=1, source_target_pairs={{0,8},{8,0},{16,24},{24,16},{32,40},{40,32},{48,56},{56,48},{1,9},... | collective-permute-start | bytes 147464 | tf_op jit(solution)/shard_map/ppermute | solution.py:48
  63.9 5.6 %collective-permute-done.2 = bf16[32,768]{1,0:T(8,128)(2,1)S(1)} collective-permute-done((bf16[32,768]{1,0:T(8,128)(2,1)S(1)}, bf16[32,768]{1,0:T(8,128)(2,1)S(1)}, u32[]{:S(2)}, u32[]{:S(2)}) %collective-permute-start.2) | collective-permute-done | bytes 49184 | tf_op jit(solution)/shard_map/ppermute | solution.py:48
  69.5 1.0 slice.12
  70.6 1.5 multiply_convert_fusion.1
  72.1 0.7 pad.4
  72.8 0.5 all-to-all-done.1
  73.3 0.1 reduce_sum.45
  73.4 0.8 broadcast_in_dim.5
  74.2 6.1 %all-to-all-start.2 = ((bf16[8,32,768]{2,1,0:T(8,128)(2,1)}), bf16[8,32,768]{2,1,0:T(8,128)(2,1)S(1)}, u32[]{:S(2)}, u32[]{:S(2)}) async-start(bf16[8,32,768]{2,1,0:T(8,128)(2,1)} %broadcast_in_dim.5), calls=%async_computation.2 | async-start | bytes 786432 | tf_op jit(solution)/shard_map/all_to_all | solution.py:21
  80.2 0.0 reduce-scatter.2.cloned.1.call-start
  80.3 10.5 %all-to-all-done.2 = bf16[8,32,768]{2,1,0:T(8,128)(2,1)S(1)} async-done(((bf16[8,32,768]{2,1,0:T(8,128)(2,1)}), bf16[8,32,768]{2,1,0:T(8,128)(2,1)S(1)}, u32[]{:S(2)}, u32[]{:S(2)}) %all-to-all-start.2) | async-done | bytes 393248 | tf_op jit(solution)/shard_map/all_to_all | solution.py:21
  90.8 0.5 reshape.70
  91.3 0.3 convolution_convert_fusion.1
  91.6 0.2 copy.14
  91.8 7.1 %all_gather.35 = bf16[2,256,768]{2,1,0:T(8,128)(2,1)S(1)} all-gather(bf16[1,256,768]{2,1,0:T(8,128)(2,1)S(1)} %copy.14), channel_id=1, replica_groups={{0,1},{2,3},{4,5},{6,7},{8,9},{10,11},{12,13},{14,15},{16,17},{18,19},{..., dimensions={0}, use_global_device_ids=true | all-gather | bytes 1179648 | tf_op jit(solution)/shard_map/all_gather | solution.py:54
  98.8 0.1 dynamic-slice_reduce_fusion
  98.9 0.2 copy.17
  99.1 17.0 %all-gather.2 = bf16[512,768]{0,1:T(8,128)(2,1)S(1)} all-gather(bf16[128,768]{0,1:T(8,128)(2,1)S(1)} %copy.17), channel_id=4, replica_groups={{0,2,4,6},{1,3,5,7},{8,10,12,14},{9,11,13,15},{16,18,20,22},{17,19,21,2..., dimensions={0}, use_global_device_ids=true | all-gather | bytes 983040 | tf_op jit(solution)/shard_map/all_gather | solution.py:58
  116.0 0.2 reshape.79
  116.2 1.0 reduce_sum.47
  117.3 2.9 %all_gather.38 = bf16[256,768]{0,1:T(8,128)(2,1)S(1)} all-gather(bf16[128,768]{0,1:T(8,128)(2,1)S(1)} %reduce_sum.47), channel_id=1, replica_groups={{0,1},{2,3},{4,5},{6,7},{8,9},{10,11},{12,13},{14,15},{16,17},{18,19},{..., dimensions={0}, use_global_device_ids=true | all-gather | bytes 589824 | tf_op jit(solution)/shard_map/all_gather | solution.py:61
  120.2 1.0 slice.14
  121.2 1.5 multiply_convert_fusion
  122.8 3.6 %all-to-all-start.3 = ((bf16[8,96,768]{2,1,0:T(8,128)(2,1)}), bf16[8,96,768]{2,1,0:T(8,128)(2,1)S(1)}, u32[]{:S(2)}, u32[]{:S(2)}) async-start(bf16[8,96,768]{2,1,0:T(8,128)(2,1)} %bitcast.26), calls=%async_computation.3 | async-start | bytes 2359296 | tf_op jit(solution)/shard_map/all_to_all | solution.py:27
  126.3 1.4 slice.13
  127.7 0.5 convolution_convert_fusion
  128.3 2.3 %collective-permute-start.3 = (bf16[2,32,768]{2,1,0:T(8,128)(2,1)S(1)}, bf16[2,32,768]{2,1,0:T(8,128)(2,1)S(1)}, u32[]{:S(2)}, u32[]{:S(2)}) collective-permute-start(bf16[2,32,768]{2,1,0:T(8,128)(2,1)S(1)} %get-tuple-element.23), channel_id=1, source_target_pairs={{0,16},{8,24},{16,32},{24,40},{32,48},{40,56},{48,0},{56,8},{1,17}... | collective-permute-start | bytes 294920 | tf_op jit(solution)/shard_map/ppermute | solution.py:42
  130.5 4.2 %collective-permute-start.5 = (bf16[2,32,768]{2,1,0:T(8,128)(2,1)S(1)}, bf16[2,32,768]{2,1,0:T(8,128)(2,1)S(1)}, u32[]{:S(2)}, u32[]{:S(2)}) collective-permute-start(bf16[2,32,768]{2,1,0:T(8,128)(2,1)S(1)} %get-tuple-element.24), channel_id=1, source_target_pairs={{0,48},{8,56},{16,0},{24,8},{32,16},{40,24},{48,32},{56,40},{1,49}... | collective-permute-start | bytes 294920 | tf_op jit(solution)/shard_map/ppermute | solution.py:42
  134.8 1.9 %collective-permute-start.4 = (bf16[2,32,768]{2,1,0:T(8,128)(2,1)S(1)}, bf16[2,32,768]{2,1,0:T(8,128)(2,1)S(1)}, u32[]{:S(2)}, u32[]{:S(2)}) collective-permute-start(bf16[2,32,768]{2,1,0:T(8,128)(2,1)S(1)} %get-tuple-element.25), channel_id=1, source_target_pairs={{0,32},{8,40},{16,48},{24,56},{32,0},{40,8},{48,16},{56,24},{1,33}... | collective-permute-start | bytes 294920 | tf_op jit(solution)/shard_map/ppermute | solution.py:42
  136.7 5.2 %collective-permute-done.4 = bf16[2,32,768]{2,1,0:T(8,128)(2,1)S(1)} collective-permute-done((bf16[2,32,768]{2,1,0:T(8,128)(2,1)S(1)}, bf16[2,32,768]{2,1,0:T(8,128)(2,1)S(1)}, u32[]{:S(2)}, u32[]{:S(2)}) %collective-permute-start.4) | collective-permute-done | bytes 98336 | tf_op jit(solution)/shard_map/ppermute | solution.py:42
  142.0 3.7 %collective-permute-start.6 = (bf16[32,768]{1,0:T(8,128)(2,1)S(1)}, bf16[32,768]{1,0:T(8,128)(2,1)S(1)}, u32[]{:S(2)}, u32[]{:S(2)}) collective-permute-start(bf16[32,768]{1,0:T(8,128)(2,1)S(1)} %fusion.4), channel_id=1, source_target_pairs={{0,8},{8,0},{16,24},{24,16},{32,40},{40,32},{48,56},{56,48},{1,9},... | collective-permute-start | bytes 147464 | tf_op jit(solution)/shard_map/ppermute | solution.py:45
  145.7 6.0 %collective-permute-done.6 = bf16[32,768]{1,0:T(8,128)(2,1)S(1)} collective-permute-done((bf16[32,768]{1,0:T(8,128)(2,1)S(1)}, bf16[32,768]{1,0:T(8,128)(2,1)S(1)}, u32[]{:S(2)}, u32[]{:S(2)}) %collective-permute-start.6) | collective-permute-done | bytes 49184 | tf_op jit(solution)/shard_map/ppermute | solution.py:45
  151.7 0.6 fusion.3
  152.4 1.6 %convert_element_type.86 = f32[96,768]{1,0:T(8,128)} convert(bf16[96,768]{1,0:T(8,128)(2,1)} %reduce-scatter.2.cloned.1.call-done) | non-fusion elementwise | flops 73728 | bytes 442368 | tf_op jit(solution)/shard_map/convert_element_type | solution.py:113
  154.0 2.0 %all-to-all-done.3 = bf16[8,96,768]{2,1,0:T(8,128)(2,1)S(1)} async-done(((bf16[8,96,768]{2,1,0:T(8,128)(2,1)}), bf16[8,96,768]{2,1,0:T(8,128)(2,1)S(1)}, u32[]{:S(2)}, u32[]{:S(2)}) %all-to-all-start.3) | async-done | bytes 1179680 | tf_op jit(solution)/shard_map/all_to_all | solution.py:27
  156.0 0.9 convert_reduce_fusion
  (21 shorter events, 0.2 us)
Async XLA Ops:
  7.2 84.1 %copy-start = (bf16[6,256,256]{2,1,0:T(8,128)(2,1)S(1)}, bf16[6,256,256]{2,1,0:T(8,128)(2,1)}, u32[]{:S(2)}) copy-start(bf16[6,256,256]{2,1,0:T(8,128)(2,1)} %param.8) | copy-start | bytes 2359300
  7.2 23.3 %copy-start.1 = (bf16[32,768]{1,0:T(8,128)(2,1)S(1)}, bf16[32,768]{1,0:T(8,128)(2,1)}, u32[]{:S(2)}) copy-start(bf16[32,768]{1,0:T(8,128)(2,1)} %param.11) | copy-start | bytes 147460
  7.2 62.3 %all-gather.7.cloned.1.call-start = ((), (), s32[]{:S(2)}) async-start(), calls=%async_computation.6 | async-start | bytes 1769472 | tf_op jit(solution)/shard_map/all_gather | solution.py:75
  8.9 21.5 %collective-permute-start = (bf16[32,768]{1,0:T(8,128)(2,1)}, bf16[32,768]{1,0:T(8,128)(2,1)S(1)}, u32[]{:S(2)}, u32[]{:S(2)}) collective-permute-start(bf16[32,768]{1,0:T(8,128)(2,1)} %param.11), channel_id=1, source_target_pairs={{0,8},{8,0},{16,24},{24,16},{32,40},{40,32},{48,56},{56,48},{1,9},... | collective-permute-start | bytes 147464 | tf_op jit(solution)/shard_map/ppermute | solution.py:48
  30.5 10.6 %collective-permute-start.1 = (bf16[4,96,768]{2,1,0:T(8,128)(2,1)S(1)}, bf16[4,96,768]{2,1,0:T(8,128)(2,1)S(1)}, u32[]{:S(2)}, u32[]{:S(2)}) collective-permute-start(bf16[4,96,768]{2,1,0:T(8,128)(2,1)S(1)} %bitcast.50), channel_id=1, source_target_pairs={{0,1},{1,0},{2,3},{3,2},{4,5},{5,4},{6,7},{7,6},{8,9},{9,8},{10,11... | collective-permute-start | bytes 1769480 | tf_op jit(solution)/shard_map/ppermute | solution.py:85
  36.9 12.0 %all-to-all-start = ((bf16[4,2,32,768]{3,2,1,0:T(8,128)(2,1)}), bf16[4,2,32,768]{3,2,1,0:T(8,128)(2,1)S(1)}, u32[]{:S(2)}, u32[]{:S(2)}) async-start(bf16[4,2,32,768]{3,2,1,0:T(8,128)(2,1)} %broadcast_in_dim.4), calls=%async_computation | async-start | bytes 786432 | tf_op jit(solution)/shard_map/all_to_all | solution.py:21
  48.9 11.3 %copy-start.2 = (bf16[32,768]{1,0:T(8,128)(2,1)S(1)}, bf16[32,768]{1,0:T(8,128)(2,1)}, u32[]{:S(2)}) copy-start(bf16[32,768]{1,0:T(8,128)(2,1)} %param.6) | copy-start | bytes 147460
  50.2 23.1 %all-to-all-start.1 = ((bf16[8,32,768]{2,1,0:T(8,128)(2,1)}), bf16[8,32,768]{2,1,0:T(8,128)(2,1)S(1)}, u32[]{:S(2)}, u32[]{:S(2)}) async-start(bf16[8,32,768]{2,1,0:T(8,128)(2,1)} %bitcast.7), calls=%async_computation.1 | async-start | bytes 786432 | tf_op jit(solution)/shard_map/all_to_all | solution.py:27
  60.2 60.0 %all-gather.9.cloned.1.call-start = ((), (), s32[]{:S(2)}) async-start(), calls=%async_computation.7 | async-start | bytes 1474560 | tf_op jit(solution)/shard_map/all_gather | solution.py:99
  60.2 9.3 %collective-permute-start.2 = (bf16[32,768]{1,0:T(8,128)(2,1)S(1)}, bf16[32,768]{1,0:T(8,128)(2,1)S(1)}, u32[]{:S(2)}, u32[]{:S(2)}) collective-permute-start(bf16[32,768]{1,0:T(8,128)(2,1)S(1)} %copy-done.2), channel_id=1, source_target_pairs={{0,8},{8,0},{16,24},{24,16},{32,40},{40,32},{48,56},{56,48},{1,9},... | collective-permute-start | bytes 147464 | tf_op jit(solution)/shard_map/ppermute | solution.py:48
  74.2 16.6 %all-to-all-start.2 = ((bf16[8,32,768]{2,1,0:T(8,128)(2,1)}), bf16[8,32,768]{2,1,0:T(8,128)(2,1)S(1)}, u32[]{:S(2)}, u32[]{:S(2)}) async-start(bf16[8,32,768]{2,1,0:T(8,128)(2,1)} %broadcast_in_dim.5), calls=%async_computation.2 | async-start | bytes 786432 | tf_op jit(solution)/shard_map/all_to_all | solution.py:21
  80.2 72.1 %reduce-scatter.2.cloned.1.call-start = ((), (), s32[]{:S(2)}) async-start(), calls=%async_computation.5 | async-start | bytes 1327104 | tf_op jit(solution)/shard_map/reduce_scatter | solution.py:106
  122.8 33.2 %all-to-all-start.3 = ((bf16[8,96,768]{2,1,0:T(8,128)(2,1)}), bf16[8,96,768]{2,1,0:T(8,128)(2,1)S(1)}, u32[]{:S(2)}, u32[]{:S(2)}) async-start(bf16[8,96,768]{2,1,0:T(8,128)(2,1)} %bitcast.26), calls=%async_computation.3 | async-start | bytes 2359296 | tf_op jit(solution)/shard_map/all_to_all | solution.py:27
  128.3 8.4 %collective-permute-start.3 = (bf16[2,32,768]{2,1,0:T(8,128)(2,1)S(1)}, bf16[2,32,768]{2,1,0:T(8,128)(2,1)S(1)}, u32[]{:S(2)}, u32[]{:S(2)}) collective-permute-start(bf16[2,32,768]{2,1,0:T(8,128)(2,1)S(1)} %get-tuple-element.23), channel_id=1, source_target_pairs={{0,16},{8,24},{16,32},{24,40},{32,48},{40,56},{48,0},{56,8},{1,17}... | collective-permute-start | bytes 294920 | tf_op jit(solution)/shard_map/ppermute | solution.py:42
  130.5 6.2 %collective-permute-start.5 = (bf16[2,32,768]{2,1,0:T(8,128)(2,1)S(1)}, bf16[2,32,768]{2,1,0:T(8,128)(2,1)S(1)}, u32[]{:S(2)}, u32[]{:S(2)}) collective-permute-start(bf16[2,32,768]{2,1,0:T(8,128)(2,1)S(1)} %get-tuple-element.24), channel_id=1, source_target_pairs={{0,48},{8,56},{16,0},{24,8},{32,16},{40,24},{48,32},{56,40},{1,49}... | collective-permute-start | bytes 294920 | tf_op jit(solution)/shard_map/ppermute | solution.py:42
  134.8 7.1 %collective-permute-start.4 = (bf16[2,32,768]{2,1,0:T(8,128)(2,1)S(1)}, bf16[2,32,768]{2,1,0:T(8,128)(2,1)S(1)}, u32[]{:S(2)}, u32[]{:S(2)}) collective-permute-start(bf16[2,32,768]{2,1,0:T(8,128)(2,1)S(1)} %get-tuple-element.25), channel_id=1, source_target_pairs={{0,32},{8,40},{16,48},{24,56},{32,0},{40,8},{48,16},{56,24},{1,33}... | collective-permute-start | bytes 294920 | tf_op jit(solution)/shard_map/ppermute | solution.py:42
  142.0 9.8 %collective-permute-start.6 = (bf16[32,768]{1,0:T(8,128)(2,1)S(1)}, bf16[32,768]{1,0:T(8,128)(2,1)S(1)}, u32[]{:S(2)}, u32[]{:S(2)}) collective-permute-start(bf16[32,768]{1,0:T(8,128)(2,1)S(1)} %fusion.4), channel_id=1, source_target_pairs={{0,8},{8,0},{16,24},{24,16},{32,40},{40,32},{48,56},{56,48},{1,9},... | collective-permute-start | bytes 147464 | tf_op jit(solution)/shard_map/ppermute | solution.py:45
Sparse Core Ops, SparseCore 0:
  10.7 44.5 all-gather.6
  73.4 25.6 all-gather.8
  117.4 30.0 reduce-scatter.1

commit v4 on v3

--- a/solution.py
+++ b/solution.py
@@ -44,10 +44,9 @@
     kept = lax.dynamic_index_in_dim(total, far, 0, False)
     return kept + lax.ppermute(sent, "gy", FAR_PAIRS).astype(F32)
 
-def far_pair(x):
-    other = lax.ppermute(x, "gy", FAR_PAIRS)
+def in_order(mine, other):
     first = (lax.axis_index("gy") & 1) == 0
-    return jnp.where(first, jnp.stack([x, other]), jnp.stack([other, x]))
+    return jnp.where(first, jnp.stack([mine, other]), jnp.stack([other, mine]))
 
 
 def all_sum_gz(x, later):
@@ -55,9 +54,10 @@
     both = both.reshape((2, 2, x.shape[0] // 2) + x.shape[1:])
     half = lax.dynamic_index_in_dim(both, lax.axis_index("gz") & 1, 1, False)
     half = jnp.sum(half.astype(F32), axis=0).astype(BF16)
-    run = lax.all_gather(half, "gz", axis=0, axis_index_groups=Y_GROUPS)
+    rows = half.shape[0]
+    run = lax.all_gather(half, "gz", axis=0, axis_index_groups=Y_GROUPS, tiled=True)
     run, later = lax.optimization_barrier((run, later))
-    half = jnp.sum(run.astype(F32), axis=0).astype(BF16)
+    half = sum(run[i : i + rows].astype(F32) for i in range(0, 4 * rows, rows)).astype(BF16)
     return lax.all_gather(half, "gz", axis=0, axis_index_groups=CORE_GROUPS, tiled=True), later
 
 
@@ -73,14 +73,12 @@
     depth = value_weight.shape[0]
 
     side = lax.all_gather(jnp.concatenate([value_weight, attended]), "gx", axis=0)
-    weight_all = side[:, :depth].reshape(-1, width)
     saved = side[:, depth:].reshape(-1, width)
 
-    pair = far_pair(out_grad)
+    other = lax.ppermute(out_grad, "gy", FAR_PAIRS)
     quarter = lax.all_gather(out_weight, "gz", axis=0, axis_index_groups=Y_GROUPS)
-    pair, quarter, late = lax.optimization_barrier((pair, quarter, inputs))
-    input_pair = far_pair(late)
-    grad_all = spread(pair, "gy", X_GROUPS).reshape(-1, out_grad.shape[1])
+    other, quarter, late = lax.optimization_barrier((other, quarter, inputs))
+    grad_all = spread(in_order(out_grad, other), "gy", X_GROUPS).reshape(-1, out_grad.shape[1])
     quarter = quarter.reshape((-1,) + out_weight.shape)
     sibling = lax.ppermute(quarter, "gz", FAR_PAIRS)
     first = (lax.axis_index("gz") & 1) == 0
@@ -91,14 +89,18 @@
 
     head_partial = dot(grad_all, out_all, ((1,), (1,))).astype(BF16)
     head_parts = exchange(head_partial, "gx")
+    other = lax.ppermute(late, "gy", FAR_PAIRS)
     out_terms = (dot(saved, grad_all, ((0,), (0,))) * grad_scale).astype(BF16)
-    input_pair, out_terms = lax.optimization_barrier((input_pair, out_terms))
-    mine = input_pair.reshape(-1, inputs.shape[1])
+    head_parts, out_terms, other = lax.optimization_barrier((head_parts, out_terms, other))
+    head_rows = jnp.sum(head_parts.astype(F32), axis=0).astype(BF16)
+    head_rows, other = lax.optimization_barrier((head_rows, other))
+    mine = in_order(late, other).reshape(-1, inputs.shape[1])
     mine = jnp.pad(mine, ((0, PAD_ROWS), (0, 0)))
-    head_parts, out_terms, mine = lax.optimization_barrier((head_parts, out_terms, mine))
+    weight_all = side[:, :depth].reshape(-1, width)
+    head_all = spread(head_rows, "gx")
     input_all = lax.all_gather(mine, "gy", axis=0, axis_index_groups=X_GROUPS)
-    head_rows = jnp.sum(head_parts.astype(F32), axis=0).astype(BF16)
-    head_grad = spread(head_rows, "gx").reshape(-1, heads, HEAD_DIM)
+    head_all, weight_all = lax.optimization_barrier((head_all, weight_all))
+    head_grad = head_all.reshape(-1, heads, HEAD_DIM)
 
     value_partial = jnp.einsum("hqk,qhd->khd", probs, head_grad, preferred_element_type=F32)
     value_partial = value_partial.reshape(-1, width).astype(BF16)

time: 165 us -> 162 us (0.982)
  starting transfers between devices: 53.6 us -> 51.1 us
    all_to_all x2, waiting for transfers between devices: 2.43 us -> 6.59 us  [exchange(): return lax.all_to_all(parts, axis, 0, 0, tiled=True)]
    all_to_all x2, starting transfers between devices: 10.2 us -> 7.54 us  [spread(): lax.all_to_all(copies, axis, 0, 0, tiled=True, axis_index_groups=groups)]
    ppermute x2, waiting for transfers between devices: 5.57 us -> 2.98 us  [the longest x1 2.97 us: body(): other = lax.ppermute(late, 'gy', FAR_PAIRS)]
  transfers between devices with their start and end apart: 14 -> 14, of which waited for: 7 -> 8; matrix products, arithmetic and copies ran while one was open for 9% -> 9% of each run, Pallas kernels for 0% -> 0%
where the time goes in v4:
time: 162 us; the launch traced here: 160 us
  starting transfers between devices  51.1 us (32%)
  blocking collectives  38.9 us (24%)
  waiting for transfers between devices  37.8 us (23%)
  between operations  14 us (9%)
  local copies, waits for them, and re-layouts  7.27 us (4%)
  other arithmetic  6.12 us (4%)
  matrix products  5.19 us (3%)
    all_to_all x2, waiting for transfers between devices, spread(): lax.all_to_all(copies, axis, 0, 0, tiled=True, axis_index_groups=groups)  18.2 us
    all_gather x1, blocking collectives, all_sum_gz(): lax.all_gather(half, 'gz', axis=0, axis_index_groups=Y_GROUPS, tiled=True)  17 us
    all_to_all x2, starting transfers between devices, exchange(): return lax.all_to_all(parts, axis, 0, 0, tiled=True)  13.5 us
    all_gather x1, blocking collectives, body(): lax.all_gather(out_weight, 'gz', axis=0, axis_index_groups=Y_GROUPS)  13.2 us
    ppermute x1, starting transfers between devices, body(): other = lax.ppermute(out_grad, 'gy', FAR_PAIRS)  8.28 us
    ppermute x3, starting transfers between devices, scatter_sum_gy(): total = total + lax.ppermute(sent, 'gy', pairs).astype(F32)  7.99 us
    all_to_all x2, starting transfers between devices, spread(): lax.all_to_all(copies, axis, 0, 0, tiled=True, axis_index_groups=groups)  7.54 us
    all_to_all x2, waiting for transfers between devices, exchange(): return lax.all_to_all(parts, axis, 0, 0, tiled=True)  6.59 us
  transfers between devices with their start and end apart: 14, of which 8 were waited for; matrix products, arithmetic and copies ran while one was open for 9% of the time, Pallas kernels for 0%

profile of v4, /device:TPU:1, one launch (start us, length us, event | category | flops | bytes accessed | tf_op | source)
XLA Modules:
  0.0 160.4 jit_solution(15581079937542490570)
XLA Ops:
  7.2 1.7 %pad_maximum_fusion = bf16[128,768]{1,0:T(8,128)(2,1)} fusion(bf16[32,768]{1,0:T(8,128)(2,1)} %param.9, bf16[96,768]{1,0:T(8,128)(2,1)} %param.7), kind=kLoop, calls=%fused_computation.10 | loop fusion | flops 393216 | bytes 393216 | tf_op jit(solution)/shard_map/concatenate | solution.py:75
  8.9 8.3 %collective-permute-start = (bf16[32,768]{1,0:T(8,128)(2,1)}, bf16[32,768]{1,0:T(8,128)(2,1)S(1)}, u32[]{:S(2)}, u32[]{:S(2)}) collective-permute-start(bf16[32,768]{1,0:T(8,128)(2,1)} %param.11), channel_id=1, source_target_pairs={{0,8},{8,0},{16,24},{24,16},{32,40},{40,32},{48,56},{56,48},{1,9},... | collective-permute-start | bytes 147464 | tf_op jit(solution)/shard_map/ppermute | solution.py:78
  17.2 13.2 %all-gather = bf16[384,768]{1,0:T(8,128)(2,1)S(1)} all-gather(bf16[96,768]{1,0:T(8,128)(2,1)} %param.10), channel_id=2, replica_groups={{0,2,4,6},{1,3,5,7},{8,10,12,14},{9,11,13,15},{16,18,20,22},{17,19,21,2..., dimensions={0}, use_global_device_ids=true | all-gather | bytes 737280 | tf_op jit(solution)/shard_map/all_gather | solution.py:79
  30.4 5.7 %collective-permute-start.1 = (bf16[4,96,768]{2,1,0:T(8,128)(2,1)S(1)}, bf16[4,96,768]{2,1,0:T(8,128)(2,1)S(1)}, u32[]{:S(2)}, u32[]{:S(2)}) collective-permute-start(bf16[4,96,768]{2,1,0:T(8,128)(2,1)S(1)} %bitcast.48), channel_id=1, source_target_pairs={{0,1},{1,0},{2,3},{3,2},{4,5},{5,4},{6,7},{7,6},{8,9},{9,8},{10,11... | collective-permute-start | bytes 1769480 | tf_op jit(solution)/shard_map/ppermute | solution.py:83
  36.2 0.8 broadcast_in_dim.4
  36.9 4.1 %all-to-all-start = ((bf16[4,2,32,768]{3,2,1,0:T(8,128)(2,1)}), bf16[4,2,32,768]{3,2,1,0:T(8,128)(2,1)S(1)}, u32[]{:S(2)}, u32[]{:S(2)}) async-start(bf16[4,2,32,768]{3,2,1,0:T(8,128)(2,1)} %broadcast_in_dim.4), calls=%async_computation | async-start | bytes 786432 | tf_op jit(solution)/shard_map/all_to_all | solution.py:21
  41.0 0.1 maximum_select_fusion
  41.1 7.8 %all-to-all-done = bf16[4,2,32,768]{3,2,1,0:T(8,128)(2,1)S(1)} async-done(((bf16[4,2,32,768]{3,2,1,0:T(8,128)(2,1)}), bf16[4,2,32,768]{3,2,1,0:T(8,128)(2,1)S(1)}, u32[]{:S(2)}, u32[]{:S(2)}) %all-to-all-start) | async-done | bytes 393248 | tf_op jit(solution)/shard_map/all_to_all | solution.py:21
  48.9 1.3 convolution_convert_fusion.2
  50.2 10.0 %all-to-all-start.1 = ((bf16[8,32,768]{2,1,0:T(8,128)(2,1)}), bf16[8,32,768]{2,1,0:T(8,128)(2,1)S(1)}, u32[]{:S(2)}, u32[]{:S(2)}) async-start(bf16[8,32,768]{2,1,0:T(8,128)(2,1)} %bitcast.7), calls=%async_computation.1 | async-start | bytes 786432 | tf_op jit(solution)/shard_map/all_to_all | solution.py:27
  60.2 3.7 %collective-permute-start.2 = (bf16[32,768]{1,0:T(8,128)(2,1)S(1)}, bf16[32,768]{1,0:T(8,128)(2,1)S(1)}, u32[]{:S(2)}, u32[]{:S(2)}) collective-permute-start(bf16[32,768]{1,0:T(8,128)(2,1)S(1)} %copy-done.3), channel_id=1, source_target_pairs={{0,8},{8,0},{16,24},{24,16},{32,40},{40,32},{48,56},{56,48},{1,9},... | collective-permute-start | bytes 147464 | tf_op jit(solution)/shard_map/ppermute | solution.py:92
  64.0 1.0 slice.28
  65.0 1.5 multiply_convert_fusion.1
  66.5 3.0 %collective-permute-done.2 = bf16[32,768]{1,0:T(8,128)(2,1)S(1)} collective-permute-done((bf16[32,768]{1,0:T(8,128)(2,1)S(1)}, bf16[32,768]{1,0:T(8,128)(2,1)S(1)}, u32[]{:S(2)}, u32[]{:S(2)}) %collective-permute-start.2) | collective-permute-done | bytes 49184 | tf_op jit(solution)/shard_map/ppermute | solution.py:92
  69.5 3.8 %all-to-all-done.1 = bf16[8,32,768]{2,1,0:T(8,128)(2,1)S(1)} async-done(((bf16[8,32,768]{2,1,0:T(8,128)(2,1)}), bf16[8,32,768]{2,1,0:T(8,128)(2,1)S(1)}, u32[]{:S(2)}, u32[]{:S(2)}) %all-to-all-start.1) | async-done | bytes 393248 | tf_op jit(solution)/shard_map/all_to_all | solution.py:27
  73.3 0.1 reduce_sum.33
  73.4 0.7 pad.4
  74.1 0.8 broadcast_in_dim.5
  74.9 3.5 %all-to-all-start.2 = ((bf16[8,32,768]{2,1,0:T(8,128)(2,1)}), bf16[8,32,768]{2,1,0:T(8,128)(2,1)S(1)}, u32[]{:S(2)}, u32[]{:S(2)}) async-start(bf16[8,32,768]{2,1,0:T(8,128)(2,1)} %broadcast_in_dim.5), calls=%async_computation.2 | async-start | bytes 786432 | tf_op jit(solution)/shard_map/all_to_all | solution.py:21
  78.4 0.0 reduce-scatter.2.cloned.1.call-start
  78.4 1.4 slice.29
  79.8 10.4 %all-to-all-done.2 = bf16[8,32,768]{2,1,0:T(8,128)(2,1)S(1)} async-done(((bf16[8,32,768]{2,1,0:T(8,128)(2,1)}), bf16[8,32,768]{2,1,0:T(8,128)(2,1)S(1)}, u32[]{:S(2)}, u32[]{:S(2)}) %all-to-all-start.2) | async-done | bytes 393248 | tf_op jit(solution)/shard_map/all_to_all | solution.py:21
  90.1 0.5 reshape.104
  90.6 0.3 convolution_convert_fusion.1
  90.9 0.2 copy.11
  91.1 5.8 %all_gather.32 = bf16[2,256,768]{2,1,0:T(8,128)(2,1)S(1)} all-gather(bf16[1,256,768]{2,1,0:T(8,128)(2,1)S(1)} %copy.11), channel_id=1, replica_groups={{0,1},{2,3},{4,5},{6,7},{8,9},{10,11},{12,13},{14,15},{16,17},{18,19},{..., dimensions={0}, use_global_device_ids=true | all-gather | bytes 1179648 | tf_op jit(solution)/shard_map/all_gather | solution.py:53
  96.9 0.1 dynamic-slice_reduce_fusion
  96.9 0.2 copy.14
  97.1 17.0 %all_gather.33 = bf16[512,768]{0,1:T(8,128)(2,1)S(1)} all-gather(bf16[128,768]{0,1:T(8,128)(2,1)S(1)} %copy.14), channel_id=1, replica_groups={{0,2,4,6},{1,3,5,7},{8,10,12,14},{9,11,13,15},{16,18,20,22},{17,19,21,2..., dimensions={0}, use_global_device_ids=true | all-gather | bytes 983040 | tf_op jit(solution)/shard_map/all_gather | solution.py:58
  114.1 0.1 add_convert_fusion
  114.2 2.9 %all_gather.34 = bf16[256,768]{0,1:T(8,128)(2,1)S(1)} all-gather(bf16[128,768]{0,1:T(8,128)(2,1)S(1)} %add_convert_fusion), channel_id=1, replica_groups={{0,1},{2,3},{4,5},{6,7},{8,9},{10,11},{12,13},{14,15},{16,17},{18,19},{..., dimensions={0}, use_global_device_ids=true | all-gather | bytes 589824 | tf_op jit(solution)/shard_map/all_gather | solution.py:61
  117.2 1.0 slice.30
  118.2 1.6 multiply_convert_fusion
  119.7 3.6 %all-to-all-start.3 = ((bf16[8,96,768]{2,1,0:T(8,128)(2,1)}), bf16[8,96,768]{2,1,0:T(8,128)(2,1)S(1)}, u32[]{:S(2)}, u32[]{:S(2)}) async-start(bf16[8,96,768]{2,1,0:T(8,128)(2,1)} %bitcast.26), calls=%async_computation.3 | async-start | bytes 2359296 | tf_op jit(solution)/shard_map/all_to_all | solution.py:27
  123.3 0.5 convolution_convert_fusion
  123.9 0.7 copy-done.1
  124.6 2.8 %collective-permute-start.5 = (bf16[2,32,768]{2,1,0:T(8,128)(2,1)S(1)}, bf16[2,32,768]{2,1,0:T(8,128)(2,1)S(1)}, u32[]{:S(2)}, u32[]{:S(2)}) collective-permute-start(bf16[2,32,768]{2,1,0:T(8,128)(2,1)S(1)} %get-tuple-element.28), channel_id=1, source_target_pairs={{0,48},{8,56},{16,0},{24,8},{32,16},{40,24},{48,32},{56,40},{1,49}... | collective-permute-start | bytes 294920 | tf_op jit(solution)/shard_map/ppermute | solution.py:42
  127.4 3.3 %collective-permute-start.4 = (bf16[2,32,768]{2,1,0:T(8,128)(2,1)S(1)}, bf16[2,32,768]{2,1,0:T(8,128)(2,1)S(1)}, u32[]{:S(2)}, u32[]{:S(2)}) collective-permute-start(bf16[2,32,768]{2,1,0:T(8,128)(2,1)S(1)} %get-tuple-element.29), channel_id=1, source_target_pairs={{0,32},{8,40},{16,48},{24,56},{32,0},{40,8},{48,16},{56,24},{1,33}... | collective-permute-start | bytes 294920 | tf_op jit(solution)/shard_map/ppermute | solution.py:42
  130.7 1.9 %collective-permute-start.3 = (bf16[2,32,768]{2,1,0:T(8,128)(2,1)S(1)}, bf16[2,32,768]{2,1,0:T(8,128)(2,1)S(1)}, u32[]{:S(2)}, u32[]{:S(2)}) collective-permute-start(bf16[2,32,768]{2,1,0:T(8,128)(2,1)S(1)} %get-tuple-element.27), channel_id=1, source_target_pairs={{0,16},{8,24},{16,32},{24,40},{32,48},{40,56},{48,0},{56,8},{1,17}... | collective-permute-start | bytes 294920 | tf_op jit(solution)/shard_map/ppermute | solution.py:42
  132.7 1.9 %collective-permute-done.4 = bf16[2,32,768]{2,1,0:T(8,128)(2,1)S(1)} collective-permute-done((bf16[2,32,768]{2,1,0:T(8,128)(2,1)S(1)}, bf16[2,32,768]{2,1,0:T(8,128)(2,1)S(1)}, u32[]{:S(2)}, u32[]{:S(2)}) %collective-permute-start.4) | collective-permute-done | bytes 98336 | tf_op jit(solution)/shard_map/ppermute | solution.py:42
  134.6 3.0 %collective-permute-done.3 = bf16[2,32,768]{2,1,0:T(8,128)(2,1)S(1)} collective-permute-done((bf16[2,32,768]{2,1,0:T(8,128)(2,1)S(1)}, bf16[2,32,768]{2,1,0:T(8,128)(2,1)S(1)}, u32[]{:S(2)}, u32[]{:S(2)}) %collective-permute-start.3) | collective-permute-done | bytes 98336 | tf_op jit(solution)/shard_map/ppermute | solution.py:42
  137.6 0.9 fusion.2
  138.6 4.2 %collective-permute-start.6 = (bf16[32,768]{1,0:T(8,128)(2,1)S(1)}, bf16[32,768]{1,0:T(8,128)(2,1)S(1)}, u32[]{:S(2)}, u32[]{:S(2)}) collective-permute-start(bf16[32,768]{1,0:T(8,128)(2,1)S(1)} %fusion.4), channel_id=1, source_target_pairs={{0,8},{8,0},{16,24},{24,16},{32,40},{40,32},{48,56},{56,48},{1,9},... | collective-permute-start | bytes 147464 | tf_op jit(solution)/shard_map/ppermute | solution.py:45
  142.8 5.1 %collective-permute-done.6 = bf16[32,768]{1,0:T(8,128)(2,1)S(1)} collective-permute-done((bf16[32,768]{1,0:T(8,128)(2,1)S(1)}, bf16[32,768]{1,0:T(8,128)(2,1)S(1)}, u32[]{:S(2)}, u32[]{:S(2)}) %collective-permute-start.6) | collective-permute-done | bytes 49184 | tf_op jit(solution)/shard_map/ppermute | solution.py:45
  147.9 0.6 fusion.3
  148.5 1.6 %convert_element_type.104 = f32[96,768]{1,0:T(8,128)} convert(bf16[96,768]{1,0:T(8,128)(2,1)} %reduce-scatter.2.cloned.1.call-done) | non-fusion elementwise | flops 73728 | bytes 442368 | tf_op jit(solution)/shard_map/convert_element_type | solution.py:115
  150.2 2.8 %all-to-all-done.3 = bf16[8,96,768]{2,1,0:T(8,128)(2,1)S(1)} async-done(((bf16[8,96,768]{2,1,0:T(8,128)(2,1)}), bf16[8,96,768]{2,1,0:T(8,128)(2,1)S(1)}, u32[]{:S(2)}, u32[]{:S(2)}) %all-to-all-start.3) | async-done | bytes 1179680 | tf_op jit(solution)/shard_map/all_to_all | solution.py:27
  153.0 0.9 convert_reduce_fusion
  (22 shorter events, 0.2 us)
Async XLA Ops:
  7.2 83.4 %copy-start = (bf16[6,256,256]{2,1,0:T(8,128)(2,1)S(1)}, bf16[6,256,256]{2,1,0:T(8,128)(2,1)}, u32[]{:S(2)}) copy-start(bf16[6,256,256]{2,1,0:T(8,128)(2,1)} %param.8) | copy-start | bytes 2359300
  7.2 29.0 %copy-start.2 = (bf16[32,768]{1,0:T(8,128)(2,1)S(1)}, bf16[32,768]{1,0:T(8,128)(2,1)}, u32[]{:S(2)}) copy-start(bf16[32,768]{1,0:T(8,128)(2,1)} %param.11) | copy-start | bytes 147460
  7.2 56.8 %all-gather.6.cloned.1.call-start = ((), (), s32[]{:S(2)}) async-start(), calls=%async_computation.6 | async-start | bytes 1769472 | tf_op jit(solution)/shard_map/all_gather | solution.py:75
  8.9 21.5 %collective-permute-start = (bf16[32,768]{1,0:T(8,128)(2,1)}, bf16[32,768]{1,0:T(8,128)(2,1)S(1)}, u32[]{:S(2)}, u32[]{:S(2)}) collective-permute-start(bf16[32,768]{1,0:T(8,128)(2,1)} %param.11), channel_id=1, source_target_pairs={{0,8},{8,0},{16,24},{24,16},{32,40},{40,32},{48,56},{56,48},{1,9},... | collective-permute-start | bytes 147464 | tf_op jit(solution)/shard_map/ppermute | solution.py:78
  30.4 10.6 %collective-permute-start.1 = (bf16[4,96,768]{2,1,0:T(8,128)(2,1)S(1)}, bf16[4,96,768]{2,1,0:T(8,128)(2,1)S(1)}, u32[]{:S(2)}, u32[]{:S(2)}) collective-permute-start(bf16[4,96,768]{2,1,0:T(8,128)(2,1)S(1)} %bitcast.48), channel_id=1, source_target_pairs={{0,1},{1,0},{2,3},{3,2},{4,5},{5,4},{6,7},{7,6},{8,9},{9,8},{10,11... | collective-permute-start | bytes 1769480 | tf_op jit(solution)/shard_map/ppermute | solution.py:83
  36.9 12.0 %all-to-all-start = ((bf16[4,2,32,768]{3,2,1,0:T(8,128)(2,1)}), bf16[4,2,32,768]{3,2,1,0:T(8,128)(2,1)S(1)}, u32[]{:S(2)}, u32[]{:S(2)}) async-start(bf16[4,2,32,768]{3,2,1,0:T(8,128)(2,1)} %broadcast_in_dim.4), calls=%async_computation | async-start | bytes 786432 | tf_op jit(solution)/shard_map/all_to_all | solution.py:21
  48.9 11.3 %copy-start.3 = (bf16[32,768]{1,0:T(8,128)(2,1)S(1)}, bf16[32,768]{1,0:T(8,128)(2,1)}, u32[]{:S(2)}) copy-start(bf16[32,768]{1,0:T(8,128)(2,1)} %param.6) | copy-start | bytes 147460
  50.2 23.1 %all-to-all-start.1 = ((bf16[8,32,768]{2,1,0:T(8,128)(2,1)}), bf16[8,32,768]{2,1,0:T(8,128)(2,1)S(1)}, u32[]{:S(2)}, u32[]{:S(2)}) async-start(bf16[8,32,768]{2,1,0:T(8,128)(2,1)} %bitcast.7), calls=%async_computation.1 | async-start | bytes 786432 | tf_op jit(solution)/shard_map/all_to_all | solution.py:27
  60.2 57.0 %all-gather.8.cloned.1.call-start = ((), (), s32[]{:S(2)}) async-start(), calls=%async_computation.7 | async-start | bytes 1474560 | tf_op jit(solution)/shard_map/all_gather | solution.py:101
  60.2 9.3 %collective-permute-start.2 = (bf16[32,768]{1,0:T(8,128)(2,1)S(1)}, bf16[32,768]{1,0:T(8,128)(2,1)S(1)}, u32[]{:S(2)}, u32[]{:S(2)}) collective-permute-start(bf16[32,768]{1,0:T(8,128)(2,1)S(1)} %copy-done.3), channel_id=1, source_target_pairs={{0,8},{8,0},{16,24},{24,16},{32,40},{40,32},{48,56},{56,48},{1,9},... | collective-permute-start | bytes 147464 | tf_op jit(solution)/shard_map/ppermute | solution.py:92
  74.9 15.2 %all-to-all-start.2 = ((bf16[8,32,768]{2,1,0:T(8,128)(2,1)}), bf16[8,32,768]{2,1,0:T(8,128)(2,1)S(1)}, u32[]{:S(2)}, u32[]{:S(2)}) async-start(bf16[8,32,768]{2,1,0:T(8,128)(2,1)} %broadcast_in_dim.5), calls=%async_computation.2 | async-start | bytes 786432 | tf_op jit(solution)/shard_map/all_to_all | solution.py:21
  78.4 70.2 %reduce-scatter.2.cloned.1.call-start = ((), (), s32[]{:S(2)}) async-start(), calls=%async_computation.5 | async-start | bytes 1327104 | tf_op jit(solution)/shard_map/reduce_scatter | solution.py:108
  119.7 33.2 %all-to-all-start.3 = ((bf16[8,96,768]{2,1,0:T(8,128)(2,1)}), bf16[8,96,768]{2,1,0:T(8,128)(2,1)S(1)}, u32[]{:S(2)}, u32[]{:S(2)}) async-start(bf16[8,96,768]{2,1,0:T(8,128)(2,1)} %bitcast.26), calls=%async_computation.3 | async-start | bytes 2359296 | tf_op jit(solution)/shard_map/all_to_all | solution.py:27
  123.9 0.7 copy-start.1
  124.6 8.0 %collective-permute-start.5 = (bf16[2,32,768]{2,1,0:T(8,128)(2,1)S(1)}, bf16[2,32,768]{2,1,0:T(8,128)(2,1)S(1)}, u32[]{:S(2)}, u32[]{:S(2)}) collective-permute-start(bf16[2,32,768]{2,1,0:T(8,128)(2,1)S(1)} %get-tuple-element.28), channel_id=1, source_target_pairs={{0,48},{8,56},{16,0},{24,8},{32,16},{40,24},{48,32},{56,40},{1,49}... | collective-permute-start | bytes 294920 | tf_op jit(solution)/shard_map/ppermute | solution.py:42
  127.4 7.2 %collective-permute-start.4 = (bf16[2,32,768]{2,1,0:T(8,128)(2,1)S(1)}, bf16[2,32,768]{2,1,0:T(8,128)(2,1)S(1)}, u32[]{:S(2)}, u32[]{:S(2)}) collective-permute-start(bf16[2,32,768]{2,1,0:T(8,128)(2,1)S(1)} %get-tuple-element.29), channel_id=1, source_target_pairs={{0,32},{8,40},{16,48},{24,56},{32,0},{40,8},{48,16},{56,24},{1,33}... | collective-permute-start | bytes 294920 | tf_op jit(solution)/shard_map/ppermute | solution.py:42
  130.7 6.9 %collective-permute-start.3 = (bf16[2,32,768]{2,1,0:T(8,128)(2,1)S(1)}, bf16[2,32,768]{2,1,0:T(8,128)(2,1)S(1)}, u32[]{:S(2)}, u32[]{:S(2)}) collective-permute-start(bf16[2,32,768]{2,1,0:T(8,128)(2,1)S(1)} %get-tuple-element.27), channel_id=1, source_target_pairs={{0,16},{8,24},{16,32},{24,40},{32,48},{40,56},{48,0},{56,8},{1,17}... | collective-permute-start | bytes 294920 | tf_op jit(solution)/shard_map/ppermute | solution.py:42
  138.6 9.4 %collective-permute-start.6 = (bf16[32,768]{1,0:T(8,128)(2,1)S(1)}, bf16[32,768]{1,0:T(8,128)(2,1)S(1)}, u32[]{:S(2)}, u32[]{:S(2)}) collective-permute-start(bf16[32,768]{1,0:T(8,128)(2,1)S(1)} %fusion.4), channel_id=1, source_target_pairs={{0,8},{8,0},{16,24},{24,16},{32,40},{40,32},{48,56},{56,48},{1,9},... | collective-permute-start | bytes 147464 | tf_op jit(solution)/shard_map/ppermute | solution.py:45
Sparse Core Ops, SparseCore 0:
  10.7 44.5 all-gather.5
  74.3 22.2 all-gather.7
  114.3 30.9 reduce-scatter.1

commit v5 on v4

--- a/solution.py
+++ b/solution.py
@@ -49,6 +49,10 @@
     return jnp.where(first, jnp.stack([mine, other]), jnp.stack([other, mine]))
 
 
+def from_run(x, k):
+    return lax.ppermute(x, "gz", [(i, i ^ (2 * k)) for i in range(8)])
+
+
 def all_sum_gz(x, later):
     both = lax.all_gather(x, "gz", axis=0, axis_index_groups=CORE_GROUPS)
     both = both.reshape((2, 2, x.shape[0] // 2) + x.shape[1:])
@@ -73,13 +77,14 @@
     depth = value_weight.shape[0]
 
     side = lax.all_gather(jnp.concatenate([value_weight, attended]), "gx", axis=0)
-    saved = side[:, depth:].reshape(-1, width)
 
     other = lax.ppermute(out_grad, "gy", FAR_PAIRS)
-    quarter = lax.all_gather(out_weight, "gz", axis=0, axis_index_groups=Y_GROUPS)
-    other, quarter, late = lax.optimization_barrier((other, quarter, inputs))
-    grad_all = spread(in_order(out_grad, other), "gy", X_GROUPS).reshape(-1, out_grad.shape[1])
-    quarter = quarter.reshape((-1,) + out_weight.shape)
+    run = [out_weight] + [from_run(out_weight, k) for k in (1, 2, 3)]
+    pair = in_order(out_grad, other).reshape(-1, out_grad.shape[1])
+    grad_all = lax.all_gather(pair, "gy", axis=0, axis_index_groups=X_GROUPS, tiled=True)
+    grad_all, *run, late = lax.optimization_barrier((grad_all, *run, inputs))
+    place = lax.axis_index("gz") >> 1
+    quarter = jnp.stack([lax.select_n(place ^ j, *run) for j in range(4)])
     sibling = lax.ppermute(quarter, "gz", FAR_PAIRS)
     first = (lax.axis_index("gz") & 1) == 0
     halves = jnp.where(
@@ -90,16 +95,17 @@
     head_partial = dot(grad_all, out_all, ((1,), (1,))).astype(BF16)
     head_parts = exchange(head_partial, "gx")
     other = lax.ppermute(late, "gy", FAR_PAIRS)
-    out_terms = (dot(saved, grad_all, ((0,), (0,))) * grad_scale).astype(BF16)
-    head_parts, out_terms, other = lax.optimization_barrier((head_parts, out_terms, other))
-    head_rows = jnp.sum(head_parts.astype(F32), axis=0).astype(BF16)
-    head_rows, other = lax.optimization_barrier((head_rows, other))
     mine = in_order(late, other).reshape(-1, inputs.shape[1])
     mine = jnp.pad(mine, ((0, PAD_ROWS), (0, 0)))
+    head_parts, mine = lax.optimization_barrier((head_parts, mine))
+    input_all = lax.all_gather(mine, "gy", axis=0, axis_index_groups=X_GROUPS)
+    head_rows = jnp.sum(head_parts.astype(F32), axis=0).astype(BF16)
+    head_rows, grad_all = lax.optimization_barrier((head_rows, grad_all))
     weight_all = side[:, :depth].reshape(-1, width)
+    saved = side[:, depth:].reshape(-1, width)
+    out_terms = (dot(saved, grad_all, ((0,), (0,))) * grad_scale).astype(BF16)
     head_all = spread(head_rows, "gx")
-    input_all = lax.all_gather(mine, "gy", axis=0, axis_index_groups=X_GROUPS)
-    head_all, weight_all = lax.optimization_barrier((head_all, weight_all))
+    head_all, weight_all, out_terms = lax.optimization_barrier((head_all, weight_all, out_terms))
     head_grad = head_all.reshape(-1, heads, HEAD_DIM)
 
     value_partial = jnp.einsum("hqk,qhd->khd", probs, head_grad, preferred_element_type=F32)

time: 162 us -> 161 us (level)
  blocking collectives: 38.9 us -> 33.2 us
  starting transfers between devices: 51.1 us -> 53.3 us
  waiting for transfers between devices: 37.8 us -> 39.5 us
    ppermute x0 -> x3, starting transfers between devices: none -> 9.28 us  [from_run(): return lax.ppermute(x, 'gz', [(i, i ^ 2 * k) for i in range(8)])]
    all_to_all x2 -> x1, waiting for transfers between devices: 18.2 us -> 11 us  [spread(): lax.all_to_all(copies, axis, 0, 0, tiled=True, axis_index_groups=groups)]
    ppermute x1, waiting for transfers between devices: 2.97 us -> 7.12 us  [body(): other = lax.ppermute(late, 'gy', FAR_PAIRS)]
    all_to_all x2 -> x1, starting transfers between devices: 7.54 us -> 3.45 us  [spread(): lax.all_to_all(copies, axis, 0, 0, tiled=True, axis_index_groups=groups)]
    all_gather x1, blocking collectives: 5.78 us -> 2.48 us  [all_sum_gz(): both = lax.all_gather(x, 'gz', axis=0, axis_index_groups=CORE_GROUPS)]
    all_gather x1, blocking collectives: 13.2 us -> 10.8 us  [body(): lax.all_gather(pair, 'gy', axis=0, axis_index_groups=X_GROUPS, tiled=True)]
    ppermute x1, waiting for transfers between devices: 5.11 us -> 7.2 us  [scatter_sum_gy(): return kept + lax.ppermute(sent, 'gy', FAR_PAIRS).astype(F32)]
    ppermute x1, starting transfers between devices: 4.24 us -> 2.19 us  [scatter_sum_gy(): return kept + lax.ppermute(sent, 'gy', FAR_PAIRS).astype(F32)]
  transfers between devices with their start and end apart: 14 -> 16, of which waited for: 8 -> 8; matrix products, arithmetic and copies ran while one was open for 9% -> 10% of each run, Pallas kernels for 0% -> 0%
where the time goes in v5:
time: 161 us; the launch traced here: 159 us
  starting transfers between devices  53.3 us (33%)
  waiting for transfers between devices  39.5 us (25%)
  blocking collectives  33.2 us (21%)
  between operations  14.1 us (9%)
  other arithmetic  7.2 us (4%)
  local copies, waits for them, and re-layouts  6.55 us (4%)
  matrix products  5.18 us (3%)
    all_gather x1, blocking collectives, all_sum_gz(): lax.all_gather(half, 'gz', axis=0, axis_index_groups=Y_GROUPS, tiled=True)  17 us
    all_to_all x2, starting transfers between devices, exchange(): return lax.all_to_all(parts, axis, 0, 0, tiled=True)  13.8 us
    all_to_all x1, waiting for transfers between devices, spread(): lax.all_to_all(copies, axis, 0, 0, tiled=True, axis_index_groups=groups)  11 us
    all_gather x1, blocking collectives, body(): lax.all_gather(pair, 'gy', axis=0, axis_index_groups=X_GROUPS, tiled=True)  10.8 us
    ppermute x3, starting transfers between devices, from_run(): return lax.ppermute(x, 'gz', [(i, i ^ 2 * k) for i in range(8)])  9.28 us
    ppermute x3, starting transfers between devices, scatter_sum_gy(): total = total + lax.ppermute(sent, 'gy', pairs).astype(F32)  8.51 us
    ppermute x1, starting transfers between devices, body(): other = lax.ppermute(out_grad, 'gy', FAR_PAIRS)  8.28 us
    all_to_all x2, waiting for transfers between devices, exchange(): return lax.all_to_all(parts, axis, 0, 0, tiled=True)  7.28 us
  transfers between devices with their start and end apart: 16, of which 8 were waited for; matrix products, arithmetic and copies ran while one was open for 10% of the time, Pallas kernels for 0%

profile of v5, /device:TPU:1, one launch (start us, length us, event | category | flops | bytes accessed | tf_op | source)
XLA Modules:
  0.0 159.0 jit_solution(2715179016348054112)
XLA Ops:
  7.2 1.7 %pad_maximum_fusion.1 = bf16[128,768]{1,0:T(8,128)(2,1)} fusion(bf16[32,768]{1,0:T(8,128)(2,1)} %param.9, bf16[96,768]{1,0:T(8,128)(2,1)} %param.7), kind=kLoop, calls=%fused_computation.11 | loop fusion | flops 393216 | bytes 393216 | tf_op jit(solution)/shard_map/concatenate | solution.py:79
  9.0 8.3 %collective-permute-start = (bf16[32,768]{1,0:T(8,128)(2,1)}, bf16[32,768]{1,0:T(8,128)(2,1)S(1)}, u32[]{:S(2)}, u32[]{:S(2)}) collective-permute-start(bf16[32,768]{1,0:T(8,128)(2,1)} %param.11), channel_id=1, source_target_pairs={{0,8},{8,0},{16,24},{24,16},{32,40},{40,32},{48,56},{56,48},{1,9},... | collective-permute-start | bytes 147464 | tf_op jit(solution)/shard_map/ppermute | solution.py:81
  17.3 2.3 %collective-permute-start.1 = (bf16[96,768]{1,0:T(8,128)(2,1)}, bf16[96,768]{1,0:T(8,128)(2,1)S(1)}, u32[]{:S(2)}, u32[]{:S(2)}) collective-permute-start(bf16[96,768]{1,0:T(8,128)(2,1)} %param.10), channel_id=1, source_target_pairs={{0,2},{1,3},{2,0},{3,1},{4,6},{5,7},{6,4},{7,5},{8,10},{9,11},{10,... | collective-permute-start | bytes 442376 | tf_op jit(solution)/shard_map/ppermute | solution.py:53
  19.6 2.4 %collective-permute-start.2 = (bf16[96,768]{1,0:T(8,128)(2,1)}, bf16[96,768]{1,0:T(8,128)(2,1)S(1)}, u32[]{:S(2)}, u32[]{:S(2)}) collective-permute-start(bf16[96,768]{1,0:T(8,128)(2,1)} %param.10), channel_id=1, source_target_pairs={{0,4},{1,5},{2,6},{3,7},{4,0},{5,1},{6,2},{7,3},{8,12},{9,13},{10,... | collective-permute-start | bytes 442376 | tf_op jit(solution)/shard_map/ppermute | solution.py:53
  22.0 4.5 %collective-permute-start.3 = (bf16[96,768]{1,0:T(8,128)(2,1)}, bf16[96,768]{1,0:T(8,128)(2,1)S(1)}, u32[]{:S(2)}, u32[]{:S(2)}) collective-permute-start(bf16[96,768]{1,0:T(8,128)(2,1)} %param.10), channel_id=1, source_target_pairs={{0,6},{1,7},{2,4},{3,5},{4,2},{5,3},{6,0},{7,1},{8,14},{9,15},{10,... | collective-permute-start | bytes 442376 | tf_op jit(solution)/shard_map/ppermute | solution.py:53
  26.6 0.9 maximum_select_fusion.1
  27.5 10.8 %all_gather.25 = bf16[256,768]{1,0:T(8,128)(2,1)S(1)} all-gather(bf16[64,768]{1,0:T(8,128)(2,1)S(1)} %bitcast.66), channel_id=1, replica_groups={{0,16,32,48},{8,24,40,56},{1,17,33,49},{9,25,41,57},{2,18,34,50},{10,26..., dimensions={0}, use_global_device_ids=true | all-gather | bytes 491520 | tf_op jit(solution)/shard_map/all_gather | solution.py:84
  38.4 0.1 fusion.5
  38.5 5.8 %collective-permute-start.4 = (bf16[4,96,768]{2,1,0:T(8,128)(2,1)S(1)}, bf16[4,96,768]{2,1,0:T(8,128)(2,1)S(1)}, u32[]{:S(2)}, u32[]{:S(2)}) collective-permute-start(bf16[4,96,768]{2,1,0:T(8,128)(2,1)S(1)} %get-tuple-element.34), channel_id=1, source_target_pairs={{0,1},{1,0},{2,3},{3,2},{4,5},{5,4},{6,7},{7,6},{8,9},{9,8},{10,11... | collective-permute-start | bytes 1769480 | tf_op jit(solution)/shard_map/ppermute | solution.py:88
  44.3 1.6 %collective-permute-done.4 = bf16[4,96,768]{2,1,0:T(8,128)(2,1)S(1)} collective-permute-done((bf16[4,96,768]{2,1,0:T(8,128)(2,1)S(1)}, bf16[4,96,768]{2,1,0:T(8,128)(2,1)S(1)}, u32[]{:S(2)}, u32[]{:S(2)}) %collective-permute-start.4) | collective-permute-done | bytes 589856 | tf_op jit(solution)/shard_map/ppermute | solution.py:88
  45.9 0.1 maximum_select_fusion
  46.0 1.3 convolution_convert_fusion.2
  47.3 10.2 %all-to-all-start = ((bf16[8,32,768]{2,1,0:T(8,128)(2,1)}), bf16[8,32,768]{2,1,0:T(8,128)(2,1)S(1)}, u32[]{:S(2)}, u32[]{:S(2)}) async-start(bf16[8,32,768]{2,1,0:T(8,128)(2,1)} %bitcast.10), calls=%async_computation | async-start | bytes 786432 | tf_op jit(solution)/shard_map/all_to_all | solution.py:27
  57.6 1.9 %collective-permute-start.5 = (bf16[32,768]{1,0:T(8,128)(2,1)S(1)}, bf16[32,768]{1,0:T(8,128)(2,1)S(1)}, u32[]{:S(2)}, u32[]{:S(2)}) collective-permute-start(bf16[32,768]{1,0:T(8,128)(2,1)S(1)} %copy-done.3), channel_id=1, source_target_pairs={{0,8},{8,0},{16,24},{24,16},{32,40},{40,32},{48,56},{56,48},{1,9},... | collective-permute-start | bytes 147464 | tf_op jit(solution)/shard_map/ppermute | solution.py:97
  59.5 7.1 %collective-permute-done.5 = bf16[32,768]{1,0:T(8,128)(2,1)S(1)} collective-permute-done((bf16[32,768]{1,0:T(8,128)(2,1)S(1)}, bf16[32,768]{1,0:T(8,128)(2,1)S(1)}, u32[]{:S(2)}, u32[]{:S(2)}) %collective-permute-start.5) | collective-permute-done | bytes 49184 | tf_op jit(solution)/shard_map/ppermute | solution.py:97
  66.7 0.7 pad.4
  67.4 5.3 %all-to-all-done = bf16[8,32,768]{2,1,0:T(8,128)(2,1)S(1)} async-done(((bf16[8,32,768]{2,1,0:T(8,128)(2,1)}), bf16[8,32,768]{2,1,0:T(8,128)(2,1)S(1)}, u32[]{:S(2)}, u32[]{:S(2)}) %all-to-all-start) | async-done | bytes 393248 | tf_op jit(solution)/shard_map/all_to_all | solution.py:27
  72.8 0.8 broadcast_in_dim.2
  73.6 3.5 %all-to-all-start.1 = ((bf16[8,32,768]{2,1,0:T(8,128)(2,1)}), bf16[8,32,768]{2,1,0:T(8,128)(2,1)S(1)}, u32[]{:S(2)}, u32[]{:S(2)}) async-start(bf16[8,32,768]{2,1,0:T(8,128)(2,1)} %broadcast_in_dim.2), calls=%async_computation.1 | async-start | bytes 786432 | tf_op jit(solution)/shard_map/all_to_all | solution.py:21
  77.1 1.4 slice.28
  78.5 1.0 slice.29
  79.5 1.6 multiply_convert_fusion.1
  81.1 11.0 %all-to-all-done.1 = bf16[8,32,768]{2,1,0:T(8,128)(2,1)S(1)} async-done(((bf16[8,32,768]{2,1,0:T(8,128)(2,1)}), bf16[8,32,768]{2,1,0:T(8,128)(2,1)S(1)}, u32[]{:S(2)}, u32[]{:S(2)}) %all-to-all-start.1) | async-done | bytes 393248 | tf_op jit(solution)/shard_map/all_to_all | solution.py:21
  92.1 0.5 reshape.64
  92.6 0.3 convolution_convert_fusion.1
  92.9 0.2 copy.11
  93.0 2.5 %all_gather.28 = bf16[2,256,768]{2,1,0:T(8,128)(2,1)S(1)} all-gather(bf16[1,256,768]{2,1,0:T(8,128)(2,1)S(1)} %copy.11), channel_id=1, replica_groups={{0,1},{2,3},{4,5},{6,7},{8,9},{10,11},{12,13},{14,15},{16,17},{18,19},{..., dimensions={0}, use_global_device_ids=true | all-gather | bytes 1179648 | tf_op jit(solution)/shard_map/all_gather | solution.py:57
  95.6 0.2 copy.14
  95.7 17.0 %all_gather.29 = bf16[512,768]{0,1:T(8,128)(2,1)S(1)} all-gather(bf16[128,768]{0,1:T(8,128)(2,1)S(1)} %copy.14), channel_id=1, replica_groups={{0,2,4,6},{1,3,5,7},{8,10,12,14},{9,11,13,15},{16,18,20,22},{17,19,21,2..., dimensions={0}, use_global_device_ids=true | all-gather | bytes 983040 | tf_op jit(solution)/shard_map/all_gather | solution.py:62
  112.7 0.1 add_convert_fusion
  112.8 2.9 %all_gather.30 = bf16[256,768]{0,1:T(8,128)(2,1)S(1)} all-gather(bf16[128,768]{0,1:T(8,128)(2,1)S(1)} %add_convert_fusion), channel_id=1, replica_groups={{0,1},{2,3},{4,5},{6,7},{8,9},{10,11},{12,13},{14,15},{16,17},{18,19},{..., dimensions={0}, use_global_device_ids=true | all-gather | bytes 589824 | tf_op jit(solution)/shard_map/all_gather | solution.py:65
  115.8 1.0 slice.30
  116.8 1.5 multiply_convert_fusion
  118.3 3.6 %all-to-all-start.2 = ((bf16[8,96,768]{2,1,0:T(8,128)(2,1)}), bf16[8,96,768]{2,1,0:T(8,128)(2,1)S(1)}, u32[]{:S(2)}, u32[]{:S(2)}) async-start(bf16[8,96,768]{2,1,0:T(8,128)(2,1)} %bitcast.29), calls=%async_computation.2 | async-start | bytes 2359296 | tf_op jit(solution)/shard_map/all_to_all | solution.py:27
  121.9 0.5 convolution_convert_fusion
  122.5 0.8 copy-done.1
  123.2 4.1 %collective-permute-start.8 = (bf16[2,32,768]{2,1,0:T(8,128)(2,1)S(1)}, bf16[2,32,768]{2,1,0:T(8,128)(2,1)S(1)}, u32[]{:S(2)}, u32[]{:S(2)}) collective-permute-start(bf16[2,32,768]{2,1,0:T(8,128)(2,1)S(1)} %get-tuple-element.40), channel_id=1, source_target_pairs={{0,48},{8,56},{16,0},{24,8},{32,16},{40,24},{48,32},{56,40},{1,49}... | collective-permute-start | bytes 294920 | tf_op jit(solution)/shard_map/ppermute | solution.py:42
  127.4 2.5 %collective-permute-start.7 = (bf16[2,32,768]{2,1,0:T(8,128)(2,1)S(1)}, bf16[2,32,768]{2,1,0:T(8,128)(2,1)S(1)}, u32[]{:S(2)}, u32[]{:S(2)}) collective-permute-start(bf16[2,32,768]{2,1,0:T(8,128)(2,1)S(1)} %get-tuple-element.41), channel_id=1, source_target_pairs={{0,32},{8,40},{16,48},{24,56},{32,0},{40,8},{48,16},{56,24},{1,33}... | collective-permute-start | bytes 294920 | tf_op jit(solution)/shard_map/ppermute | solution.py:42
  129.8 1.9 %collective-permute-start.6 = (bf16[2,32,768]{2,1,0:T(8,128)(2,1)S(1)}, bf16[2,32,768]{2,1,0:T(8,128)(2,1)S(1)}, u32[]{:S(2)}, u32[]{:S(2)}) collective-permute-start(bf16[2,32,768]{2,1,0:T(8,128)(2,1)S(1)} %get-tuple-element.39), channel_id=1, source_target_pairs={{0,16},{8,24},{16,32},{24,40},{32,48},{40,56},{48,0},{56,8},{1,17}... | collective-permute-start | bytes 294920 | tf_op jit(solution)/shard_map/ppermute | solution.py:42
  131.8 2.7 %collective-permute-done.7 = bf16[2,32,768]{2,1,0:T(8,128)(2,1)S(1)} collective-permute-done((bf16[2,32,768]{2,1,0:T(8,128)(2,1)S(1)}, bf16[2,32,768]{2,1,0:T(8,128)(2,1)S(1)}, u32[]{:S(2)}, u32[]{:S(2)}) %collective-permute-start.7) | collective-permute-done | bytes 98336 | tf_op jit(solution)/shard_map/ppermute | solution.py:42
  134.5 2.4 %collective-permute-done.6 = bf16[2,32,768]{2,1,0:T(8,128)(2,1)S(1)} collective-permute-done((bf16[2,32,768]{2,1,0:T(8,128)(2,1)S(1)}, bf16[2,32,768]{2,1,0:T(8,128)(2,1)S(1)}, u32[]{:S(2)}, u32[]{:S(2)}) %collective-permute-start.6) | collective-permute-done | bytes 98336 | tf_op jit(solution)/shard_map/ppermute | solution.py:42
  136.9 0.9 fusion.2
  137.9 2.2 %collective-permute-start.9 = (bf16[32,768]{1,0:T(8,128)(2,1)S(1)}, bf16[32,768]{1,0:T(8,128)(2,1)S(1)}, u32[]{:S(2)}, u32[]{:S(2)}) collective-permute-start(bf16[32,768]{1,0:T(8,128)(2,1)S(1)} %fusion.4), channel_id=1, source_target_pairs={{0,8},{8,0},{16,24},{24,16},{32,40},{40,32},{48,56},{56,48},{1,9},... | collective-permute-start | bytes 147464 | tf_op jit(solution)/shard_map/ppermute | solution.py:45
  140.1 7.2 %collective-permute-done.9 = bf16[32,768]{1,0:T(8,128)(2,1)S(1)} collective-permute-done((bf16[32,768]{1,0:T(8,128)(2,1)S(1)}, bf16[32,768]{1,0:T(8,128)(2,1)S(1)}, u32[]{:S(2)}, u32[]{:S(2)}) %collective-permute-start.9) | collective-permute-done | bytes 49184 | tf_op jit(solution)/shard_map/ppermute | solution.py:45
  147.3 0.6 fusion.3
  147.9 1.6 %convert_element_type.104 = f32[96,768]{1,0:T(8,128)} convert(bf16[96,768]{1,0:T(8,128)(2,1)} %reduce-scatter.2.cloned.1.call-done) | non-fusion elementwise | flops 73728 | bytes 442368 | tf_op jit(solution)/shard_map/convert_element_type | solution.py:121
  149.6 2.0 %all-to-all-done.2 = bf16[8,96,768]{2,1,0:T(8,128)(2,1)S(1)} async-done(((bf16[8,96,768]{2,1,0:T(8,128)(2,1)}), bf16[8,96,768]{2,1,0:T(8,128)(2,1)S(1)}, u32[]{:S(2)}, u32[]{:S(2)}) %all-to-all-start.2) | async-done | bytes 1179680 | tf_op jit(solution)/shard_map/all_to_all | solution.py:27
  151.6 0.9 convert_reduce_fusion
  (27 shorter events, 0.5 us)
Async XLA Ops:
  7.2 85.4 %copy-start = (bf16[6,256,256]{2,1,0:T(8,128)(2,1)S(1)}, bf16[6,256,256]{2,1,0:T(8,128)(2,1)}, u32[]{:S(2)}) copy-start(bf16[6,256,256]{2,1,0:T(8,128)(2,1)} %param.8) | copy-start | bytes 2359300
  7.2 31.1 %copy-start.2 = (bf16[96,768]{1,0:T(8,128)(2,1)S(1)}, bf16[96,768]{1,0:T(8,128)(2,1)}, u32[]{:S(2)}) copy-start(bf16[96,768]{1,0:T(8,128)(2,1)} %param.10) | copy-start | bytes 442372
  7.2 69.9 %all-gather.5.cloned.1.call-start = ((), (), s32[]{:S(2)}) async-start(), calls=%async_computation.5 | async-start | bytes 1769472 | tf_op jit(solution)/shard_map/all_gather | solution.py:79
  9.0 17.6 %collective-permute-start = (bf16[32,768]{1,0:T(8,128)(2,1)}, bf16[32,768]{1,0:T(8,128)(2,1)S(1)}, u32[]{:S(2)}, u32[]{:S(2)}) collective-permute-start(bf16[32,768]{1,0:T(8,128)(2,1)} %param.11), channel_id=1, source_target_pairs={{0,8},{8,0},{16,24},{24,16},{32,40},{40,32},{48,56},{56,48},{1,9},... | collective-permute-start | bytes 147464 | tf_op jit(solution)/shard_map/ppermute | solution.py:81
  17.3 21.0 %collective-permute-start.1 = (bf16[96,768]{1,0:T(8,128)(2,1)}, bf16[96,768]{1,0:T(8,128)(2,1)S(1)}, u32[]{:S(2)}, u32[]{:S(2)}) collective-permute-start(bf16[96,768]{1,0:T(8,128)(2,1)} %param.10), channel_id=1, source_target_pairs={{0,2},{1,3},{2,0},{3,1},{4,6},{5,7},{6,4},{7,5},{8,10},{9,11},{10,... | collective-permute-start | bytes 442376 | tf_op jit(solution)/shard_map/ppermute | solution.py:53
  19.6 18.7 %collective-permute-start.2 = (bf16[96,768]{1,0:T(8,128)(2,1)}, bf16[96,768]{1,0:T(8,128)(2,1)S(1)}, u32[]{:S(2)}, u32[]{:S(2)}) collective-permute-start(bf16[96,768]{1,0:T(8,128)(2,1)} %param.10), channel_id=1, source_target_pairs={{0,4},{1,5},{2,6},{3,7},{4,0},{5,1},{6,2},{7,3},{8,12},{9,13},{10,... | collective-permute-start | bytes 442376 | tf_op jit(solution)/shard_map/ppermute | solution.py:53
  22.0 16.3 %collective-permute-start.3 = (bf16[96,768]{1,0:T(8,128)(2,1)}, bf16[96,768]{1,0:T(8,128)(2,1)S(1)}, u32[]{:S(2)}, u32[]{:S(2)}) collective-permute-start(bf16[96,768]{1,0:T(8,128)(2,1)} %param.10), channel_id=1, source_target_pairs={{0,6},{1,7},{2,4},{3,5},{4,2},{5,3},{6,0},{7,1},{8,14},{9,15},{10,... | collective-permute-start | bytes 442376 | tf_op jit(solution)/shard_map/ppermute | solution.py:53
  38.5 7.4 %collective-permute-start.4 = (bf16[4,96,768]{2,1,0:T(8,128)(2,1)S(1)}, bf16[4,96,768]{2,1,0:T(8,128)(2,1)S(1)}, u32[]{:S(2)}, u32[]{:S(2)}) collective-permute-start(bf16[4,96,768]{2,1,0:T(8,128)(2,1)S(1)} %get-tuple-element.34), channel_id=1, source_target_pairs={{0,1},{1,0},{2,3},{3,2},{4,5},{5,4},{6,7},{7,6},{8,9},{9,8},{10,11... | collective-permute-start | bytes 1769480 | tf_op jit(solution)/shard_map/ppermute | solution.py:88
  46.0 11.6 %copy-start.3 = (bf16[32,768]{1,0:T(8,128)(2,1)S(1)}, bf16[32,768]{1,0:T(8,128)(2,1)}, u32[]{:S(2)}) copy-start(bf16[32,768]{1,0:T(8,128)(2,1)} %param.6) | copy-start | bytes 147460
  47.3 25.4 %all-to-all-start = ((bf16[8,32,768]{2,1,0:T(8,128)(2,1)}), bf16[8,32,768]{2,1,0:T(8,128)(2,1)S(1)}, u32[]{:S(2)}, u32[]{:S(2)}) async-start(bf16[8,32,768]{2,1,0:T(8,128)(2,1)} %bitcast.10), calls=%async_computation | async-start | bytes 786432 | tf_op jit(solution)/shard_map/all_to_all | solution.py:27
  57.5 58.3 %all-gather.7.cloned.1.call-start = ((), (), s32[]{:S(2)}) async-start(), calls=%async_computation.6 | async-start | bytes 1474560 | tf_op jit(solution)/shard_map/all_gather | solution.py:101
  57.6 9.0 %collective-permute-start.5 = (bf16[32,768]{1,0:T(8,128)(2,1)S(1)}, bf16[32,768]{1,0:T(8,128)(2,1)S(1)}, u32[]{:S(2)}, u32[]{:S(2)}) collective-permute-start(bf16[32,768]{1,0:T(8,128)(2,1)S(1)} %copy-done.3), channel_id=1, source_target_pairs={{0,8},{8,0},{16,24},{24,16},{32,40},{40,32},{48,56},{56,48},{1,9},... | collective-permute-start | bytes 147464 | tf_op jit(solution)/shard_map/ppermute | solution.py:97
  73.6 18.5 %all-to-all-start.1 = ((bf16[8,32,768]{2,1,0:T(8,128)(2,1)}), bf16[8,32,768]{2,1,0:T(8,128)(2,1)S(1)}, u32[]{:S(2)}, u32[]{:S(2)}) async-start(bf16[8,32,768]{2,1,0:T(8,128)(2,1)} %broadcast_in_dim.2), calls=%async_computation.1 | async-start | bytes 786432 | tf_op jit(solution)/shard_map/all_to_all | solution.py:21
  77.0 70.9 %reduce-scatter.2.cloned.1.call-start = ((), (), s32[]{:S(2)}) async-start(), calls=%async_computation.4 | async-start | bytes 1327104 | tf_op jit(solution)/shard_map/reduce_scatter | solution.py:114
  118.3 33.2 %all-to-all-start.2 = ((bf16[8,96,768]{2,1,0:T(8,128)(2,1)}), bf16[8,96,768]{2,1,0:T(8,128)(2,1)S(1)}, u32[]{:S(2)}, u32[]{:S(2)}) async-start(bf16[8,96,768]{2,1,0:T(8,128)(2,1)} %bitcast.29), calls=%async_computation.2 | async-start | bytes 2359296 | tf_op jit(solution)/shard_map/all_to_all | solution.py:27
  122.4 0.8 copy-start.1
  123.2 8.5 %collective-permute-start.8 = (bf16[2,32,768]{2,1,0:T(8,128)(2,1)S(1)}, bf16[2,32,768]{2,1,0:T(8,128)(2,1)S(1)}, u32[]{:S(2)}, u32[]{:S(2)}) collective-permute-start(bf16[2,32,768]{2,1,0:T(8,128)(2,1)S(1)} %get-tuple-element.40), channel_id=1, source_target_pairs={{0,48},{8,56},{16,0},{24,8},{32,16},{40,24},{48,32},{56,40},{1,49}... | collective-permute-start | bytes 294920 | tf_op jit(solution)/shard_map/ppermute | solution.py:42
  127.4 7.2 %collective-permute-start.7 = (bf16[2,32,768]{2,1,0:T(8,128)(2,1)S(1)}, bf16[2,32,768]{2,1,0:T(8,128)(2,1)S(1)}, u32[]{:S(2)}, u32[]{:S(2)}) collective-permute-start(bf16[2,32,768]{2,1,0:T(8,128)(2,1)S(1)} %get-tuple-element.41), channel_id=1, source_target_pairs={{0,32},{8,40},{16,48},{24,56},{32,0},{40,8},{48,16},{56,24},{1,33}... | collective-permute-start | bytes 294920 | tf_op jit(solution)/shard_map/ppermute | solution.py:42
  129.8 7.1 %collective-permute-start.6 = (bf16[2,32,768]{2,1,0:T(8,128)(2,1)S(1)}, bf16[2,32,768]{2,1,0:T(8,128)(2,1)S(1)}, u32[]{:S(2)}, u32[]{:S(2)}) collective-permute-start(bf16[2,32,768]{2,1,0:T(8,128)(2,1)S(1)} %get-tuple-element.39), channel_id=1, source_target_pairs={{0,16},{8,24},{16,32},{24,40},{32,48},{40,56},{48,0},{56,8},{1,17}... | collective-permute-start | bytes 294920 | tf_op jit(solution)/shard_map/ppermute | solution.py:42
  137.9 9.4 %collective-permute-start.9 = (bf16[32,768]{1,0:T(8,128)(2,1)S(1)}, bf16[32,768]{1,0:T(8,128)(2,1)S(1)}, u32[]{:S(2)}, u32[]{:S(2)}) collective-permute-start(bf16[32,768]{1,0:T(8,128)(2,1)S(1)} %fusion.4), channel_id=1, source_target_pairs={{0,8},{8,0},{16,24},{24,16},{32,40},{40,32},{48,56},{56,48},{1,9},... | collective-permute-start | bytes 147464 | tf_op jit(solution)/shard_map/ppermute | solution.py:45
Sparse Core Ops, SparseCore 0:
  10.7 45.0 all-gather.4
  72.8 20.3 all-gather.6
  113.0 30.1 reduce-scatter.1

commit v6 on v5

--- a/solution.py
+++ b/solution.py
@@ -10,7 +10,7 @@
 CORE_GROUPS = [[0, 1], [2, 3], [4, 5], [6, 7]]
 X_GROUPS = [[0, 2, 4, 6], [1, 3, 5, 7]]
 FAR_PAIRS = [(i, i ^ 1) for i in range(8)]
-PAD_ROWS = 128
+PAD_BLOCKS = 2
 F32 = jnp.float32
 BF16 = jnp.bfloat16
 
@@ -95,10 +95,10 @@
     head_partial = dot(grad_all, out_all, ((1,), (1,))).astype(BF16)
     head_parts = exchange(head_partial, "gx")
     other = lax.ppermute(late, "gy", FAR_PAIRS)
-    mine = in_order(late, other).reshape(-1, inputs.shape[1])
-    mine = jnp.pad(mine, ((0, PAD_ROWS), (0, 0)))
+    mine = in_order(late, other).reshape(1, -1, inputs.shape[1])
+    mine = jnp.pad(mine, ((0, PAD_BLOCKS), (0, 0), (0, 0)))
     head_parts, mine = lax.optimization_barrier((head_parts, mine))
-    input_all = lax.all_gather(mine, "gy", axis=0, axis_index_groups=X_GROUPS)
+    input_all = lax.all_gather(mine, "gy", axis=1, axis_index_groups=X_GROUPS, tiled=True)
     head_rows = jnp.sum(head_parts.astype(F32), axis=0).astype(BF16)
     head_rows, grad_all = lax.optimization_barrier((head_rows, grad_all))
     weight_all = side[:, :depth].reshape(-1, width)
@@ -113,7 +113,7 @@
     value_grad, out_terms = all_sum_gz(value_partial, out_terms)
     grad_out_weight = lax.psum_scatter(out_terms, "gz", scatter_dimension=0, tiled=True)
 
-    input_all = input_all[:, : 2 * inputs.shape[0]].reshape(-1, inputs.shape[1])
+    input_all = input_all[0]
     value_terms = (dot(input_all, value_grad, ((0,), (0,))) * grad_scale).astype(BF16)
     input_partial = dot(value_grad, weight_all, ((1,), (1,))).astype(BF16)
     grad_value_weight = scatter_sum(value_terms, "gx")

time: 161 us -> 161 us (level)
  no operation moved by 1% of the time
where the time goes in v6:
time: 161 us; the launch traced here: 159 us
  starting transfers between devices  53.4 us (33%)
  waiting for transfers between devices  39.5 us (25%)
  blocking collectives  33.2 us (21%)
  between operations  14.1 us (9%)
  other arithmetic  7.2 us (4%)
  matrix products  6.16 us (4%)
  local copies, waits for them, and re-layouts  5.51 us (3%)
    all_gather x1, blocking collectives, all_sum_gz(): lax.all_gather(half, 'gz', axis=0, axis_index_groups=Y_GROUPS, tiled=True)  17 us
    all_to_all x2, starting transfers between devices, exchange(): return lax.all_to_all(parts, axis, 0, 0, tiled=True)  13.8 us
    all_to_all x1, waiting for transfers between devices, spread(): lax.all_to_all(copies, axis, 0, 0, tiled=True, axis_index_groups=groups)  11.1 us
    all_gather x1, blocking collectives, body(): lax.all_gather(pair, 'gy', axis=0, axis_index_groups=X_GROUPS, tiled=True)  10.8 us
    ppermute x3, starting transfers between devices, from_run(): return lax.ppermute(x, 'gz', [(i, i ^ 2 * k) for i in range(8)])  9.28 us
    ppermute x3, starting transfers between devices, scatter_sum_gy(): total = total + lax.ppermute(sent, 'gy', pairs).astype(F32)  8.52 us
    ppermute x1, starting transfers between devices, body(): other = lax.ppermute(out_grad, 'gy', FAR_PAIRS)  8.28 us
    all_to_all x2, waiting for transfers between devices, exchange(): return lax.all_to_all(parts, axis, 0, 0, tiled=True)  7.3 us
  transfers between devices with their start and end apart: 16, of which 8 were waited for; matrix products, arithmetic and copies ran while one was open for 10% of the time, Pallas kernels for 0%

profile of v6, /device:TPU:1, one launch (start us, length us, event | category | flops | bytes accessed | tf_op | source)
XLA Modules:
  0.0 159.0 jit_solution(7523126787431476184)
XLA Ops:
  7.2 1.7 %pad_maximum_fusion.1 = bf16[128,768]{1,0:T(8,128)(2,1)} fusion(bf16[32,768]{1,0:T(8,128)(2,1)} %param.9, bf16[96,768]{1,0:T(8,128)(2,1)} %param.7), kind=kLoop, calls=%fused_computation.12 | loop fusion | flops 393216 | bytes 393216 | tf_op jit(solution)/shard_map/concatenate | solution.py:79
  9.0 8.3 %collective-permute-start = (bf16[32,768]{1,0:T(8,128)(2,1)}, bf16[32,768]{1,0:T(8,128)(2,1)S(1)}, u32[]{:S(2)}, u32[]{:S(2)}) collective-permute-start(bf16[32,768]{1,0:T(8,128)(2,1)} %param.11), channel_id=1, source_target_pairs={{0,8},{8,0},{16,24},{24,16},{32,40},{40,32},{48,56},{56,48},{1,9},... | collective-permute-start | bytes 147464 | tf_op jit(solution)/shard_map/ppermute | solution.py:81
  17.3 2.3 %collective-permute-start.1 = (bf16[96,768]{1,0:T(8,128)(2,1)}, bf16[96,768]{1,0:T(8,128)(2,1)S(1)}, u32[]{:S(2)}, u32[]{:S(2)}) collective-permute-start(bf16[96,768]{1,0:T(8,128)(2,1)} %param.10), channel_id=1, source_target_pairs={{0,2},{1,3},{2,0},{3,1},{4,6},{5,7},{6,4},{7,5},{8,10},{9,11},{10,... | collective-permute-start | bytes 442376 | tf_op jit(solution)/shard_map/ppermute | solution.py:53
  19.6 2.4 %collective-permute-start.2 = (bf16[96,768]{1,0:T(8,128)(2,1)}, bf16[96,768]{1,0:T(8,128)(2,1)S(1)}, u32[]{:S(2)}, u32[]{:S(2)}) collective-permute-start(bf16[96,768]{1,0:T(8,128)(2,1)} %param.10), channel_id=1, source_target_pairs={{0,4},{1,5},{2,6},{3,7},{4,0},{5,1},{6,2},{7,3},{8,12},{9,13},{10,... | collective-permute-start | bytes 442376 | tf_op jit(solution)/shard_map/ppermute | solution.py:53
  22.0 4.5 %collective-permute-start.3 = (bf16[96,768]{1,0:T(8,128)(2,1)}, bf16[96,768]{1,0:T(8,128)(2,1)S(1)}, u32[]{:S(2)}, u32[]{:S(2)}) collective-permute-start(bf16[96,768]{1,0:T(8,128)(2,1)} %param.10), channel_id=1, source_target_pairs={{0,6},{1,7},{2,4},{3,5},{4,2},{5,3},{6,0},{7,1},{8,14},{9,15},{10,... | collective-permute-start | bytes 442376 | tf_op jit(solution)/shard_map/ppermute | solution.py:53
  26.6 0.9 maximum_select_fusion.1
  27.5 10.8 %all_gather.22 = bf16[256,768]{1,0:T(8,128)(2,1)S(1)} all-gather(bf16[64,768]{1,0:T(8,128)(2,1)S(1)} %bitcast.66), channel_id=1, replica_groups={{0,16,32,48},{8,24,40,56},{1,17,33,49},{9,25,41,57},{2,18,34,50},{10,26..., dimensions={0}, use_global_device_ids=true | all-gather | bytes 491520 | tf_op jit(solution)/shard_map/all_gather | solution.py:84
  38.3 0.1 select_bitcast_fusion.3
  38.4 0.1 fusion.5
  38.5 5.8 %collective-permute-start.4 = (bf16[4,96,768]{2,1,0:T(8,128)(2,1)S(1)}, bf16[4,96,768]{2,1,0:T(8,128)(2,1)S(1)}, u32[]{:S(2)}, u32[]{:S(2)}) collective-permute-start(bf16[4,96,768]{2,1,0:T(8,128)(2,1)S(1)} %get-tuple-element.34), channel_id=1, source_target_pairs={{0,1},{1,0},{2,3},{3,2},{4,5},{5,4},{6,7},{7,6},{8,9},{9,8},{10,11... | collective-permute-start | bytes 1769480 | tf_op jit(solution)/shard_map/ppermute | solution.py:88
  44.3 1.6 %collective-permute-done.4 = bf16[4,96,768]{2,1,0:T(8,128)(2,1)S(1)} collective-permute-done((bf16[4,96,768]{2,1,0:T(8,128)(2,1)S(1)}, bf16[4,96,768]{2,1,0:T(8,128)(2,1)S(1)}, u32[]{:S(2)}, u32[]{:S(2)}) %collective-permute-start.4) | collective-permute-done | bytes 589856 | tf_op jit(solution)/shard_map/ppermute | solution.py:88
  45.9 0.1 maximum_select_fusion
  46.0 1.3 convolution_convert_fusion.2
  47.3 10.2 %all-to-all-start = ((bf16[8,32,768]{2,1,0:T(8,128)(2,1)}), bf16[8,32,768]{2,1,0:T(8,128)(2,1)S(1)}, u32[]{:S(2)}, u32[]{:S(2)}) async-start(bf16[8,32,768]{2,1,0:T(8,128)(2,1)} %bitcast.10), calls=%async_computation | async-start | bytes 786432 | tf_op jit(solution)/shard_map/all_to_all | solution.py:27
  57.6 1.9 %collective-permute-start.5 = (bf16[32,768]{1,0:T(8,128)(2,1)S(1)}, bf16[32,768]{1,0:T(8,128)(2,1)S(1)}, u32[]{:S(2)}, u32[]{:S(2)}) collective-permute-start(bf16[32,768]{1,0:T(8,128)(2,1)S(1)} %copy-done.3), channel_id=1, source_target_pairs={{0,8},{8,0},{16,24},{24,16},{32,40},{40,32},{48,56},{56,48},{1,9},... | collective-permute-start | bytes 147464 | tf_op jit(solution)/shard_map/ppermute | solution.py:97
  59.5 7.1 %collective-permute-done.5 = bf16[32,768]{1,0:T(8,128)(2,1)S(1)} collective-permute-done((bf16[32,768]{1,0:T(8,128)(2,1)S(1)}, bf16[32,768]{1,0:T(8,128)(2,1)S(1)}, u32[]{:S(2)}, u32[]{:S(2)}) %collective-permute-start.5) | collective-permute-done | bytes 49184 | tf_op jit(solution)/shard_map/ppermute | solution.py:97
  66.6 0.7 pad.4
  67.4 5.3 %all-to-all-done = bf16[8,32,768]{2,1,0:T(8,128)(2,1)S(1)} async-done(((bf16[8,32,768]{2,1,0:T(8,128)(2,1)}), bf16[8,32,768]{2,1,0:T(8,128)(2,1)S(1)}, u32[]{:S(2)}, u32[]{:S(2)}) %all-to-all-start) | async-done | bytes 393248 | tf_op jit(solution)/shard_map/all_to_all | solution.py:27
  72.8 0.8 broadcast_in_dim.2
  73.5 3.5 %all-to-all-start.1 = ((bf16[8,32,768]{2,1,0:T(8,128)(2,1)}), bf16[8,32,768]{2,1,0:T(8,128)(2,1)S(1)}, u32[]{:S(2)}, u32[]{:S(2)}) async-start(bf16[8,32,768]{2,1,0:T(8,128)(2,1)} %broadcast_in_dim.2), calls=%async_computation.1 | async-start | bytes 786432 | tf_op jit(solution)/shard_map/all_to_all | solution.py:21
  77.1 1.4 slice.28
  78.4 1.0 slice.29
  79.5 1.5 multiply_convert_fusion.1
  81.0 11.1 %all-to-all-done.1 = bf16[8,32,768]{2,1,0:T(8,128)(2,1)S(1)} async-done(((bf16[8,32,768]{2,1,0:T(8,128)(2,1)}), bf16[8,32,768]{2,1,0:T(8,128)(2,1)S(1)}, u32[]{:S(2)}, u32[]{:S(2)}) %all-to-all-start.1) | async-done | bytes 393248 | tf_op jit(solution)/shard_map/all_to_all | solution.py:21
  92.1 0.5 reshape.76
  92.5 0.3 convolution_convert_fusion.1
  92.8 0.2 copy.11
  93.0 2.5 %all_gather.25 = bf16[2,256,768]{2,1,0:T(8,128)(2,1)S(1)} all-gather(bf16[1,256,768]{2,1,0:T(8,128)(2,1)S(1)} %copy.11), channel_id=1, replica_groups={{0,1},{2,3},{4,5},{6,7},{8,9},{10,11},{12,13},{14,15},{16,17},{18,19},{..., dimensions={0}, use_global_device_ids=true | all-gather | bytes 1179648 | tf_op jit(solution)/shard_map/all_gather | solution.py:57
  95.6 0.2 copy.14
  95.7 17.0 %all_gather.26 = bf16[512,768]{0,1:T(8,128)(2,1)S(1)} all-gather(bf16[128,768]{0,1:T(8,128)(2,1)S(1)} %copy.14), channel_id=1, replica_groups={{0,2,4,6},{1,3,5,7},{8,10,12,14},{9,11,13,15},{16,18,20,22},{17,19,21,2..., dimensions={0}, use_global_device_ids=true | all-gather | bytes 983040 | tf_op jit(solution)/shard_map/all_gather | solution.py:62
  112.7 0.1 add_convert_fusion
  112.8 2.9 %all_gather.27 = bf16[256,768]{0,1:T(8,128)(2,1)S(1)} all-gather(bf16[128,768]{0,1:T(8,128)(2,1)S(1)} %add_convert_fusion), channel_id=1, replica_groups={{0,1},{2,3},{4,5},{6,7},{8,9},{10,11},{12,13},{14,15},{16,17},{18,19},{..., dimensions={0}, use_global_device_ids=true | all-gather | bytes 589824 | tf_op jit(solution)/shard_map/all_gather | solution.py:65
  115.8 2.6 %multiply_convert_fusion = bf16[768,768]{1,0:T(8,128)(2,1)} fusion(bf16[256,768]{0,1:T(8,128)(2,1)S(1)} %all_gather.27, bf16[3,256,768]{2,1,0:T(8,128)(2,1)} %all-gather.4.cloned.1.call-done), kind=kOutput, calls=%fused_computation.1 | convolution fusion | flops 303169536 | bytes 1966080 | tf_op jit(solution)/shard_map/dot_general | solution.py:69
  118.3 3.6 %all-to-all-start.2 = ((bf16[8,96,768]{2,1,0:T(8,128)(2,1)}), bf16[8,96,768]{2,1,0:T(8,128)(2,1)S(1)}, u32[]{:S(2)}, u32[]{:S(2)}) async-start(bf16[8,96,768]{2,1,0:T(8,128)(2,1)} %bitcast.62), calls=%async_computation.2 | async-start | bytes 2359296 | tf_op jit(solution)/shard_map/all_to_all | solution.py:27
  121.9 0.5 convolution_convert_fusion
  122.5 0.7 copy-done.1
  123.2 4.1 %collective-permute-start.8 = (bf16[2,32,768]{2,1,0:T(8,128)(2,1)S(1)}, bf16[2,32,768]{2,1,0:T(8,128)(2,1)S(1)}, u32[]{:S(2)}, u32[]{:S(2)}) collective-permute-start(bf16[2,32,768]{2,1,0:T(8,128)(2,1)S(1)} %get-tuple-element.40), channel_id=1, source_target_pairs={{0,48},{8,56},{16,0},{24,8},{32,16},{40,24},{48,32},{56,40},{1,49}... | collective-permute-start | bytes 294920 | tf_op jit(solution)/shard_map/ppermute | solution.py:42
  127.3 2.5 %collective-permute-start.7 = (bf16[2,32,768]{2,1,0:T(8,128)(2,1)S(1)}, bf16[2,32,768]{2,1,0:T(8,128)(2,1)S(1)}, u32[]{:S(2)}, u32[]{:S(2)}) collective-permute-start(bf16[2,32,768]{2,1,0:T(8,128)(2,1)S(1)} %get-tuple-element.41), channel_id=1, source_target_pairs={{0,32},{8,40},{16,48},{24,56},{32,0},{40,8},{48,16},{56,24},{1,33}... | collective-permute-start | bytes 294920 | tf_op jit(solution)/shard_map/ppermute | solution.py:42
  129.8 1.9 %collective-permute-start.6 = (bf16[2,32,768]{2,1,0:T(8,128)(2,1)S(1)}, bf16[2,32,768]{2,1,0:T(8,128)(2,1)S(1)}, u32[]{:S(2)}, u32[]{:S(2)}) collective-permute-start(bf16[2,32,768]{2,1,0:T(8,128)(2,1)S(1)} %get-tuple-element.39), channel_id=1, source_target_pairs={{0,16},{8,24},{16,32},{24,40},{32,48},{40,56},{48,0},{56,8},{1,17}... | collective-permute-start | bytes 294920 | tf_op jit(solution)/shard_map/ppermute | solution.py:42
  131.8 2.7 %collective-permute-done.7 = bf16[2,32,768]{2,1,0:T(8,128)(2,1)S(1)} collective-permute-done((bf16[2,32,768]{2,1,0:T(8,128)(2,1)S(1)}, bf16[2,32,768]{2,1,0:T(8,128)(2,1)S(1)}, u32[]{:S(2)}, u32[]{:S(2)}) %collective-permute-start.7) | collective-permute-done | bytes 98336 | tf_op jit(solution)/shard_map/ppermute | solution.py:42
  134.5 2.4 %collective-permute-done.6 = bf16[2,32,768]{2,1,0:T(8,128)(2,1)S(1)} collective-permute-done((bf16[2,32,768]{2,1,0:T(8,128)(2,1)S(1)}, bf16[2,32,768]{2,1,0:T(8,128)(2,1)S(1)}, u32[]{:S(2)}, u32[]{:S(2)}) %collective-permute-start.6) | collective-permute-done | bytes 98336 | tf_op jit(solution)/shard_map/ppermute | solution.py:42
  136.9 0.9 fusion.2
  137.9 2.2 %collective-permute-start.9 = (bf16[32,768]{1,0:T(8,128)(2,1)S(1)}, bf16[32,768]{1,0:T(8,128)(2,1)S(1)}, u32[]{:S(2)}, u32[]{:S(2)}) collective-permute-start(bf16[32,768]{1,0:T(8,128)(2,1)S(1)} %fusion.4), channel_id=1, source_target_pairs={{0,8},{8,0},{16,24},{24,16},{32,40},{40,32},{48,56},{56,48},{1,9},... | collective-permute-start | bytes 147464 | tf_op jit(solution)/shard_map/ppermute | solution.py:45
  140.1 7.2 %collective-permute-done.9 = bf16[32,768]{1,0:T(8,128)(2,1)S(1)} collective-permute-done((bf16[32,768]{1,0:T(8,128)(2,1)S(1)}, bf16[32,768]{1,0:T(8,128)(2,1)S(1)}, u32[]{:S(2)}, u32[]{:S(2)}) %collective-permute-start.9) | collective-permute-done | bytes 49184 | tf_op jit(solution)/shard_map/ppermute | solution.py:45
  147.3 0.6 fusion.3
  147.9 1.6 %convert_element_type.104 = f32[96,768]{1,0:T(8,128)} convert(bf16[96,768]{1,0:T(8,128)(2,1)} %reduce-scatter.2.cloned.1.call-done) | non-fusion elementwise | flops 73728 | bytes 442368 | tf_op jit(solution)/shard_map/convert_element_type | solution.py:121
  149.6 2.0 %all-to-all-done.2 = bf16[8,96,768]{2,1,0:T(8,128)(2,1)S(1)} async-done(((bf16[8,96,768]{2,1,0:T(8,128)(2,1)}), bf16[8,96,768]{2,1,0:T(8,128)(2,1)S(1)}, u32[]{:S(2)}, u32[]{:S(2)}) %all-to-all-start.2) | async-done | bytes 1179680 | tf_op jit(solution)/shard_map/all_to_all | solution.py:27
  151.6 0.9 convert_reduce_fusion
  (26 shorter events, 0.4 us)
Async XLA Ops:
  7.2 85.4 %copy-start = (bf16[6,256,256]{2,1,0:T(8,128)(2,1)S(1)}, bf16[6,256,256]{2,1,0:T(8,128)(2,1)}, u32[]{:S(2)}) copy-start(bf16[6,256,256]{2,1,0:T(8,128)(2,1)} %param.8) | copy-start | bytes 2359300
  7.2 31.1 %copy-start.2 = (bf16[96,768]{1,0:T(8,128)(2,1)S(1)}, bf16[96,768]{1,0:T(8,128)(2,1)}, u32[]{:S(2)}) copy-start(bf16[96,768]{1,0:T(8,128)(2,1)} %param.10) | copy-start | bytes 442372
  7.2 69.9 %all-gather.6.cloned.1.call-start = ((), (), s32[]{:S(2)}) async-start(), calls=%async_computation.6 | async-start | bytes 1769472 | tf_op jit(solution)/shard_map/all_gather | solution.py:79
  9.0 17.6 %collective-permute-start = (bf16[32,768]{1,0:T(8,128)(2,1)}, bf16[32,768]{1,0:T(8,128)(2,1)S(1)}, u32[]{:S(2)}, u32[]{:S(2)}) collective-permute-start(bf16[32,768]{1,0:T(8,128)(2,1)} %param.11), channel_id=1, source_target_pairs={{0,8},{8,0},{16,24},{24,16},{32,40},{40,32},{48,56},{56,48},{1,9},... | collective-permute-start | bytes 147464 | tf_op jit(solution)/shard_map/ppermute | solution.py:81
  17.3 21.0 %collective-permute-start.1 = (bf16[96,768]{1,0:T(8,128)(2,1)}, bf16[96,768]{1,0:T(8,128)(2,1)S(1)}, u32[]{:S(2)}, u32[]{:S(2)}) collective-permute-start(bf16[96,768]{1,0:T(8,128)(2,1)} %param.10), channel_id=1, source_target_pairs={{0,2},{1,3},{2,0},{3,1},{4,6},{5,7},{6,4},{7,5},{8,10},{9,11},{10,... | collective-permute-start | bytes 442376 | tf_op jit(solution)/shard_map/ppermute | solution.py:53
  19.6 18.7 %collective-permute-start.2 = (bf16[96,768]{1,0:T(8,128)(2,1)}, bf16[96,768]{1,0:T(8,128)(2,1)S(1)}, u32[]{:S(2)}, u32[]{:S(2)}) collective-permute-start(bf16[96,768]{1,0:T(8,128)(2,1)} %param.10), channel_id=1, source_target_pairs={{0,4},{1,5},{2,6},{3,7},{4,0},{5,1},{6,2},{7,3},{8,12},{9,13},{10,... | collective-permute-start | bytes 442376 | tf_op jit(solution)/shard_map/ppermute | solution.py:53
  22.0 16.3 %collective-permute-start.3 = (bf16[96,768]{1,0:T(8,128)(2,1)}, bf16[96,768]{1,0:T(8,128)(2,1)S(1)}, u32[]{:S(2)}, u32[]{:S(2)}) collective-permute-start(bf16[96,768]{1,0:T(8,128)(2,1)} %param.10), channel_id=1, source_target_pairs={{0,6},{1,7},{2,4},{3,5},{4,2},{5,3},{6,0},{7,1},{8,14},{9,15},{10,... | collective-permute-start | bytes 442376 | tf_op jit(solution)/shard_map/ppermute | solution.py:53
  38.5 7.4 %collective-permute-start.4 = (bf16[4,96,768]{2,1,0:T(8,128)(2,1)S(1)}, bf16[4,96,768]{2,1,0:T(8,128)(2,1)S(1)}, u32[]{:S(2)}, u32[]{:S(2)}) collective-permute-start(bf16[4,96,768]{2,1,0:T(8,128)(2,1)S(1)} %get-tuple-element.34), channel_id=1, source_target_pairs={{0,1},{1,0},{2,3},{3,2},{4,5},{5,4},{6,7},{7,6},{8,9},{9,8},{10,11... | collective-permute-start | bytes 1769480 | tf_op jit(solution)/shard_map/ppermute | solution.py:88
  46.0 11.5 %copy-start.3 = (bf16[32,768]{1,0:T(8,128)(2,1)S(1)}, bf16[32,768]{1,0:T(8,128)(2,1)}, u32[]{:S(2)}) copy-start(bf16[32,768]{1,0:T(8,128)(2,1)} %param.6) | copy-start | bytes 147460
  47.3 25.4 %all-to-all-start = ((bf16[8,32,768]{2,1,0:T(8,128)(2,1)}), bf16[8,32,768]{2,1,0:T(8,128)(2,1)S(1)}, u32[]{:S(2)}, u32[]{:S(2)}) async-start(bf16[8,32,768]{2,1,0:T(8,128)(2,1)} %bitcast.10), calls=%async_computation | async-start | bytes 786432 | tf_op jit(solution)/shard_map/all_to_all | solution.py:27
  57.5 58.3 %all-gather.4.cloned.1.call-start = ((), (), s32[]{:S(2)}) async-start(), calls=%async_computation.4 | async-start | bytes 1474560 | tf_op jit(solution)/shard_map/all_gather | solution.py:101
  57.6 9.0 %collective-permute-start.5 = (bf16[32,768]{1,0:T(8,128)(2,1)S(1)}, bf16[32,768]{1,0:T(8,128)(2,1)S(1)}, u32[]{:S(2)}, u32[]{:S(2)}) collective-permute-start(bf16[32,768]{1,0:T(8,128)(2,1)S(1)} %copy-done.3), channel_id=1, source_target_pairs={{0,8},{8,0},{16,24},{24,16},{32,40},{40,32},{48,56},{56,48},{1,9},... | collective-permute-start | bytes 147464 | tf_op jit(solution)/shard_map/ppermute | solution.py:97
  73.5 18.5 %all-to-all-start.1 = ((bf16[8,32,768]{2,1,0:T(8,128)(2,1)}), bf16[8,32,768]{2,1,0:T(8,128)(2,1)S(1)}, u32[]{:S(2)}, u32[]{:S(2)}) async-start(bf16[8,32,768]{2,1,0:T(8,128)(2,1)} %broadcast_in_dim.2), calls=%async_computation.1 | async-start | bytes 786432 | tf_op jit(solution)/shard_map/all_to_all | solution.py:21
  77.0 70.9 %reduce-scatter.2.cloned.1.call-start = ((), (), s32[]{:S(2)}) async-start(), calls=%async_computation.5 | async-start | bytes 1327104 | tf_op jit(solution)/shard_map/reduce_scatter | solution.py:114
  118.3 33.2 %all-to-all-start.2 = ((bf16[8,96,768]{2,1,0:T(8,128)(2,1)}), bf16[8,96,768]{2,1,0:T(8,128)(2,1)S(1)}, u32[]{:S(2)}, u32[]{:S(2)}) async-start(bf16[8,96,768]{2,1,0:T(8,128)(2,1)} %bitcast.62), calls=%async_computation.2 | async-start | bytes 2359296 | tf_op jit(solution)/shard_map/all_to_all | solution.py:27
  122.4 0.8 copy-start.1
  123.2 8.5 %collective-permute-start.8 = (bf16[2,32,768]{2,1,0:T(8,128)(2,1)S(1)}, bf16[2,32,768]{2,1,0:T(8,128)(2,1)S(1)}, u32[]{:S(2)}, u32[]{:S(2)}) collective-permute-start(bf16[2,32,768]{2,1,0:T(8,128)(2,1)S(1)} %get-tuple-element.40), channel_id=1, source_target_pairs={{0,48},{8,56},{16,0},{24,8},{32,16},{40,24},{48,32},{56,40},{1,49}... | collective-permute-start | bytes 294920 | tf_op jit(solution)/shard_map/ppermute | solution.py:42
  127.3 7.2 %collective-permute-start.7 = (bf16[2,32,768]{2,1,0:T(8,128)(2,1)S(1)}, bf16[2,32,768]{2,1,0:T(8,128)(2,1)S(1)}, u32[]{:S(2)}, u32[]{:S(2)}) collective-permute-start(bf16[2,32,768]{2,1,0:T(8,128)(2,1)S(1)} %get-tuple-element.41), channel_id=1, source_target_pairs={{0,32},{8,40},{16,48},{24,56},{32,0},{40,8},{48,16},{56,24},{1,33}... | collective-permute-start | bytes 294920 | tf_op jit(solution)/shard_map/ppermute | solution.py:42
  129.8 7.1 %collective-permute-start.6 = (bf16[2,32,768]{2,1,0:T(8,128)(2,1)S(1)}, bf16[2,32,768]{2,1,0:T(8,128)(2,1)S(1)}, u32[]{:S(2)}, u32[]{:S(2)}) collective-permute-start(bf16[2,32,768]{2,1,0:T(8,128)(2,1)S(1)} %get-tuple-element.39), channel_id=1, source_target_pairs={{0,16},{8,24},{16,32},{24,40},{32,48},{40,56},{48,0},{56,8},{1,17}... | collective-permute-start | bytes 294920 | tf_op jit(solution)/shard_map/ppermute | solution.py:42
  137.9 9.4 %collective-permute-start.9 = (bf16[32,768]{1,0:T(8,128)(2,1)S(1)}, bf16[32,768]{1,0:T(8,128)(2,1)S(1)}, u32[]{:S(2)}, u32[]{:S(2)}) collective-permute-start(bf16[32,768]{1,0:T(8,128)(2,1)S(1)} %fusion.4), channel_id=1, source_target_pairs={{0,8},{8,0},{16,24},{24,16},{32,40},{40,32},{48,56},{56,48},{1,9},... | collective-permute-start | bytes 147464 | tf_op jit(solution)/shard_map/ppermute | solution.py:45
Sparse Core Ops, SparseCore 0:
  10.7 45.0 all-gather.5
  72.8 20.3 all-gather.3
  113.0 30.1 reduce-scatter.1

commit v7 on v6

--- a/solution.py
+++ b/solution.py
@@ -31,7 +31,7 @@
     return jnp.sum(exchange(x, axis).astype(F32), axis=0)
 
 
-def scatter_sum_gy(x):
+def scatter_sum_gy(x, beside):
     me = lax.axis_index("gy")
     ring, far = me >> 1, me & 1
     parts = x.reshape((4, 2, x.shape[0] // 8) + x.shape[1:])
@@ -42,7 +42,8 @@
         total = total + lax.ppermute(sent, "gy", pairs).astype(F32)
     sent = lax.dynamic_index_in_dim(total, 1 - far, 0, False).astype(BF16)
     kept = lax.dynamic_index_in_dim(total, far, 0, False)
-    return kept + lax.ppermute(sent, "gy", FAR_PAIRS).astype(F32)
+    received, beside = lax.optimization_barrier((lax.ppermute(sent, "gy", FAR_PAIRS), beside))
+    return kept + received.astype(F32), beside
 
 def in_order(mine, other):
     first = (lax.axis_index("gy") & 1) == 0
@@ -117,8 +118,9 @@
     value_terms = (dot(input_all, value_grad, ((0,), (0,))) * grad_scale).astype(BF16)
     input_partial = dot(value_grad, weight_all, ((1,), (1,))).astype(BF16)
     grad_value_weight = scatter_sum(value_terms, "gx")
-    grad_inputs = scatter_sum_gy(input_partial)
-    return grad_inputs.astype(BF16), grad_value_weight.astype(F32), grad_out_weight.astype(F32)
+    grad_out_weight = grad_out_weight.astype(F32)
+    grad_inputs, grad_out_weight = scatter_sum_gy(input_partial, grad_out_weight)
+    return grad_inputs.astype(BF16), grad_value_weight.astype(F32), grad_out_weight
 
 
 def solution(mesh):

time: 161 us -> 161 us (level)
    ppermute x1, waiting for transfers between devices: 7.18 us -> 1.96 us  [scatter_sum_gy(): lax.ppermute(sent, 'gy', FAR_PAIRS)]
    reduce_scatter x1, waiting for transfers between devices: 0.01 us -> 3.14 us  [body(): lax.psum_scatter(out_terms, 'gz', scatter_dimension=0, tiled=True)]
    all_to_all x2, waiting for transfers between devices: 7.3 us -> 9.39 us  [exchange(): return lax.all_to_all(parts, axis, 0, 0, tiled=True)]
  transfers between devices with their start and end apart: 16 -> 16, of which waited for: 8 -> 9; matrix products, arithmetic and copies ran while one was open for 10% -> 10% of each run, Pallas kernels for 0% -> 0%
where the time goes in v7:
time: 161 us; the launch traced here: 159 us
  starting transfers between devices  53.3 us (33%)
  waiting for transfers between devices  39.5 us (25%)
  blocking collectives  33.2 us (21%)
  between operations  14.1 us (9%)
  other arithmetic  7.2 us (4%)
  matrix products  6.16 us (4%)
  local copies, waits for them, and re-layouts  5.51 us (3%)
    all_gather x1, blocking collectives, all_sum_gz(): lax.all_gather(half, 'gz', axis=0, axis_index_groups=Y_GROUPS, tiled=True)  17 us
    all_to_all x2, starting transfers between devices, exchange(): return lax.all_to_all(parts, axis, 0, 0, tiled=True)  13.8 us
    all_to_all x1, waiting for transfers between devices, spread(): lax.all_to_all(copies, axis, 0, 0, tiled=True, axis_index_groups=groups)  11.1 us
    all_gather x1, blocking collectives, body(): lax.all_gather(pair, 'gy', axis=0, axis_index_groups=X_GROUPS, tiled=True)  10.8 us
    all_to_all x2, waiting for transfers between devices, exchange(): return lax.all_to_all(parts, axis, 0, 0, tiled=True)  9.39 us
    ppermute x3, starting transfers between devices, from_run(): return lax.ppermute(x, 'gz', [(i, i ^ 2 * k) for i in range(8)])  9.28 us
    ppermute x3, starting transfers between devices, scatter_sum_gy(): total = total + lax.ppermute(sent, 'gy', pairs).astype(F32)  8.51 us
    ppermute x1, starting transfers between devices, body(): other = lax.ppermute(out_grad, 'gy', FAR_PAIRS)  8.28 us
  transfers between devices with their start and end apart: 16, of which 9 were waited for; matrix products, arithmetic and copies ran while one was open for 10% of the time, Pallas kernels for 0%

profile of v7, /device:TPU:1, one launch (start us, length us, event | category | flops | bytes accessed | tf_op | source)
XLA Modules:
  0.0 159.0 jit_solution(3528865647642279018)
XLA Ops:
  7.2 1.7 %pad_maximum_fusion.1 = bf16[128,768]{1,0:T(8,128)(2,1)} fusion(bf16[32,768]{1,0:T(8,128)(2,1)} %param.9, bf16[96,768]{1,0:T(8,128)(2,1)} %param.7), kind=kLoop, calls=%fused_computation.12 | loop fusion | flops 393216 | bytes 393216 | tf_op jit(solution)/shard_map/concatenate | solution.py:80
  9.0 8.3 %collective-permute-start = (bf16[32,768]{1,0:T(8,128)(2,1)}, bf16[32,768]{1,0:T(8,128)(2,1)S(1)}, u32[]{:S(2)}, u32[]{:S(2)}) collective-permute-start(bf16[32,768]{1,0:T(8,128)(2,1)} %param.11), channel_id=1, source_target_pairs={{0,8},{8,0},{16,24},{24,16},{32,40},{40,32},{48,56},{56,48},{1,9},... | collective-permute-start | bytes 147464 | tf_op jit(solution)/shard_map/ppermute | solution.py:82
  17.3 2.3 %collective-permute-start.1 = (bf16[96,768]{1,0:T(8,128)(2,1)}, bf16[96,768]{1,0:T(8,128)(2,1)S(1)}, u32[]{:S(2)}, u32[]{:S(2)}) collective-permute-start(bf16[96,768]{1,0:T(8,128)(2,1)} %param.10), channel_id=1, source_target_pairs={{0,2},{1,3},{2,0},{3,1},{4,6},{5,7},{6,4},{7,5},{8,10},{9,11},{10,... | collective-permute-start | bytes 442376 | tf_op jit(solution)/shard_map/ppermute | solution.py:54
  19.6 2.4 %collective-permute-start.2 = (bf16[96,768]{1,0:T(8,128)(2,1)}, bf16[96,768]{1,0:T(8,128)(2,1)S(1)}, u32[]{:S(2)}, u32[]{:S(2)}) collective-permute-start(bf16[96,768]{1,0:T(8,128)(2,1)} %param.10), channel_id=1, source_target_pairs={{0,4},{1,5},{2,6},{3,7},{4,0},{5,1},{6,2},{7,3},{8,12},{9,13},{10,... | collective-permute-start | bytes 442376 | tf_op jit(solution)/shard_map/ppermute | solution.py:54
  22.0 4.5 %collective-permute-start.3 = (bf16[96,768]{1,0:T(8,128)(2,1)}, bf16[96,768]{1,0:T(8,128)(2,1)S(1)}, u32[]{:S(2)}, u32[]{:S(2)}) collective-permute-start(bf16[96,768]{1,0:T(8,128)(2,1)} %param.10), channel_id=1, source_target_pairs={{0,6},{1,7},{2,4},{3,5},{4,2},{5,3},{6,0},{7,1},{8,14},{9,15},{10,... | collective-permute-start | bytes 442376 | tf_op jit(solution)/shard_map/ppermute | solution.py:54
  26.6 0.9 maximum_select_fusion.1
  27.5 10.8 %all_gather.22 = bf16[256,768]{1,0:T(8,128)(2,1)S(1)} all-gather(bf16[64,768]{1,0:T(8,128)(2,1)S(1)} %bitcast.66), channel_id=1, replica_groups={{0,16,32,48},{8,24,40,56},{1,17,33,49},{9,25,41,57},{2,18,34,50},{10,26..., dimensions={0}, use_global_device_ids=true | all-gather | bytes 491520 | tf_op jit(solution)/shard_map/all_gather | solution.py:85
  38.4 0.1 fusion.5
  38.5 5.8 %collective-permute-start.4 = (bf16[4,96,768]{2,1,0:T(8,128)(2,1)S(1)}, bf16[4,96,768]{2,1,0:T(8,128)(2,1)S(1)}, u32[]{:S(2)}, u32[]{:S(2)}) collective-permute-start(bf16[4,96,768]{2,1,0:T(8,128)(2,1)S(1)} %get-tuple-element.38), channel_id=1, source_target_pairs={{0,1},{1,0},{2,3},{3,2},{4,5},{5,4},{6,7},{7,6},{8,9},{9,8},{10,11... | collective-permute-start | bytes 1769480 | tf_op jit(solution)/shard_map/ppermute | solution.py:89
  44.3 1.6 %collective-permute-done.4 = bf16[4,96,768]{2,1,0:T(8,128)(2,1)S(1)} collective-permute-done((bf16[4,96,768]{2,1,0:T(8,128)(2,1)S(1)}, bf16[4,96,768]{2,1,0:T(8,128)(2,1)S(1)}, u32[]{:S(2)}, u32[]{:S(2)}) %collective-permute-start.4) | collective-permute-done | bytes 589856 | tf_op jit(solution)/shard_map/ppermute | solution.py:89
  45.9 0.1 maximum_select_fusion
  46.0 1.3 convolution_convert_fusion.2
  47.3 10.2 %all-to-all-start = ((bf16[8,32,768]{2,1,0:T(8,128)(2,1)}), bf16[8,32,768]{2,1,0:T(8,128)(2,1)S(1)}, u32[]{:S(2)}, u32[]{:S(2)}) async-start(bf16[8,32,768]{2,1,0:T(8,128)(2,1)} %bitcast.10), calls=%async_computation | async-start | bytes 786432 | tf_op jit(solution)/shard_map/all_to_all | solution.py:27
  57.6 1.9 %collective-permute-start.5 = (bf16[32,768]{1,0:T(8,128)(2,1)S(1)}, bf16[32,768]{1,0:T(8,128)(2,1)S(1)}, u32[]{:S(2)}, u32[]{:S(2)}) collective-permute-start(bf16[32,768]{1,0:T(8,128)(2,1)S(1)} %copy-done.3), channel_id=1, source_target_pairs={{0,8},{8,0},{16,24},{24,16},{32,40},{40,32},{48,56},{56,48},{1,9},... | collective-permute-start | bytes 147464 | tf_op jit(solution)/shard_map/ppermute | solution.py:98
  59.5 7.1 %collective-permute-done.5 = bf16[32,768]{1,0:T(8,128)(2,1)S(1)} collective-permute-done((bf16[32,768]{1,0:T(8,128)(2,1)S(1)}, bf16[32,768]{1,0:T(8,128)(2,1)S(1)}, u32[]{:S(2)}, u32[]{:S(2)}) %collective-permute-start.5) | collective-permute-done | bytes 49184 | tf_op jit(solution)/shard_map/ppermute | solution.py:98
  66.6 0.7 pad.4
  67.4 5.3 %all-to-all-done = bf16[8,32,768]{2,1,0:T(8,128)(2,1)S(1)} async-done(((bf16[8,32,768]{2,1,0:T(8,128)(2,1)}), bf16[8,32,768]{2,1,0:T(8,128)(2,1)S(1)}, u32[]{:S(2)}, u32[]{:S(2)}) %all-to-all-start) | async-done | bytes 393248 | tf_op jit(solution)/shard_map/all_to_all | solution.py:27
  72.8 0.8 broadcast_in_dim.2
  73.5 3.5 %all-to-all-start.1 = ((bf16[8,32,768]{2,1,0:T(8,128)(2,1)}), bf16[8,32,768]{2,1,0:T(8,128)(2,1)S(1)}, u32[]{:S(2)}, u32[]{:S(2)}) async-start(bf16[8,32,768]{2,1,0:T(8,128)(2,1)} %broadcast_in_dim.2), calls=%async_computation.1 | async-start | bytes 786432 | tf_op jit(solution)/shard_map/all_to_all | solution.py:21
  77.1 1.4 slice.28
  78.4 1.0 slice.29
  79.5 1.5 multiply_convert_fusion.1
  81.0 11.1 %all-to-all-done.1 = bf16[8,32,768]{2,1,0:T(8,128)(2,1)S(1)} async-done(((bf16[8,32,768]{2,1,0:T(8,128)(2,1)}), bf16[8,32,768]{2,1,0:T(8,128)(2,1)S(1)}, u32[]{:S(2)}, u32[]{:S(2)}) %all-to-all-start.1) | async-done | bytes 393248 | tf_op jit(solution)/shard_map/all_to_all | solution.py:21
  92.1 0.5 reshape.76
  92.5 0.3 convolution_convert_fusion.1
  92.8 0.2 copy.11
  93.0 2.5 %all_gather.25 = bf16[2,256,768]{2,1,0:T(8,128)(2,1)S(1)} all-gather(bf16[1,256,768]{2,1,0:T(8,128)(2,1)S(1)} %copy.11), channel_id=1, replica_groups={{0,1},{2,3},{4,5},{6,7},{8,9},{10,11},{12,13},{14,15},{16,17},{18,19},{..., dimensions={0}, use_global_device_ids=true | all-gather | bytes 1179648 | tf_op jit(solution)/shard_map/all_gather | solution.py:58
  95.6 0.2 copy.14
  95.7 17.0 %all_gather.26 = bf16[512,768]{0,1:T(8,128)(2,1)S(1)} all-gather(bf16[128,768]{0,1:T(8,128)(2,1)S(1)} %copy.14), channel_id=1, replica_groups={{0,2,4,6},{1,3,5,7},{8,10,12,14},{9,11,13,15},{16,18,20,22},{17,19,21,2..., dimensions={0}, use_global_device_ids=true | all-gather | bytes 983040 | tf_op jit(solution)/shard_map/all_gather | solution.py:63
  112.7 0.1 add_convert_fusion
  112.8 2.9 %all_gather.27 = bf16[256,768]{0,1:T(8,128)(2,1)S(1)} all-gather(bf16[128,768]{0,1:T(8,128)(2,1)S(1)} %add_convert_fusion), channel_id=1, replica_groups={{0,1},{2,3},{4,5},{6,7},{8,9},{10,11},{12,13},{14,15},{16,17},{18,19},{..., dimensions={0}, use_global_device_ids=true | all-gather | bytes 589824 | tf_op jit(solution)/shard_map/all_gather | solution.py:66
  115.8 2.6 %multiply_convert_fusion = bf16[768,768]{1,0:T(8,128)(2,1)} fusion(bf16[256,768]{0,1:T(8,128)(2,1)S(1)} %all_gather.27, bf16[3,256,768]{2,1,0:T(8,128)(2,1)} %all-gather.4.cloned.1.call-done), kind=kOutput, calls=%fused_computation.1 | convolution fusion | flops 303169536 | bytes 1966080 | tf_op jit(solution)/shard_map/dot_general | solution.py:70
  118.3 3.6 %all-to-all-start.2 = ((bf16[8,96,768]{2,1,0:T(8,128)(2,1)}), bf16[8,96,768]{2,1,0:T(8,128)(2,1)S(1)}, u32[]{:S(2)}, u32[]{:S(2)}) async-start(bf16[8,96,768]{2,1,0:T(8,128)(2,1)} %bitcast.62), calls=%async_computation.3 | async-start | bytes 2359296 | tf_op jit(solution)/shard_map/all_to_all | solution.py:27
  121.9 0.5 convolution_convert_fusion
  122.5 0.7 copy-done.1
  123.2 4.1 %collective-permute-start.8 = (bf16[2,32,768]{2,1,0:T(8,128)(2,1)S(1)}, bf16[2,32,768]{2,1,0:T(8,128)(2,1)S(1)}, u32[]{:S(2)}, u32[]{:S(2)}) collective-permute-start(bf16[2,32,768]{2,1,0:T(8,128)(2,1)S(1)} %get-tuple-element.44), channel_id=1, source_target_pairs={{0,48},{8,56},{16,0},{24,8},{32,16},{40,24},{48,32},{56,40},{1,49}... | collective-permute-start | bytes 294920 | tf_op jit(solution)/shard_map/ppermute | solution.py:42
  127.3 2.5 %collective-permute-start.7 = (bf16[2,32,768]{2,1,0:T(8,128)(2,1)S(1)}, bf16[2,32,768]{2,1,0:T(8,128)(2,1)S(1)}, u32[]{:S(2)}, u32[]{:S(2)}) collective-permute-start(bf16[2,32,768]{2,1,0:T(8,128)(2,1)S(1)} %get-tuple-element.45), channel_id=1, source_target_pairs={{0,32},{8,40},{16,48},{24,56},{32,0},{40,8},{48,16},{56,24},{1,33}... | collective-permute-start | bytes 294920 | tf_op jit(solution)/shard_map/ppermute | solution.py:42
  129.8 1.9 %collective-permute-start.6 = (bf16[2,32,768]{2,1,0:T(8,128)(2,1)S(1)}, bf16[2,32,768]{2,1,0:T(8,128)(2,1)S(1)}, u32[]{:S(2)}, u32[]{:S(2)}) collective-permute-start(bf16[2,32,768]{2,1,0:T(8,128)(2,1)S(1)} %get-tuple-element.43), channel_id=1, source_target_pairs={{0,16},{8,24},{16,32},{24,40},{32,48},{40,56},{48,0},{56,8},{1,17}... | collective-permute-start | bytes 294920 | tf_op jit(solution)/shard_map/ppermute | solution.py:42
  131.8 2.7 %collective-permute-done.7 = bf16[2,32,768]{2,1,0:T(8,128)(2,1)S(1)} collective-permute-done((bf16[2,32,768]{2,1,0:T(8,128)(2,1)S(1)}, bf16[2,32,768]{2,1,0:T(8,128)(2,1)S(1)}, u32[]{:S(2)}, u32[]{:S(2)}) %collective-permute-start.7) | collective-permute-done | bytes 98336 | tf_op jit(solution)/shard_map/ppermute | solution.py:42
  134.5 2.4 %collective-permute-done.6 = bf16[2,32,768]{2,1,0:T(8,128)(2,1)S(1)} collective-permute-done((bf16[2,32,768]{2,1,0:T(8,128)(2,1)S(1)}, bf16[2,32,768]{2,1,0:T(8,128)(2,1)S(1)}, u32[]{:S(2)}, u32[]{:S(2)}) %collective-permute-start.6) | collective-permute-done | bytes 98336 | tf_op jit(solution)/shard_map/ppermute | solution.py:42
  136.9 0.9 fusion.2
  137.9 2.2 %collective-permute-start.9 = (bf16[32,768]{1,0:T(8,128)(2,1)S(1)}, bf16[32,768]{1,0:T(8,128)(2,1)S(1)}, u32[]{:S(2)}, u32[]{:S(2)}) collective-permute-start(bf16[32,768]{1,0:T(8,128)(2,1)S(1)} %fusion.4), channel_id=1, source_target_pairs={{0,8},{8,0},{16,24},{24,16},{32,40},{40,32},{48,56},{56,48},{1,9},... | collective-permute-start | bytes 147464 | tf_op jit(solution)/shard_map/ppermute | solution.py:45
  140.1 3.1 %reduce-scatter.2.cloned.1.call-done = bf16[96,768]{1,0:T(8,128)(2,1)} async-done(((bf16[768,768]{1,0:T(8,128)(2,1)}), bf16[96,768]{1,0:T(8,128)(2,1)}) %reduce-scatter.2.cloned.1.call-update) | async-done | bytes 147472 | tf_op jit(solution)/shard_map/reduce_scatter | solution.py:115
  143.2 1.6 %convert_element_type.100 = f32[96,768]{1,0:T(8,128)} convert(bf16[96,768]{1,0:T(8,128)(2,1)} %reduce-scatter.2.cloned.1.call-done) | non-fusion elementwise | flops 73728 | bytes 442368 | tf_op jit(solution)/shard_map/convert_element_type | solution.py:121
  144.9 2.0 %collective-permute-done.9 = bf16[32,768]{1,0:T(8,128)(2,1)S(1)} collective-permute-done((bf16[32,768]{1,0:T(8,128)(2,1)S(1)}, bf16[32,768]{1,0:T(8,128)(2,1)S(1)}, u32[]{:S(2)}, u32[]{:S(2)}) %collective-permute-start.9) | collective-permute-done | bytes 49184 | tf_op jit(solution)/shard_map/ppermute | solution.py:45
  146.8 0.6 fusion.3
  147.5 4.1 %all-to-all-done.2 = bf16[8,96,768]{2,1,0:T(8,128)(2,1)S(1)} async-done(((bf16[8,96,768]{2,1,0:T(8,128)(2,1)}), bf16[8,96,768]{2,1,0:T(8,128)(2,1)S(1)}, u32[]{:S(2)}, u32[]{:S(2)}) %all-to-all-start.2) | async-done | bytes 1179680 | tf_op jit(solution)/shard_map/all_to_all | solution.py:27
  151.6 0.9 convert_reduce_fusion
  (26 shorter events, 0.5 us)
Async XLA Ops:
  7.2 85.4 %copy-start = (bf16[6,256,256]{2,1,0:T(8,128)(2,1)S(1)}, bf16[6,256,256]{2,1,0:T(8,128)(2,1)}, u32[]{:S(2)}) copy-start(bf16[6,256,256]{2,1,0:T(8,128)(2,1)} %param.8) | copy-start | bytes 2359300
  7.2 31.1 %copy-start.2 = (bf16[96,768]{1,0:T(8,128)(2,1)S(1)}, bf16[96,768]{1,0:T(8,128)(2,1)}, u32[]{:S(2)}) copy-start(bf16[96,768]{1,0:T(8,128)(2,1)} %param.10) | copy-start | bytes 442372
  7.2 69.9 %all-gather.6.cloned.1.call-start = ((), (), s32[]{:S(2)}) async-start(), calls=%async_computation.6 | async-start | bytes 1769472 | tf_op jit(solution)/shard_map/all_gather | solution.py:80
  9.0 17.6 %collective-permute-start = (bf16[32,768]{1,0:T(8,128)(2,1)}, bf16[32,768]{1,0:T(8,128)(2,1)S(1)}, u32[]{:S(2)}, u32[]{:S(2)}) collective-permute-start(bf16[32,768]{1,0:T(8,128)(2,1)} %param.11), channel_id=1, source_target_pairs={{0,8},{8,0},{16,24},{24,16},{32,40},{40,32},{48,56},{56,48},{1,9},... | collective-permute-start | bytes 147464 | tf_op jit(solution)/shard_map/ppermute | solution.py:82
  17.3 21.0 %collective-permute-start.1 = (bf16[96,768]{1,0:T(8,128)(2,1)}, bf16[96,768]{1,0:T(8,128)(2,1)S(1)}, u32[]{:S(2)}, u32[]{:S(2)}) collective-permute-start(bf16[96,768]{1,0:T(8,128)(2,1)} %param.10), channel_id=1, source_target_pairs={{0,2},{1,3},{2,0},{3,1},{4,6},{5,7},{6,4},{7,5},{8,10},{9,11},{10,... | collective-permute-start | bytes 442376 | tf_op jit(solution)/shard_map/ppermute | solution.py:54
  19.6 18.7 %collective-permute-start.2 = (bf16[96,768]{1,0:T(8,128)(2,1)}, bf16[96,768]{1,0:T(8,128)(2,1)S(1)}, u32[]{:S(2)}, u32[]{:S(2)}) collective-permute-start(bf16[96,768]{1,0:T(8,128)(2,1)} %param.10), channel_id=1, source_target_pairs={{0,4},{1,5},{2,6},{3,7},{4,0},{5,1},{6,2},{7,3},{8,12},{9,13},{10,... | collective-permute-start | bytes 442376 | tf_op jit(solution)/shard_map/ppermute | solution.py:54
  22.0 16.3 %collective-permute-start.3 = (bf16[96,768]{1,0:T(8,128)(2,1)}, bf16[96,768]{1,0:T(8,128)(2,1)S(1)}, u32[]{:S(2)}, u32[]{:S(2)}) collective-permute-start(bf16[96,768]{1,0:T(8,128)(2,1)} %param.10), channel_id=1, source_target_pairs={{0,6},{1,7},{2,4},{3,5},{4,2},{5,3},{6,0},{7,1},{8,14},{9,15},{10,... | collective-permute-start | bytes 442376 | tf_op jit(solution)/shard_map/ppermute | solution.py:54
  38.5 7.4 %collective-permute-start.4 = (bf16[4,96,768]{2,1,0:T(8,128)(2,1)S(1)}, bf16[4,96,768]{2,1,0:T(8,128)(2,1)S(1)}, u32[]{:S(2)}, u32[]{:S(2)}) collective-permute-start(bf16[4,96,768]{2,1,0:T(8,128)(2,1)S(1)} %get-tuple-element.38), channel_id=1, source_target_pairs={{0,1},{1,0},{2,3},{3,2},{4,5},{5,4},{6,7},{7,6},{8,9},{9,8},{10,11... | collective-permute-start | bytes 1769480 | tf_op jit(solution)/shard_map/ppermute | solution.py:89
  46.0 11.5 %copy-start.3 = (bf16[32,768]{1,0:T(8,128)(2,1)S(1)}, bf16[32,768]{1,0:T(8,128)(2,1)}, u32[]{:S(2)}) copy-start(bf16[32,768]{1,0:T(8,128)(2,1)} %param.6) | copy-start | bytes 147460
  47.3 25.4 %all-to-all-start = ((bf16[8,32,768]{2,1,0:T(8,128)(2,1)}), bf16[8,32,768]{2,1,0:T(8,128)(2,1)S(1)}, u32[]{:S(2)}, u32[]{:S(2)}) async-start(bf16[8,32,768]{2,1,0:T(8,128)(2,1)} %bitcast.10), calls=%async_computation | async-start | bytes 786432 | tf_op jit(solution)/shard_map/all_to_all | solution.py:27
  57.5 58.3 %all-gather.4.cloned.1.call-start = ((), (), s32[]{:S(2)}) async-start(), calls=%async_computation.5 | async-start | bytes 1474560 | tf_op jit(solution)/shard_map/all_gather | solution.py:102
  57.6 9.0 %collective-permute-start.5 = (bf16[32,768]{1,0:T(8,128)(2,1)S(1)}, bf16[32,768]{1,0:T(8,128)(2,1)S(1)}, u32[]{:S(2)}, u32[]{:S(2)}) collective-permute-start(bf16[32,768]{1,0:T(8,128)(2,1)S(1)} %copy-done.3), channel_id=1, source_target_pairs={{0,8},{8,0},{16,24},{24,16},{32,40},{40,32},{48,56},{56,48},{1,9},... | collective-permute-start | bytes 147464 | tf_op jit(solution)/shard_map/ppermute | solution.py:98
  73.5 18.5 %all-to-all-start.1 = ((bf16[8,32,768]{2,1,0:T(8,128)(2,1)}), bf16[8,32,768]{2,1,0:T(8,128)(2,1)S(1)}, u32[]{:S(2)}, u32[]{:S(2)}) async-start(bf16[8,32,768]{2,1,0:T(8,128)(2,1)} %broadcast_in_dim.2), calls=%async_computation.1 | async-start | bytes 786432 | tf_op jit(solution)/shard_map/all_to_all | solution.py:21
  77.0 66.2 %reduce-scatter.2.cloned.1.call-start = ((), (), s32[]{:S(2)}) async-start(), calls=%async_computation.4 | async-start | bytes 1327104 | tf_op jit(solution)/shard_map/reduce_scatter | solution.py:115
  118.3 33.2 %all-to-all-start.2 = ((bf16[8,96,768]{2,1,0:T(8,128)(2,1)}), bf16[8,96,768]{2,1,0:T(8,128)(2,1)S(1)}, u32[]{:S(2)}, u32[]{:S(2)}) async-start(bf16[8,96,768]{2,1,0:T(8,128)(2,1)} %bitcast.62), calls=%async_computation.3 | async-start | bytes 2359296 | tf_op jit(solution)/shard_map/all_to_all | solution.py:27
  122.5 0.8 copy-start.1
  123.2 8.5 %collective-permute-start.8 = (bf16[2,32,768]{2,1,0:T(8,128)(2,1)S(1)}, bf16[2,32,768]{2,1,0:T(8,128)(2,1)S(1)}, u32[]{:S(2)}, u32[]{:S(2)}) collective-permute-start(bf16[2,32,768]{2,1,0:T(8,128)(2,1)S(1)} %get-tuple-element.44), channel_id=1, source_target_pairs={{0,48},{8,56},{16,0},{24,8},{32,16},{40,24},{48,32},{56,40},{1,49}... | collective-permute-start | bytes 294920 | tf_op jit(solution)/shard_map/ppermute | solution.py:42
  127.3 7.2 %collective-permute-start.7 = (bf16[2,32,768]{2,1,0:T(8,128)(2,1)S(1)}, bf16[2,32,768]{2,1,0:T(8,128)(2,1)S(1)}, u32[]{:S(2)}, u32[]{:S(2)}) collective-permute-start(bf16[2,32,768]{2,1,0:T(8,128)(2,1)S(1)} %get-tuple-element.45), channel_id=1, source_target_pairs={{0,32},{8,40},{16,48},{24,56},{32,0},{40,8},{48,16},{56,24},{1,33}... | collective-permute-start | bytes 294920 | tf_op jit(solution)/shard_map/ppermute | solution.py:42
  129.8 7.1 %collective-permute-start.6 = (bf16[2,32,768]{2,1,0:T(8,128)(2,1)S(1)}, bf16[2,32,768]{2,1,0:T(8,128)(2,1)S(1)}, u32[]{:S(2)}, u32[]{:S(2)}) collective-permute-start(bf16[2,32,768]{2,1,0:T(8,128)(2,1)S(1)} %get-tuple-element.43), channel_id=1, source_target_pairs={{0,16},{8,24},{16,32},{24,40},{32,48},{40,56},{48,0},{56,8},{1,17}... | collective-permute-start | bytes 294920 | tf_op jit(solution)/shard_map/ppermute | solution.py:42
  137.9 8.9 %collective-permute-start.9 = (bf16[32,768]{1,0:T(8,128)(2,1)S(1)}, bf16[32,768]{1,0:T(8,128)(2,1)S(1)}, u32[]{:S(2)}, u32[]{:S(2)}) collective-permute-start(bf16[32,768]{1,0:T(8,128)(2,1)S(1)} %fusion.4), channel_id=1, source_target_pairs={{0,8},{8,0},{16,24},{24,16},{32,40},{40,32},{48,56},{56,48},{1,9},... | collective-permute-start | bytes 147464 | tf_op jit(solution)/shard_map/ppermute | solution.py:45
Sparse Core Ops, SparseCore 0:
  10.7 45.0 all-gather.5
  72.8 20.3 all-gather.3
  112.8 30.3 reduce-scatter.1
